TPU v7x, 256 devices: a whole 4x4x8 slice. The times are simulated.
256 devices in a mesh: ctx: 32 (over z, y_lo, core), head: 8 (over y_hi, x).
Axes of the slice: x: 4, y: 4 (y_hi: 2, y_lo: 2; y = y_hi * 2 + y_lo), z: 8, core: 2. Of those that a mesh axis runs over, the one named last changes fastest.
Arguments:
- queries: bfloat16 [4096, 5120], P('ctx', 'head'), may hold values from -80 to 80
- keys: bfloat16 [4096, 1024], P('ctx', 'head'), may hold values from -4 to 4
- values: bfloat16 [4096, 1024], P('ctx', 'head'), may hold values from -6 to 6
- out_grad: bfloat16 [4096, 5120], P('ctx', 'head'), may hold values from -6 to 6
- out_weight: bfloat16 [5120, 5120], P('head'), may hold values from -0.078125 to 0.078125
- seq_lengths: int32 [4], replicated, may hold values from 1 to 2048, as said below
- prompt_lengths: int32 [4], replicated, may hold values from 1 to 127
Outputs:
- query_grad: bfloat16 [4096, 5120], P('ctx', 'head')
- key_grad: bfloat16 [4096, 1024], P('ctx', 'head')
- value_grad: bfloat16 [4096, 1024], P('ctx', 'head')
Inputs may be any that keep to these rules, and one draw needn't show every extreme that they name: `seq_lengths`: the lengths sum to 4096; the first is exactly 2048.
All inputs are finite; a program needn't handle non-finite values.
Results may differ from a plain program's by a relative error of at most 0.015.
Values may be sent and summed in bfloat16 or wider, within the bound.
No kernel may reach another device: no remote copies, remote signals or barrier semaphores. Data moves between devices by JAX's collectives and lax.ppermute only.
A program may use at most 64 MiB of HBM per device.

v0:
```python
import math

import jax
import jax.numpy as jnp
from jax import lax
from jax.sharding import PartitionSpec as P

HEADS_Q = 40
HEADS_KV = 8
HEAD_DIM = 128


NEG_LARGE = -1e30


def passed_along(value, axis, steps):
    count = lax.axis_size(axis)
    first, last = (max(0, -steps), min(count, count - steps))
    return lax.ppermute(value, axis, [(source, source + steps) for source in range(first, last)])


def shifted(block, axis, distance):
    devices = range(lax.axis_size(axis))
    route = [((i - distance) % len(devices), i) for i in devices]
    return lax.ppermute(block, axis, route)


def segment_of(positions, bounds):
    return jnp.sum((positions[:, None] >= bounds[None, :]).astype(jnp.int32), axis=1)


def layout(seq_lengths, prompt_lengths, positions):
    bounds = jnp.cumsum(seq_lengths)
    answer_start = bounds - seq_lengths + jnp.minimum(prompt_lengths, seq_lengths - 1)
    segment = segment_of(positions, bounds)
    labels = jnp.arange(bounds.shape[0], dtype=jnp.int32)
    picked = jnp.sum(
        jnp.where(segment[:, None] == labels[None, :], answer_start[None, :], 0), axis=1
    )
    return (segment, positions >= picked)


def shards(queries, keys, values, out_grad, out_weight, seq_lengths, prompt_lengths):
    cycle_size = lax.axis_size("ctx")
    own_block = lax.axis_index("ctx")
    count = queries.shape[0]
    kv_local = keys.shape[1] // HEAD_DIM
    group = HEADS_Q // HEADS_KV
    scale = 1.0 / math.sqrt(HEAD_DIM)
    offsets = jnp.arange(count, dtype=jnp.int32)
    bounds = jnp.cumsum(seq_lengths)
    query_pos = own_block * count + offsets
    query_seg, answer = layout(seq_lengths, prompt_lengths, query_pos)
    summed = lax.dot_general(
        lax.all_gather(out_grad, "head", axis=1, tiled=True),
        out_weight,
        (((1,), (1,)), ((), ())),
        preferred_element_type=jnp.float32,
    )
    grads = (summed * answer[:, None].astype(jnp.float32)).astype(jnp.bfloat16)
    query_split = queries.reshape(count, kv_local, group, HEAD_DIM)
    grad_split = grads.reshape(count, kv_local, group, HEAD_DIM)
    pair_home = jnp.stack(
        [keys.reshape(count, kv_local, HEAD_DIM), values.reshape(count, kv_local, HEAD_DIM)]
    )

    def block_view(block):
        key_pos = block * count + offsets
        key_seg = segment_of(key_pos, bounds)
        allowed = (key_pos[None, :] <= query_pos[:, None]) & (
            key_seg[None, :] == query_seg[:, None]
        )
        edges = segment_of(jnp.stack([block * count + count - 1, own_block * count]), bounds)
        active = (block == own_block) | (block < own_block) & (edges[0] == edges[1])
        return (allowed, active)

    def scores_of(key_rows):
        return (
            jnp.einsum("qhgd,khd->hgqk", query_split, key_rows, preferred_element_type=jnp.float32)
            * scale
        )

    def dprobs_of(value_rows):
        return jnp.einsum(
            "qhgd,khd->hgqk", grad_split, value_rows, preferred_element_type=jnp.float32
        )

    def forward_update(stats, pair, block):
        allowed, active = block_view(block)

        def update(current):
            peak, mass, weighted = current
            scores = scores_of(pair[0])
            new_peak = jnp.maximum(peak, jnp.max(jnp.where(allowed, scores, NEG_LARGE), axis=3))
            shrink = jnp.exp(peak - new_peak)
            probs = jnp.where(allowed, jnp.exp(scores - new_peak[..., None]), 0.0)
            dprobs = dprobs_of(pair[1])
            return (
                new_peak,
                mass * shrink + jnp.sum(probs, axis=3),
                weighted * shrink + jnp.sum(probs * dprobs, axis=3),
            )

        return lax.cond(active, update, lambda current: current, stats)

    def forward_shift(pair):
        return passed_along(pair, "ctx", 1)

    stat_shape = (kv_local, group, count)
    stats = (
        jnp.full(stat_shape, NEG_LARGE, jnp.float32),
        jnp.zeros(stat_shape, jnp.float32),
        jnp.zeros(stat_shape, jnp.float32),
    )
    stats = forward_update(stats, pair_home, own_block)

    def forward_step(step, carry):
        pair = forward_shift(carry[0])
        return (pair, forward_update(carry[1], pair, (own_block - step) % cycle_size))

    stats = lax.fori_loop(1, cycle_size, forward_step, (pair_home, stats))[1]

    def fetch_pair(previous):
        return passed_along(previous, "ctx", 1)

    logsum = stats[0] + jnp.log(stats[1])
    delta = stats[2] / stats[1]

    def contributions(pair, allowed):
        scores = scores_of(pair[0])
        probs = jnp.where(allowed, jnp.exp(scores - logsum[..., None]), 0.0)
        dprobs = dprobs_of(pair[1])
        dscores = (probs * (dprobs - delta[..., None])).astype(jnp.bfloat16)
        probs_half = probs.astype(jnp.bfloat16)
        dvalue = jnp.einsum(
            "hgqk,qhgd->khd", probs_half, grad_split, preferred_element_type=jnp.float32
        )
        dkey = (
            jnp.einsum("hgqk,qhgd->khd", dscores, query_split, preferred_element_type=jnp.float32)
            * scale
        )
        dquery = (
            jnp.einsum("hgqk,khd->qhgd", dscores, pair[0], preferred_element_type=jnp.float32)
            * scale
        )
        return (jnp.stack([dkey, dvalue]), dquery)

    query_acc = jnp.zeros((count, kv_local, group, HEAD_DIM), jnp.float32)

    def pass_on(owed):
        return shifted(owed, "ctx", 1)

    def travel_work(pair, block, owed, dquery):
        allowed, active = block_view(block)

        def update(state):
            kv_part, q_part = contributions(pair, allowed)
            return (state[0] + kv_part, state[1] + q_part)

        return lax.cond(active, update, lambda state: state, (owed, dquery))

    owed, query_acc = travel_work(
        pair_home, own_block, jnp.zeros((2, count, kv_local, HEAD_DIM), jnp.float32), query_acc
    )

    def travel_step(step, carry):
        pair = fetch_pair(carry[0])
        owed = pass_on(carry[1])
        owed, dquery = travel_work(pair, (own_block - step) % cycle_size, owed, carry[2])
        return (pair, owed, dquery)

    final = lax.fori_loop(1, cycle_size, travel_step, (pair_home, owed, query_acc))
    owed = pass_on(final[1])
    query_acc = final[2]
    query_grad = query_acc.reshape(count, kv_local * group * HEAD_DIM).astype(jnp.bfloat16)
    key_grad = owed[0].reshape(count, kv_local * HEAD_DIM).astype(jnp.bfloat16)
    value_grad = owed[1].reshape(count, kv_local * HEAD_DIM).astype(jnp.bfloat16)
    return (query_grad, key_grad, value_grad)


def solution(mesh):
    return jax.shard_map(
        shards,
        mesh=mesh,
        in_specs=(
            P("ctx", "head"),
            P("ctx", "head"),
            P("ctx", "head"),
            P("ctx", "head"),
            P("head", None),
            P(),
            P(),
        ),
        out_specs=(P("ctx", "head"), P("ctx", "head"), P("ctx", "head")),
        check_vma=False,
    )
```

profile of v0, /device:TPU:128, one launch (start us, length us, event | category | flops | bytes accessed | tf_op | source)
XLA Modules:
  0.0 609.0 jit_solution(7232245549722975515)
XLA Ops:
  12.7 53.6 %all-gather.2.cloned.1.call-done = bf16[128,5120]{1,0:T(8,128)(2,1)} async-done(((bf16[128,640]{1,0:T(8,128)(2,1)}), bf16[128,5120]{1,0:T(8,128)(2,1)}) %all-gather.2.cloned.1.call-update) | async-done | bytes 1310736 | tf_op jit(solution)/shard_map/all_gather | solution.py:55
  66.4 5.4 fusion.46
  72.4 239.4 %while.50 = (s32[]{:T(128)}, bf16[2,128,1,128]{3,1,2,0:T(8,128)(2,1)S(1)}, f32[1,5,128]{2,1,0:T(8,128)S(1)}, f32[1,5,128]{2,1,0:T(8,128)S(1)}, f32[1,5,128]{2,1,...) while((s32[]{:T(128)}, ...), condition=%wide.region_14.15_spmd.clone.clone.clone, body=%wide.region_6.14_spmd.clone.clone.clone.sunk | while | flops 42815148 | bytes 1893492 | solution.py:121
  76.5 3.6 collective-permute-done
  84.2 3.6 collective-permute-done
  91.9 3.6 collective-permute-done
  99.7 3.6 collective-permute-done
  107.4 3.6 collective-permute-done
  115.1 3.6 collective-permute-done
  122.8 3.6 collective-permute-done
  130.5 3.6 collective-permute-done
  138.3 3.6 collective-permute-done
  146.0 3.6 collective-permute-done
  153.7 3.6 collective-permute-done
  161.4 3.6 collective-permute-done
  169.2 3.6 collective-permute-done
  176.9 3.6 collective-permute-done
  184.6 3.6 collective-permute-done
  192.3 3.6 collective-permute-done
  200.0 3.6 collective-permute-done
  207.8 3.6 collective-permute-done
  215.5 3.6 collective-permute-done
  223.2 3.6 collective-permute-done
  230.9 3.6 collective-permute-done
  238.7 3.6 collective-permute-done
  246.4 3.6 collective-permute-done
  254.1 3.6 collective-permute-done
  261.8 3.6 collective-permute-done
  269.5 3.6 collective-permute-done
  277.3 3.6 collective-permute-done
  312.6 283.0 %while.51 = (s32[]{:T(128)}, bf16[2,128,1,128]{3,1,2,0:T(8,128)(2,1)S(1)}, f32[2,128,1,128]{3,1,2,0:T(8,128)S(1)}, f32[128,1,5,128]{3,0,2,1:T(8,128)S(1)}, s32[]...) while((s32[]{:T(128)}, ...), condition=%wide.region_20.21_spmd.clone.clone.clone, body=%wide.region_15.20_spmd.clone.clone.clone.sunk | while | flops 105727792 | bytes 4639388 | solution.py:172
  596.7 4.8 collective-permute-done.3
  (720 shorter events, 354.4 us)
Async XLA Ops:
  7.2 59.2 %all-gather.2.cloned.1.call-start = ((), (), s32[]{:S(2)}) async-start(), calls=%async_computation | async-start | bytes 1474560 | tf_op jit(solution)/shard_map/all_gather | solution.py:55
  72.4 7.7 %collective-permute-start = (bf16[2,128,1,128]{3,1,2,0:T(8,128)(2,1)S(1)}, bf16[2,128,1,128]{3,1,2,0:T(8,128)(2,1)S(1)}, u32[]{:S(2)}, u32[]{:S(2)}) collective-permute-start(bf16[2,128,1,128]{3,1,2,0:T(8,128)(2,1)S(1)} %get-tuple-element.1501), channel_id=1, source_target_pairs={{0,8},{8,16},{16,24},{24,32},{32,40},{40,48},{48,56},{56,64},{64,7... | collective-permute-start | bytes 196616 | tf_op jit(solution)/shard_map/while/body/eval_jaxpr/ppermute | solution.py:19
  80.1 7.7 %collective-permute-start = (bf16[2,128,1,128]{3,1,2,0:T(8,128)(2,1)S(1)}, bf16[2,128,1,128]{3,1,2,0:T(8,128)(2,1)S(1)}, u32[]{:S(2)}, u32[]{:S(2)}) collective-permute-start(bf16[2,128,1,128]{3,1,2,0:T(8,128)(2,1)S(1)} %get-tuple-element.1501), channel_id=1, source_target_pairs={{0,8},{8,16},{16,24},{24,32},{32,40},{40,48},{48,56},{56,64},{64,7... | collective-permute-start | bytes 196616 | tf_op jit(solution)/shard_map/while/body/eval_jaxpr/ppermute | solution.py:19
  87.8 7.7 %collective-permute-start = (bf16[2,128,1,128]{3,1,2,0:T(8,128)(2,1)S(1)}, bf16[2,128,1,128]{3,1,2,0:T(8,128)(2,1)S(1)}, u32[]{:S(2)}, u32[]{:S(2)}) collective-permute-start(bf16[2,128,1,128]{3,1,2,0:T(8,128)(2,1)S(1)} %get-tuple-element.1501), channel_id=1, source_target_pairs={{0,8},{8,16},{16,24},{24,32},{32,40},{40,48},{48,56},{56,64},{64,7... | collective-permute-start | bytes 196616 | tf_op jit(solution)/shard_map/while/body/eval_jaxpr/ppermute | solution.py:19
  95.6 7.7 %collective-permute-start = (bf16[2,128,1,128]{3,1,2,0:T(8,128)(2,1)S(1)}, bf16[2,128,1,128]{3,1,2,0:T(8,128)(2,1)S(1)}, u32[]{:S(2)}, u32[]{:S(2)}) collective-permute-start(bf16[2,128,1,128]{3,1,2,0:T(8,128)(2,1)S(1)} %get-tuple-element.1501), channel_id=1, source_target_pairs={{0,8},{8,16},{16,24},{24,32},{32,40},{40,48},{48,56},{56,64},{64,7... | collective-permute-start | bytes 196616 | tf_op jit(solution)/shard_map/while/body/eval_jaxpr/ppermute | solution.py:19
  103.3 7.7 %collective-permute-start = (bf16[2,128,1,128]{3,1,2,0:T(8,128)(2,1)S(1)}, bf16[2,128,1,128]{3,1,2,0:T(8,128)(2,1)S(1)}, u32[]{:S(2)}, u32[]{:S(2)}) collective-permute-start(bf16[2,128,1,128]{3,1,2,0:T(8,128)(2,1)S(1)} %get-tuple-element.1501), channel_id=1, source_target_pairs={{0,8},{8,16},{16,24},{24,32},{32,40},{40,48},{48,56},{56,64},{64,7... | collective-permute-start | bytes 196616 | tf_op jit(solution)/shard_map/while/body/eval_jaxpr/ppermute | solution.py:19
  111.0 7.7 %collective-permute-start = (bf16[2,128,1,128]{3,1,2,0:T(8,128)(2,1)S(1)}, bf16[2,128,1,128]{3,1,2,0:T(8,128)(2,1)S(1)}, u32[]{:S(2)}, u32[]{:S(2)}) collective-permute-start(bf16[2,128,1,128]{3,1,2,0:T(8,128)(2,1)S(1)} %get-tuple-element.1501), channel_id=1, source_target_pairs={{0,8},{8,16},{16,24},{24,32},{32,40},{40,48},{48,56},{56,64},{64,7... | collective-permute-start | bytes 196616 | tf_op jit(solution)/shard_map/while/body/eval_jaxpr/ppermute | solution.py:19
  118.7 7.7 %collective-permute-start = (bf16[2,128,1,128]{3,1,2,0:T(8,128)(2,1)S(1)}, bf16[2,128,1,128]{3,1,2,0:T(8,128)(2,1)S(1)}, u32[]{:S(2)}, u32[]{:S(2)}) collective-permute-start(bf16[2,128,1,128]{3,1,2,0:T(8,128)(2,1)S(1)} %get-tuple-element.1501), channel_id=1, source_target_pairs={{0,8},{8,16},{16,24},{24,32},{32,40},{40,48},{48,56},{56,64},{64,7... | collective-permute-start | bytes 196616 | tf_op jit(solution)/shard_map/while/body/eval_jaxpr/ppermute | solution.py:19
  126.5 7.7 %collective-permute-start = (bf16[2,128,1,128]{3,1,2,0:T(8,128)(2,1)S(1)}, bf16[2,128,1,128]{3,1,2,0:T(8,128)(2,1)S(1)}, u32[]{:S(2)}, u32[]{:S(2)}) collective-permute-start(bf16[2,128,1,128]{3,1,2,0:T(8,128)(2,1)S(1)} %get-tuple-element.1501), channel_id=1, source_target_pairs={{0,8},{8,16},{16,24},{24,32},{32,40},{40,48},{48,56},{56,64},{64,7... | collective-permute-start | bytes 196616 | tf_op jit(solution)/shard_map/while/body/eval_jaxpr/ppermute | solution.py:19
  134.2 7.7 %collective-permute-start = (bf16[2,128,1,128]{3,1,2,0:T(8,128)(2,1)S(1)}, bf16[2,128,1,128]{3,1,2,0:T(8,128)(2,1)S(1)}, u32[]{:S(2)}, u32[]{:S(2)}) collective-permute-start(bf16[2,128,1,128]{3,1,2,0:T(8,128)(2,1)S(1)} %get-tuple-element.1501), channel_id=1, source_target_pairs={{0,8},{8,16},{16,24},{24,32},{32,40},{40,48},{48,56},{56,64},{64,7... | collective-permute-start | bytes 196616 | tf_op jit(solution)/shard_map/while/body/eval_jaxpr/ppermute | solution.py:19
  141.9 7.7 %collective-permute-start = (bf16[2,128,1,128]{3,1,2,0:T(8,128)(2,1)S(1)}, bf16[2,128,1,128]{3,1,2,0:T(8,128)(2,1)S(1)}, u32[]{:S(2)}, u32[]{:S(2)}) collective-permute-start(bf16[2,128,1,128]{3,1,2,0:T(8,128)(2,1)S(1)} %get-tuple-element.1501), channel_id=1, source_target_pairs={{0,8},{8,16},{16,24},{24,32},{32,40},{40,48},{48,56},{56,64},{64,7... | collective-permute-start | bytes 196616 | tf_op jit(solution)/shard_map/while/body/eval_jaxpr/ppermute | solution.py:19
  149.6 7.7 %collective-permute-start = (bf16[2,128,1,128]{3,1,2,0:T(8,128)(2,1)S(1)}, bf16[2,128,1,128]{3,1,2,0:T(8,128)(2,1)S(1)}, u32[]{:S(2)}, u32[]{:S(2)}) collective-permute-start(bf16[2,128,1,128]{3,1,2,0:T(8,128)(2,1)S(1)} %get-tuple-element.1501), channel_id=1, source_target_pairs={{0,8},{8,16},{16,24},{24,32},{32,40},{40,48},{48,56},{56,64},{64,7... | collective-permute-start | bytes 196616 | tf_op jit(solution)/shard_map/while/body/eval_jaxpr/ppermute | solution.py:19
  157.3 7.7 %collective-permute-start = (bf16[2,128,1,128]{3,1,2,0:T(8,128)(2,1)S(1)}, bf16[2,128,1,128]{3,1,2,0:T(8,128)(2,1)S(1)}, u32[]{:S(2)}, u32[]{:S(2)}) collective-permute-start(bf16[2,128,1,128]{3,1,2,0:T(8,128)(2,1)S(1)} %get-tuple-element.1501), channel_id=1, source_target_pairs={{0,8},{8,16},{16,24},{24,32},{32,40},{40,48},{48,56},{56,64},{64,7... | collective-permute-start | bytes 196616 | tf_op jit(solution)/shard_map/while/body/eval_jaxpr/ppermute | solution.py:19
  165.1 7.7 %collective-permute-start = (bf16[2,128,1,128]{3,1,2,0:T(8,128)(2,1)S(1)}, bf16[2,128,1,128]{3,1,2,0:T(8,128)(2,1)S(1)}, u32[]{:S(2)}, u32[]{:S(2)}) collective-permute-start(bf16[2,128,1,128]{3,1,2,0:T(8,128)(2,1)S(1)} %get-tuple-element.1501), channel_id=1, source_target_pairs={{0,8},{8,16},{16,24},{24,32},{32,40},{40,48},{48,56},{56,64},{64,7... | collective-permute-start | bytes 196616 | tf_op jit(solution)/shard_map/while/body/eval_jaxpr/ppermute | solution.py:19
  172.8 7.7 %collective-permute-start = (bf16[2,128,1,128]{3,1,2,0:T(8,128)(2,1)S(1)}, bf16[2,128,1,128]{3,1,2,0:T(8,128)(2,1)S(1)}, u32[]{:S(2)}, u32[]{:S(2)}) collective-permute-start(bf16[2,128,1,128]{3,1,2,0:T(8,128)(2,1)S(1)} %get-tuple-element.1501), channel_id=1, source_target_pairs={{0,8},{8,16},{16,24},{24,32},{32,40},{40,48},{48,56},{56,64},{64,7... | collective-permute-start | bytes 196616 | tf_op jit(solution)/shard_map/while/body/eval_jaxpr/ppermute | solution.py:19
  180.5 7.7 %collective-permute-start = (bf16[2,128,1,128]{3,1,2,0:T(8,128)(2,1)S(1)}, bf16[2,128,1,128]{3,1,2,0:T(8,128)(2,1)S(1)}, u32[]{:S(2)}, u32[]{:S(2)}) collective-permute-start(bf16[2,128,1,128]{3,1,2,0:T(8,128)(2,1)S(1)} %get-tuple-element.1501), channel_id=1, source_target_pairs={{0,8},{8,16},{16,24},{24,32},{32,40},{40,48},{48,56},{56,64},{64,7... | collective-permute-start | bytes 196616 | tf_op jit(solution)/shard_map/while/body/eval_jaxpr/ppermute | solution.py:19
  188.2 7.7 %collective-permute-start = (bf16[2,128,1,128]{3,1,2,0:T(8,128)(2,1)S(1)}, bf16[2,128,1,128]{3,1,2,0:T(8,128)(2,1)S(1)}, u32[]{:S(2)}, u32[]{:S(2)}) collective-permute-start(bf16[2,128,1,128]{3,1,2,0:T(8,128)(2,1)S(1)} %get-tuple-element.1501), channel_id=1, source_target_pairs={{0,8},{8,16},{16,24},{24,32},{32,40},{40,48},{48,56},{56,64},{64,7... | collective-permute-start | bytes 196616 | tf_op jit(solution)/shard_map/while/body/eval_jaxpr/ppermute | solution.py:19
  196.0 7.7 %collective-permute-start = (bf16[2,128,1,128]{3,1,2,0:T(8,128)(2,1)S(1)}, bf16[2,128,1,128]{3,1,2,0:T(8,128)(2,1)S(1)}, u32[]{:S(2)}, u32[]{:S(2)}) collective-permute-start(bf16[2,128,1,128]{3,1,2,0:T(8,128)(2,1)S(1)} %get-tuple-element.1501), channel_id=1, source_target_pairs={{0,8},{8,16},{16,24},{24,32},{32,40},{40,48},{48,56},{56,64},{64,7... | collective-permute-start | bytes 196616 | tf_op jit(solution)/shard_map/while/body/eval_jaxpr/ppermute | solution.py:19
  203.7 7.7 %collective-permute-start = (bf16[2,128,1,128]{3,1,2,0:T(8,128)(2,1)S(1)}, bf16[2,128,1,128]{3,1,2,0:T(8,128)(2,1)S(1)}, u32[]{:S(2)}, u32[]{:S(2)}) collective-permute-start(bf16[2,128,1,128]{3,1,2,0:T(8,128)(2,1)S(1)} %get-tuple-element.1501), channel_id=1, source_target_pairs={{0,8},{8,16},{16,24},{24,32},{32,40},{40,48},{48,56},{56,64},{64,7... | collective-permute-start | bytes 196616 | tf_op jit(solution)/shard_map/while/body/eval_jaxpr/ppermute | solution.py:19
  211.4 7.7 %collective-permute-start = (bf16[2,128,1,128]{3,1,2,0:T(8,128)(2,1)S(1)}, bf16[2,128,1,128]{3,1,2,0:T(8,128)(2,1)S(1)}, u32[]{:S(2)}, u32[]{:S(2)}) collective-permute-start(bf16[2,128,1,128]{3,1,2,0:T(8,128)(2,1)S(1)} %get-tuple-element.1501), channel_id=1, source_target_pairs={{0,8},{8,16},{16,24},{24,32},{32,40},{40,48},{48,56},{56,64},{64,7... | collective-permute-start | bytes 196616 | tf_op jit(solution)/shard_map/while/body/eval_jaxpr/ppermute | solution.py:19
  219.1 7.7 %collective-permute-start = (bf16[2,128,1,128]{3,1,2,0:T(8,128)(2,1)S(1)}, bf16[2,128,1,128]{3,1,2,0:T(8,128)(2,1)S(1)}, u32[]{:S(2)}, u32[]{:S(2)}) collective-permute-start(bf16[2,128,1,128]{3,1,2,0:T(8,128)(2,1)S(1)} %get-tuple-element.1501), channel_id=1, source_target_pairs={{0,8},{8,16},{16,24},{24,32},{32,40},{40,48},{48,56},{56,64},{64,7... | collective-permute-start | bytes 196616 | tf_op jit(solution)/shard_map/while/body/eval_jaxpr/ppermute | solution.py:19
  226.8 7.7 %collective-permute-start = (bf16[2,128,1,128]{3,1,2,0:T(8,128)(2,1)S(1)}, bf16[2,128,1,128]{3,1,2,0:T(8,128)(2,1)S(1)}, u32[]{:S(2)}, u32[]{:S(2)}) collective-permute-start(bf16[2,128,1,128]{3,1,2,0:T(8,128)(2,1)S(1)} %get-tuple-element.1501), channel_id=1, source_target_pairs={{0,8},{8,16},{16,24},{24,32},{32,40},{40,48},{48,56},{56,64},{64,7... | collective-permute-start | bytes 196616 | tf_op jit(solution)/shard_map/while/body/eval_jaxpr/ppermute | solution.py:19
  234.6 7.7 %collective-permute-start = (bf16[2,128,1,128]{3,1,2,0:T(8,128)(2,1)S(1)}, bf16[2,128,1,128]{3,1,2,0:T(8,128)(2,1)S(1)}, u32[]{:S(2)}, u32[]{:S(2)}) collective-permute-start(bf16[2,128,1,128]{3,1,2,0:T(8,128)(2,1)S(1)} %get-tuple-element.1501), channel_id=1, source_target_pairs={{0,8},{8,16},{16,24},{24,32},{32,40},{40,48},{48,56},{56,64},{64,7... | collective-permute-start | bytes 196616 | tf_op jit(solution)/shard_map/while/body/eval_jaxpr/ppermute | solution.py:19
  242.3 7.7 %collective-permute-start = (bf16[2,128,1,128]{3,1,2,0:T(8,128)(2,1)S(1)}, bf16[2,128,1,128]{3,1,2,0:T(8,128)(2,1)S(1)}, u32[]{:S(2)}, u32[]{:S(2)}) collective-permute-start(bf16[2,128,1,128]{3,1,2,0:T(8,128)(2,1)S(1)} %get-tuple-element.1501), channel_id=1, source_target_pairs={{0,8},{8,16},{16,24},{24,32},{32,40},{40,48},{48,56},{56,64},{64,7... | collective-permute-start | bytes 196616 | tf_op jit(solution)/shard_map/while/body/eval_jaxpr/ppermute | solution.py:19
  250.0 7.7 %collective-permute-start = (bf16[2,128,1,128]{3,1,2,0:T(8,128)(2,1)S(1)}, bf16[2,128,1,128]{3,1,2,0:T(8,128)(2,1)S(1)}, u32[]{:S(2)}, u32[]{:S(2)}) collective-permute-start(bf16[2,128,1,128]{3,1,2,0:T(8,128)(2,1)S(1)} %get-tuple-element.1501), channel_id=1, source_target_pairs={{0,8},{8,16},{16,24},{24,32},{32,40},{40,48},{48,56},{56,64},{64,7... | collective-permute-start | bytes 196616 | tf_op jit(solution)/shard_map/while/body/eval_jaxpr/ppermute | solution.py:19
  257.7 7.7 %collective-permute-start = (bf16[2,128,1,128]{3,1,2,0:T(8,128)(2,1)S(1)}, bf16[2,128,1,128]{3,1,2,0:T(8,128)(2,1)S(1)}, u32[]{:S(2)}, u32[]{:S(2)}) collective-permute-start(bf16[2,128,1,128]{3,1,2,0:T(8,128)(2,1)S(1)} %get-tuple-element.1501), channel_id=1, source_target_pairs={{0,8},{8,16},{16,24},{24,32},{32,40},{40,48},{48,56},{56,64},{64,7... | collective-permute-start | bytes 196616 | tf_op jit(solution)/shard_map/while/body/eval_jaxpr/ppermute | solution.py:19
  265.5 7.7 %collective-permute-start = (bf16[2,128,1,128]{3,1,2,0:T(8,128)(2,1)S(1)}, bf16[2,128,1,128]{3,1,2,0:T(8,128)(2,1)S(1)}, u32[]{:S(2)}, u32[]{:S(2)}) collective-permute-start(bf16[2,128,1,128]{3,1,2,0:T(8,128)(2,1)S(1)} %get-tuple-element.1501), channel_id=1, source_target_pairs={{0,8},{8,16},{16,24},{24,32},{32,40},{40,48},{48,56},{56,64},{64,7... | collective-permute-start | bytes 196616 | tf_op jit(solution)/shard_map/while/body/eval_jaxpr/ppermute | solution.py:19
  273.2 7.7 %collective-permute-start = (bf16[2,128,1,128]{3,1,2,0:T(8,128)(2,1)S(1)}, bf16[2,128,1,128]{3,1,2,0:T(8,128)(2,1)S(1)}, u32[]{:S(2)}, u32[]{:S(2)}) collective-permute-start(bf16[2,128,1,128]{3,1,2,0:T(8,128)(2,1)S(1)} %get-tuple-element.1501), channel_id=1, source_target_pairs={{0,8},{8,16},{16,24},{24,32},{32,40},{40,48},{48,56},{56,64},{64,7... | collective-permute-start | bytes 196616 | tf_op jit(solution)/shard_map/while/body/eval_jaxpr/ppermute | solution.py:19
  280.9 7.7 %collective-permute-start = (bf16[2,128,1,128]{3,1,2,0:T(8,128)(2,1)S(1)}, bf16[2,128,1,128]{3,1,2,0:T(8,128)(2,1)S(1)}, u32[]{:S(2)}, u32[]{:S(2)}) collective-permute-start(bf16[2,128,1,128]{3,1,2,0:T(8,128)(2,1)S(1)} %get-tuple-element.1501), channel_id=1, source_target_pairs={{0,8},{8,16},{16,24},{24,32},{32,40},{40,48},{48,56},{56,64},{64,7... | collective-permute-start | bytes 196616 | tf_op jit(solution)/shard_map/while/body/eval_jaxpr/ppermute | solution.py:19
  288.6 7.7 %collective-permute-start = (bf16[2,128,1,128]{3,1,2,0:T(8,128)(2,1)S(1)}, bf16[2,128,1,128]{3,1,2,0:T(8,128)(2,1)S(1)}, u32[]{:S(2)}, u32[]{:S(2)}) collective-permute-start(bf16[2,128,1,128]{3,1,2,0:T(8,128)(2,1)S(1)} %get-tuple-element.1501), channel_id=1, source_target_pairs={{0,8},{8,16},{16,24},{24,32},{32,40},{40,48},{48,56},{56,64},{64,7... | collective-permute-start | bytes 196616 | tf_op jit(solution)/shard_map/while/body/eval_jaxpr/ppermute | solution.py:19
  296.3 7.7 %collective-permute-start = (bf16[2,128,1,128]{3,1,2,0:T(8,128)(2,1)S(1)}, bf16[2,128,1,128]{3,1,2,0:T(8,128)(2,1)S(1)}, u32[]{:S(2)}, u32[]{:S(2)}) collective-permute-start(bf16[2,128,1,128]{3,1,2,0:T(8,128)(2,1)S(1)} %get-tuple-element.1501), channel_id=1, source_target_pairs={{0,8},{8,16},{16,24},{24,32},{32,40},{40,48},{48,56},{56,64},{64,7... | collective-permute-start | bytes 196616 | tf_op jit(solution)/shard_map/while/body/eval_jaxpr/ppermute | solution.py:19
  304.1 7.7 %collective-permute-start = (bf16[2,128,1,128]{3,1,2,0:T(8,128)(2,1)S(1)}, bf16[2,128,1,128]{3,1,2,0:T(8,128)(2,1)S(1)}, u32[]{:S(2)}, u32[]{:S(2)}) collective-permute-start(bf16[2,128,1,128]{3,1,2,0:T(8,128)(2,1)S(1)} %get-tuple-element.1501), channel_id=1, source_target_pairs={{0,8},{8,16},{16,24},{24,32},{32,40},{40,48},{48,56},{56,64},{64,7... | collective-permute-start | bytes 196616 | tf_op jit(solution)/shard_map/while/body/eval_jaxpr/ppermute | solution.py:19
  (65 other events, 772.2 us)
Sparse Core Ops, SparseCore 0:
  10.6 55.7 all-gather.1
where the time goes:
time: 612 us; the launch traced here: 609 us
  waiting for transfers between devices  323 us (53%)
  starting transfers between devices  122 us (20%)
  loops' own time  79.3 us (13%)
  local copies, waits for them, and re-layouts  39.9 us (7%)
  other arithmetic  23.5 us (4%)
  between operations  14.2 us (2%)
  matrix products  7.21 us (1%)
    ppermute x62, waiting for transfers between devices, passed_along(): lax.ppermute(value, axis, [(source, source + steps) for source in range(f...  221 us
    ppermute x62, starting transfers between devices, passed_along(): lax.ppermute(value, axis, [(source, source + steps) for source in range(f...  119 us
    all_gather x1, waiting for transfers between devices, shards(): lax.all_gather(out_grad, 'head', axis=1, tiled=True)  53.6 us
    ppermute x32, waiting for transfers between devices, shifted(): return lax.ppermute(block, axis, route)  48.1 us
    another operation x1, loops' own time, shards(): lax.fori_loop(1, cycle_size, travel_step, (pair_home, owed, query_acc))  39.7 us
    another operation x1, loops' own time, shards(): stats = lax.fori_loop(1, cycle_size, forward_step, (pair_home, stats))[1]  39.6 us
    slice x62, local copies, waits for them, and re-layouts, block_view(): active = (block == own_block) | (block < own_block) & (edges[0] == edges[1])  35.9 us
  transfers between devices with their start and end apart: 95, of which 95 were waited for; matrix products, arithmetic and copies ran while one was open for 10% of the time, Pallas kernels for 0%

commit v1 on v0

v1 whole, which is shorter than its diff:
```python
import math

import jax
import jax.numpy as jnp
from jax import lax
from jax.experimental import pallas as pl
from jax.experimental.pallas import tpu as pltpu
from jax.sharding import PartitionSpec as P

HEADS_Q = 40
HEADS_KV = 8
HEAD_DIM = 128
GROUP = HEADS_Q // HEADS_KV
HALF = 16
TILES = 8
NEG = -1e30
SCALE = 1.0 / math.sqrt(HEAD_DIM)
LOG2_SCALE = SCALE * math.log2(math.e)
BF16 = jnp.bfloat16
F32 = jnp.float32
VMEM_LIMIT = 32 * 1024 * 1024
WIDE_LIMIT = 40 * 1024 * 1024


def ctx_swap(value, bits):
    count = lax.axis_size("ctx")
    return lax.ppermute(value, "ctx", [(i, i ^ bits) for i in range(count)])


def head_swap(value, bits):
    count = lax.axis_size("head")
    return lax.ppermute(value, "head", [(i, i ^ bits) for i in range(count)])


def dot_nn(a, b):
    return lax.dot_general(a, b, (((1,), (0,)), ((), ())), preferred_element_type=F32)


def dot_nt(a, b):
    return lax.dot_general(a, b, (((1,), (1,)), ((), ())), preferred_element_type=F32)


def heads(index):
    return slice(index * HEAD_DIM, (index + 1) * HEAD_DIM)


TILE_BLOCKS = (((0, 0), (1, 0)), ((0, 1), (1, 1)), ((0, 2), (0, 3)), ((1, 2), (1, 3)))


def tile_blocks(own, tile):
    return [own ^ (z * 4 + y * 2 + tile // 4) for y, z in TILE_BLOCKS[tile % 4]]


def own_geometry(geo_ref, count):
    place = lax.axis_index("ctx")
    own = place % HALF
    base = place - own
    low_block = jnp.maximum(jnp.min(geo_ref[0]) // count - base, 0)
    return place, own, base, low_block


def tile_active(own, low_block, tile):
    first, second = tile_blocks(own, tile)
    return ((first <= own) & (first >= low_block)) | ((second <= own) & (second >= low_block))


def fold_rows(values, reduce):
    rows, lanes = values.shape
    return reduce(values.reshape(rows // 8, 8, lanes), axis=0)


def prepare_kernel(lens_ref, prompts_ref, k_ref, v_ref, q_ref, kv_ref, qt_ref, qs_ref, geo_ref):
    kv_ref[:, :HEAD_DIM] = k_ref[...]
    kv_ref[:, HEAD_DIM:] = v_ref[...]
    for h in range(GROUP):
        qt_ref[:, heads(h)] = q_ref[:, heads(h)].T
        qs_ref[heads(h), :] = q_ref[:, heads(h)]
    rows, count = geo_ref.shape[1:]
    position = lax.axis_index("ctx") * count + lax.broadcasted_iota(jnp.int32, (rows, count), 1)
    start = jnp.int32(0)
    begin = jnp.zeros((rows, count), jnp.int32)
    answer_from = jnp.zeros((rows, count), jnp.int32)
    for s in range(lens_ref.shape[0]):
        answer = start + jnp.minimum(prompts_ref[s], lens_ref[s] - 1)
        begin = jnp.where(position >= start, start, begin)
        answer_from = jnp.where(position >= start, answer, answer_from)
        start = start + lens_ref[s]
    geo_ref[0] = begin
    geo_ref[1] = jnp.where(position >= answer_from, 1, 0)


def attend_kernel(geo_ref, w_ref, qt_ref, *refs):
    kv_refs = refs[:TILES]
    p_ref, o_ref, inv_ref, w_out, s_ref, m_ref, l_ref, sem = refs[TILES:]
    weights = pltpu.make_async_copy(w_ref, w_out, sem)
    weights.start()
    count = kv_refs[0].shape[0] // 2
    place, own, base, low_block = own_geometry(geo_ref, count)
    q_pos = place * count + lax.broadcasted_iota(jnp.int32, (count, count), 1)
    q_start = geo_ref[0, 0:1, :]
    m_ref[...] = jnp.full(m_ref.shape, NEG, F32)
    l_ref[...] = jnp.zeros(l_ref.shape, F32)
    o_ref[...] = jnp.zeros(o_ref.shape, F32)

    for tile in range(TILES):

        @pl.when(tile_active(own, low_block, tile))
        def _(tile=tile):
            biases = []
            for block in tile_blocks(own, tile):
                k_pos = (base + block) * count + lax.broadcasted_iota(jnp.int32, (count, count), 0)
                biases.append(jnp.where((k_pos <= q_pos) & (k_pos >= q_start), 0.0, NEG).astype(F32))
            bias = jnp.concatenate(biases, axis=0)
            keys = kv_refs[tile][:, :HEAD_DIM]
            for h in range(GROUP):
                scores = dot_nn(keys, qt_ref[:, heads(h)]) * LOG2_SCALE + bias
                s_ref[tile, :, heads(h)] = scores
                m_ref[:, heads(h)] = jnp.maximum(m_ref[:, heads(h)], fold_rows(scores, jnp.max))

    m_ref[...] = jnp.broadcast_to(jnp.max(m_ref[...], axis=0, keepdims=True), m_ref.shape)

    for tile in range(TILES):

        @pl.when(tile_active(own, low_block, tile))
        def _(tile=tile):
            values = kv_refs[tile][:, HEAD_DIM:].T
            for h in range(GROUP):
                probs = jnp.exp2(s_ref[tile, :, heads(h)] - m_ref[0:1, heads(h)])
                l_ref[:, heads(h)] = l_ref[:, heads(h)] + fold_rows(probs, jnp.sum)
                half = probs.astype(BF16)
                p_ref[tile, :, heads(h)] = half
                o_ref[:, heads(h)] += dot_nn(values, half)

    inverse = 1.0 / jnp.sum(l_ref[...], axis=0, keepdims=True)
    inv_ref[...] = jnp.broadcast_to(inverse, inv_ref.shape)
    weights.wait()


def tile_gradients(tile, p_ref, kv_ref, gt_ref, g_ref, qs_ref, delta_ref, ds_ref, dqt_ref, out):
    count = out.shape[2]
    keys, values = kv_ref[:, :HEAD_DIM], kv_ref[:, HEAD_DIM:]
    for h in range(GROUP):
        dprobs = dot_nn(values, gt_ref[:, heads(h)])
        probs = p_ref[tile, :, heads(h)].astype(F32)
        ds_ref[:, heads(h)] = (probs * (dprobs - delta_ref[0:1, heads(h)])).astype(BF16)
    dvalue = dot_nn(p_ref[tile], g_ref[...])
    dkey = dot_nn(ds_ref[...], qs_ref[...]) * SCALE
    dqt_ref[...] += dot_nn(keys.T, ds_ref[...])
    for n, (y, z) in enumerate(TILE_BLOCKS[tile % 4]):
        rows = slice(n * count, (n + 1) * count)
        out[y, z % 2, :, :HEAD_DIM] = dkey[rows].astype(out.dtype)
        out[y, z % 2, :, HEAD_DIM:] = dvalue[rows].astype(out.dtype)


def all_tiles(group, geo_ref, count, p_ref, kv_refs, gt_ref, g_ref, qs_ref, delta_ref, ds_ref, dqt_ref, keep_ref, send_ref):
    _, own, _, low_block = own_geometry(geo_ref, count)
    for core, out in ((1, send_ref), (0, keep_ref)):
        for n, member in enumerate(group):
            tile = core * 4 + member
            kv_ref = kv_refs[core * len(group) + n]
            active = tile_active(own, low_block, tile)

            @pl.when(active)
            def _(tile=tile, kv_ref=kv_ref, out=out):
                tile_gradients(tile, p_ref, kv_ref, gt_ref, g_ref, qs_ref, delta_ref, ds_ref, dqt_ref, out)

            @pl.when(jnp.logical_not(active))
            def _(tile=tile, out=out):
                for y, z in TILE_BLOCKS[tile % 4]:
                    out[y, z % 2] = jnp.zeros(out.shape[2:], out.dtype)


def far_kernel(group, geo_ref, w_ref, qs_ref, o_ref, inv_ref, p_ref, *refs):
    og_refs, kv_refs = refs[:4], refs[4 : 4 + 2 * len(group)]
    keep_ref, send_ref, gt_ref, g_ref, delta_ref, dqt_ref, ds_ref, acc_ref = refs[4 + 2 * len(group) :]
    _, count, width = og_refs[0].shape
    mine = lax.axis_index("head")
    parts = [(slot ^ (4 * n), slot, n) for slot in range(4) for n in range(2)]
    for n, (slot, array, half) in enumerate(parts):
        columns = pl.ds(pl.multiple_of((mine ^ slot) * width, HEAD_DIM), width)
        part = dot_nt(w_ref[:, columns], og_refs[array][half])
        if n == 0:
            acc_ref[...] = part
        else:
            acc_ref[...] += part
    answer = geo_ref[1, 0:1, :].astype(F32)
    for h in range(GROUP):
        inverse = inv_ref[0:1, heads(h)]
        grads = (acc_ref[heads(h), :] * answer).astype(BF16).astype(F32)
        scaled = (grads * inverse).astype(BF16)
        gt_ref[:, heads(h)] = scaled
        g_ref[heads(h), :] = scaled.T
        delta = jnp.sum(scaled.astype(F32) * (o_ref[:, heads(h)] * inverse), axis=0, keepdims=True)
        delta_ref[:, heads(h)] = jnp.broadcast_to(delta, (8, HEAD_DIM))
    dqt_ref[...] = jnp.zeros(dqt_ref.shape, F32)
    all_tiles(group, geo_ref, count, p_ref, kv_refs, gt_ref, g_ref, qs_ref, delta_ref, ds_ref, dqt_ref, keep_ref, send_ref)


def near_kernel(group, geo_ref, p_ref, gt_ref, g_ref, qs_ref, delta_ref, dqt_in, *refs):
    n_kv = 2 * len(group)
    kv_refs = refs[:n_kv]
    keep_ref, send_ref, dq_ref, ds_ref, dqt_ref = refs[n_kv:]
    count = dq_ref.shape[0]
    dqt_ref[...] = dqt_in[...]
    all_tiles(group, geo_ref, count, p_ref, kv_refs, gt_ref, g_ref, qs_ref, delta_ref, ds_ref, dqt_ref, keep_ref, send_ref)
    for h in range(GROUP):
        dq_ref[:, heads(h)] = (dqt_ref[:, heads(h)] * SCALE).T.astype(BF16)


VMEM_SPEC = pl.BlockSpec(memory_space=pltpu.VMEM)
SMEM_SPEC = pl.BlockSpec(memory_space=pltpu.SMEM)
ANY_SPEC = pl.BlockSpec(memory_space=pltpu.HBM)
PARAMS = pltpu.CompilerParams(vmem_limit_bytes=VMEM_LIMIT)


def prepare(seq_lengths, prompt_lengths, keys, values, queries):
    count, features = queries.shape
    return pl.pallas_call(
        prepare_kernel,
        out_shape=(
            jax.ShapeDtypeStruct((count, 2 * HEAD_DIM), BF16),
            jax.ShapeDtypeStruct((HEAD_DIM, features), BF16),
            jax.ShapeDtypeStruct((features, HEAD_DIM), BF16),
            jax.ShapeDtypeStruct((2, 8, count), jnp.int32),
        ),
        in_specs=[SMEM_SPEC] * 2 + [VMEM_SPEC] * 3,
        out_specs=(VMEM_SPEC,) * 4,
        name="prepare",
    )(seq_lengths, prompt_lengths, keys, values, queries)


def attend(geometry, weight, query_t, kv_tiles):
    _, features = query_t.shape
    keys = kv_tiles[0].shape[0]
    flops = 2 * TILES * keys * features * HEAD_DIM
    return pl.pallas_call(
        attend_kernel,
        out_shape=(
            jax.ShapeDtypeStruct((TILES, keys, features), BF16),
            jax.ShapeDtypeStruct((HEAD_DIM, features), F32),
            jax.ShapeDtypeStruct((8, features), F32),
            jax.ShapeDtypeStruct(weight.shape, BF16),
        ),
        in_specs=[VMEM_SPEC, ANY_SPEC] + [VMEM_SPEC] * (1 + TILES),
        out_specs=(VMEM_SPEC,) * 4,
        scratch_shapes=[
            pltpu.VMEM((TILES, keys, features), F32),
            pltpu.VMEM((8, features), F32),
            pltpu.VMEM((8, features), F32),
            pltpu.SemaphoreType.DMA,
        ],
        compiler_params=pltpu.CompilerParams(vmem_limit_bytes=WIDE_LIMIT),
        cost_estimate=pl.CostEstimate(
            flops=2 * flops, bytes_accessed=TILES * keys * features * 2, transcendentals=TILES * keys * features
        ),
        name="attend",
    )(geometry, weight, query_t, *kv_tiles)


def far_gradients(group, geometry, weight, query_s, attended, probs, blocks, kv_tiles):
    _, count, width = blocks[0].shape
    features = query_s.shape[0]
    keys = kv_tiles[0].shape[0]
    flops = 2 * len(kv_tiles) * keys * features * HEAD_DIM
    partial = (2, len(group), count, 2 * HEAD_DIM)

    def kernel(*refs):
        far_kernel(group, *refs)

    return pl.pallas_call(
        kernel,
        out_shape=(
            jax.ShapeDtypeStruct(partial, F32),
            jax.ShapeDtypeStruct(partial, BF16),
            jax.ShapeDtypeStruct((HEAD_DIM, features), BF16),
            jax.ShapeDtypeStruct((features, HEAD_DIM), BF16),
            jax.ShapeDtypeStruct((8, features), F32),
            jax.ShapeDtypeStruct((HEAD_DIM, features), F32),
        ),
        in_specs=[VMEM_SPEC] * (6 + len(blocks) + len(kv_tiles)),
        out_specs=(VMEM_SPEC,) * 6,
        scratch_shapes=[
            pltpu.VMEM((keys, features), BF16),
            pltpu.VMEM((features, count), F32),
        ],
        compiler_params=PARAMS,
        cost_estimate=pl.CostEstimate(
            flops=4 * flops + 2 * weight.size * count, bytes_accessed=2 * weight.size, transcendentals=0
        ),
        name="far_gradients",
    )(geometry, weight, query_s, *attended, probs, *blocks, *kv_tiles)


def near_gradients(group, geometry, probs, shared, kv_tiles):
    features, _ = shared[1].shape
    keys = kv_tiles[0].shape[0]
    count = keys // 2
    n_kv = len(kv_tiles)
    flops = 2 * n_kv * keys * features * HEAD_DIM
    partial = (2, len(group), count, 2 * HEAD_DIM)

    def kernel(*refs):
        near_kernel(group, *refs)

    return pl.pallas_call(
        kernel,
        out_shape=(
            jax.ShapeDtypeStruct(partial, F32),
            jax.ShapeDtypeStruct(partial, BF16),
            jax.ShapeDtypeStruct((count, features), BF16),
        ),
        in_specs=[VMEM_SPEC] * (7 + n_kv),
        out_specs=(VMEM_SPEC,) * 3,
        scratch_shapes=[pltpu.VMEM((keys, features), BF16), pltpu.VMEM((HEAD_DIM, features), F32)],
        compiler_params=PARAMS,
        cost_estimate=pl.CostEstimate(
            flops=4 * flops, bytes_accessed=2 * n_kv * keys * features, transcendentals=0
        ),
        name="near_gradients",
    )(geometry, probs, *shared, *kv_tiles)


def over_cores_and_y(keep, send):
    total = keep + ctx_swap(send, 1).astype(F32)
    return total[0] + ctx_swap(total[1].astype(BF16), 2).astype(F32)


def shards(queries, keys, values, out_grad, out_weight, seq_lengths, prompt_lengths):
    own, query_t, query_s, geometry = prepare(seq_lengths, prompt_lengths, keys, values, queries)
    og_pair = jnp.stack([out_grad, head_swap(out_grad, 4)])
    reach = jnp.concatenate([ctx_swap(own, 8), ctx_swap(own, 12)], axis=0)
    pair = jnp.concatenate([own, ctx_swap(own, 2)], axis=0)
    blocks = [og_pair] + [head_swap(og_pair, x) for x in (1, 2, 3)]
    tiles = [*lax.optimization_barrier((pair, ctx_swap(pair, 4))), *lax.optimization_barrier((reach, ctx_swap(reach, 2)))]
    tiles += [ctx_swap(tile, 1) for tile in tiles]
    far, near = (2, 3), (0, 1)
    probs, *attended, weight = attend(geometry, out_weight, query_t, tiles)
    far_keep, far_send, grads_t, grads, delta, dquery_t = far_gradients(
        far, geometry, weight, query_s, attended, probs, blocks, [tiles[4 * core + n] for core in (0, 1) for n in far]
    )
    shared = (grads_t, grads, query_s, delta, dquery_t)
    near_keep, near_send, query_grad = near_gradients(
        near, geometry, probs, shared, [tiles[4 * core + n] for core in (0, 1) for n in near]
    )
    far_total = over_cores_and_y(far_keep, far_send)
    near_total = over_cores_and_y(near_keep, near_send)
    kv_grad = near_total[0]
    kv_grad = kv_grad + ctx_swap(far_total[0].astype(BF16), 8).astype(F32)
    kv_grad = kv_grad + ctx_swap(far_total[1].astype(BF16), 12).astype(F32)
    kv_grad = kv_grad + ctx_swap(near_total[1].astype(BF16), 4).astype(F32)
    kv_grad = kv_grad.astype(BF16)
    return (query_grad, kv_grad[:, :HEAD_DIM], kv_grad[:, HEAD_DIM:])


def solution(mesh):
    return jax.shard_map(
        shards,
        mesh=mesh,
        in_specs=(
            P("ctx", "head"),
            P("ctx", "head"),
            P("ctx", "head"),
            P("ctx", "head"),
            P("head", None),
            P(),
            P(),
        ),
        out_specs=(P("ctx", "head"), P("ctx", "head"), P("ctx", "head")),
        check_vma=False,
    )
```

time: 612 us -> 59.8 us (0.10)
  the two profiles are of different devices: /device:TPU:128 before, /device:TPU:2 now
where the time goes in v1:
time: 59.8 us; the launch traced here: 59.5 us
  starting transfers between devices  24.4 us (41%)
  waiting for transfers between devices  21.7 us (36%)
  Pallas kernels  8.32 us (14%)
  local copies, waits for them, and re-layouts  3.16 us (5%)
  other arithmetic  1.17 us (2%)
  between operations  0.75 us (1%)
    ppermute x16, starting transfers between devices, ctx_swap(): return lax.ppermute(value, 'ctx', [(i, i ^ bits) for i in range(count)])  17.3 us
    ppermute x16, waiting for transfers between devices, ctx_swap(): return lax.ppermute(value, 'ctx', [(i, i ^ bits) for i in range(count)])  13.4 us
    ppermute x4, waiting for transfers between devices, head_swap(): return lax.ppermute(value, 'head', [(i, i ^ bits) for i in range(count)])  8.26 us
    ppermute x4, starting transfers between devices, head_swap(): return lax.ppermute(value, 'head', [(i, i ^ bits) for i in range(count)])  7.08 us
    pallas_call x1, Pallas kernels, attend(): pl.pallas_call(attend_kernel, out_shape=(jax.ShapeDtypeStruct((TILES, key...  2.87 us
    unnamed x8, local copies, waits for them, and re-layouts  2.46 us
    pallas_call x1, Pallas kernels, far_gradients(): pl.pallas_call(kernel, out_shape=(jax.ShapeDtypeStruct(partial, F32), jax...  2.1 us
    pallas_call x1, Pallas kernels, prepare(): pl.pallas_call(prepare_kernel, out_shape=(jax.ShapeDtypeStruct((count, 2...  1.8 us
  transfers between devices with their start and end apart: 20, of which 11 were waited for; matrix products, arithmetic and copies ran while one was open for 3% of the time, Pallas kernels for 5%

profile of v1, /device:TPU:2, one launch (start us, length us, event | category | flops | bytes accessed | tf_op | source)
XLA Modules:
  0.0 59.5 jit_solution(15714241457110545234)
XLA Ops:
  0.6 1.8 %prepare.1 = (bf16[128,256]{1,0:T(8,128)(2,1)}, bf16[128,640]{1,0:T(8,128)(2,1)}, bf16[640,128]{1,0:T(8,128)(2,1)}, s32[2,8,128]{2,1,0:T(8,128)}) custom-call(s32[4]{0:T(128)} %lens_ref.1, s32[4]{0:T(128)} %prompts_ref.1, bf16[128,128]{1,0:T(8,128)(2,1)} %k_ref.1, bf16[128,128]{1,0:T(8,128)(2,1)} %v_ref.1, bf16[128,640]{1,0:T(8,128)(2,1)} %q_ref.1), custom_call_target="tpu_custom_call" | custom-call | tf_op jit(solution)/shard_map/prepare/pallas_call | solution.py:218
  2.4 4.6 %collective-permute-start.3 = (bf16[128,256]{1,0:T(8,128)(2,1)}, bf16[128,256]{1,0:T(8,128)(2,1)S(1)}, u32[]{:S(2)}, u32[]{:S(2)}) collective-permute-start(bf16[128,256]{1,0:T(8,128)(2,1)} %get-tuple-element.26), channel_id=1, source_target_pairs={{0,96},{8,104},{16,112},{24,120},{32,64},{40,72},{48,80},{56,88},{... | collective-permute-start | bytes 196616 | tf_op jit(solution)/shard_map/ppermute | solution.py:27
  7.1 1.6 %collective-permute-start = (bf16[128,256]{1,0:T(8,128)(2,1)}, bf16[128,256]{1,0:T(8,128)(2,1)S(1)}, u32[]{:S(2)}, u32[]{:S(2)}) collective-permute-start(bf16[128,256]{1,0:T(8,128)(2,1)} %get-tuple-element.26), channel_id=1, source_target_pairs={{0,16},{8,24},{16,0},{24,8},{32,48},{40,56},{48,32},{56,40},{64,80... | collective-permute-start | bytes 196616 | tf_op jit(solution)/shard_map/ppermute | solution.py:27
  8.6 2.9 %collective-permute-start.9 = (bf16[128,640]{1,0:T(8,128)(2,1)}, bf16[128,640]{1,0:T(8,128)(2,1)S(1)}, u32[]{:S(2)}, u32[]{:S(2)}) collective-permute-start(bf16[128,640]{1,0:T(8,128)(2,1)} %param.10), channel_id=1, source_target_pairs={{0,4},{1,5},{2,6},{3,7},{4,0},{5,1},{6,2},{7,3},{8,12},{9,13},{10,... | collective-permute-start | bytes 491528 | tf_op jit(solution)/shard_map/ppermute | solution.py:32
  11.5 0.8 %constant_dynamic-update-slice_fusion.1 = bf16[256,256]{1,0:T(8,128)(2,1)S(1)} fusion(bf16[128,256]{1,0:T(8,128)(2,1)} %get-tuple-element.26), kind=kLoop, calls=%fused_computation.22 | loop fusion | bytes 131072
  12.4 0.7 %collective-permute-start.1 = (bf16[256,256]{1,0:T(8,128)(2,1)S(1)}, bf16[256,256]{1,0:T(8,128)(2,1)S(1)}, u32[]{:S(2)}, u32[]{:S(2)}) collective-permute-start(bf16[256,256]{1,0:T(8,128)(2,1)S(1)} %constant_dynamic-update-slice_fusion.refs_0_.refs_7_), channel_id=1, source_target_pairs={{0,32},{8,40},{16,48},{24,56},{32,0},{40,8},{48,16},{56,24},{64,96... | collective-permute-start | bytes 393224 | tf_op jit(solution)/shard_map/ppermute | solution.py:27
  13.2 1.0 %collective-permute-start.4 = (bf16[256,256]{1,0:T(8,128)(2,1)S(1)}, bf16[256,256]{1,0:T(8,128)(2,1)S(1)}, u32[]{:S(2)}, u32[]{:S(2)}) collective-permute-start(bf16[256,256]{1,0:T(8,128)(2,1)S(1)} %constant_dynamic-update-slice_fusion.2.refs_2_.refs_10_), channel_id=1, source_target_pairs={{0,16},{8,24},{16,0},{24,8},{32,48},{40,56},{48,32},{56,40},{64,80... | collective-permute-start | bytes 393224 | tf_op jit(solution)/shard_map/ppermute | solution.py:27
  14.2 2.6 %collective-permute-done.9 = bf16[128,640]{1,0:T(8,128)(2,1)S(1)} collective-permute-done((bf16[128,640]{1,0:T(8,128)(2,1)}, bf16[128,640]{1,0:T(8,128)(2,1)S(1)}, u32[]{:S(2)}, u32[]{:S(2)}) %collective-permute-start.9) | collective-permute-done | bytes 163872 | tf_op jit(solution)/shard_map/ppermute | solution.py:32
  16.8 1.0 %pad_maximum_fusion.refs_6_ = bf16[2,128,640]{2,1,0:T(8,128)(2,1)S(1)} fusion(bf16[1,128,640]{2,1,0:T(8,128)(2,1)S(1)} %bitcast.33, bf16[1,128,640]{2,1,0:T(8,128)(2,1)} %bitcast.32), kind=kLoop, calls=%fused_computation.2 | loop fusion | flops 163840 | bytes 655360 | tf_op jit(solution)/shard_map/stack | solution.py:330
  17.7 1.6 %collective-permute-start.12 = (bf16[2,128,640]{2,1,0:T(8,128)(2,1)S(1)}, bf16[2,128,640]{2,1,0:T(8,128)(2,1)S(1)}, u32[]{:S(2)}, u32[]{:S(2)}) collective-permute-start(bf16[2,128,640]{2,1,0:T(8,128)(2,1)S(1)} %pad_maximum_fusion.refs_6_), channel_id=1, source_target_pairs={{0,3},{1,2},{2,1},{3,0},{4,7},{5,6},{6,5},{7,4},{8,11},{9,10},{10,... | collective-permute-start | bytes 983048 | tf_op jit(solution)/shard_map/ppermute | solution.py:32
  19.3 1.1 %collective-permute-start.11 = (bf16[2,128,640]{2,1,0:T(8,128)(2,1)S(1)}, bf16[2,128,640]{2,1,0:T(8,128)(2,1)S(1)}, u32[]{:S(2)}, u32[]{:S(2)}) collective-permute-start(bf16[2,128,640]{2,1,0:T(8,128)(2,1)S(1)} %pad_maximum_fusion.refs_6_), channel_id=1, source_target_pairs={{0,2},{1,3},{2,0},{3,1},{4,6},{5,7},{6,4},{7,5},{8,10},{9,11},{10,... | collective-permute-start | bytes 983048 | tf_op jit(solution)/shard_map/ppermute | solution.py:32
  20.4 1.5 %collective-permute-start.10 = (bf16[2,128,640]{2,1,0:T(8,128)(2,1)S(1)}, bf16[2,128,640]{2,1,0:T(8,128)(2,1)S(1)}, u32[]{:S(2)}, u32[]{:S(2)}) collective-permute-start(bf16[2,128,640]{2,1,0:T(8,128)(2,1)S(1)} %pad_maximum_fusion.refs_6_), channel_id=1, source_target_pairs={{0,1},{1,0},{2,3},{3,2},{4,5},{5,4},{6,7},{7,6},{8,9},{9,8},{10,11... | collective-permute-start | bytes 983048 | tf_op jit(solution)/shard_map/ppermute | solution.py:32
  21.9 0.5 collective-permute-start.6
  22.4 0.8 %collective-permute-done.5.refs_4_.refs_9_ = bf16[256,256]{1,0:T(8,128)(2,1)S(1)} collective-permute-done((bf16[256,256]{1,0:T(8,128)(2,1)S(1)}, bf16[256,256]{1,0:T(8,128)(2,1)S(1)}, u32[]{:S(2)}, u32[]{:S(2)}) %collective-permute-start.5) | collective-permute-done | bytes 131104 | tf_op jit(solution)/shard_map/ppermute | solution.py:27
  23.8 0.8 %collective-permute-done.7.refs_6_.refs_12_ = bf16[256,256]{1,0:T(8,128)(2,1)S(1)} collective-permute-done((bf16[256,256]{1,0:T(8,128)(2,1)S(1)}, bf16[256,256]{1,0:T(8,128)(2,1)S(1)}, u32[]{:S(2)}, u32[]{:S(2)}) %collective-permute-start.7) | collective-permute-done | bytes 131104 | tf_op jit(solution)/shard_map/ppermute | solution.py:27
  24.8 0.9 %copy-done.1 = bf16[128,640]{1,0:T(8,128)(2,1)S(1)} copy-done((bf16[128,640]{1,0:T(8,128)(2,1)S(1)}, bf16[128,640]{1,0:T(8,128)(2,1)}, u32[]{:S(2)}) %copy-start.1) | copy-done | bytes 163864
  25.7 0.7 %copy-done.2 = s32[2,8,128]{2,1,0:T(8,128)S(1)} copy-done((s32[2,8,128]{2,1,0:T(8,128)S(1)}, s32[2,8,128]{2,1,0:T(8,128)}, u32[]{:S(2)}) %copy-start.2) | copy-done | bytes 8216
  26.4 2.9 %attend.1 = (bf16[8,256,640]{2,1,0:T(8,128)(2,1)S(1)}, f32[128,640]{1,0:T(8,128)S(1)}, f32[8,640]{1,0:T(8,128)S(1)}, bf16[640,5120]{1,0:T(8,128)(2,1)S(1)}) custom-call(s32[2,8,128]{2,1,0:T(8,128)S(1)} %copy-done.2, bf16[640,5120]{1,0:T(8,128)(2,1)} %w_ref.1, bf16[128,640]{1,0:T(8,128)(2,1)S(1)} %copy-done.1, ...), custom_call_target="tpu_custom_call" | custom-call | flops 671088640 | bytes 2621440 | tf_op jit(solution)/shard_map/attend/pallas_call | solution.py:236
  29.3 3.8 %collective-permute-done.12.refs_9_ = bf16[2,128,640]{2,1,0:T(8,128)(2,1)S(1)} collective-permute-done((bf16[2,128,640]{2,1,0:T(8,128)(2,1)S(1)}, bf16[2,128,640]{2,1,0:T(8,128)(2,1)S(1)}, u32[]{:S(2)}, u32[]{:S(2)}) %collective-permute-start.12) | collective-permute-done | bytes 327712 | tf_op jit(solution)/shard_map/ppermute | solution.py:32
  33.1 1.8 %collective-permute-done.10.refs_7_ = bf16[2,128,640]{2,1,0:T(8,128)(2,1)S(1)} collective-permute-done((bf16[2,128,640]{2,1,0:T(8,128)(2,1)S(1)}, bf16[2,128,640]{2,1,0:T(8,128)(2,1)S(1)}, u32[]{:S(2)}, u32[]{:S(2)}) %collective-permute-start.10) | collective-permute-done | bytes 327712 | tf_op jit(solution)/shard_map/ppermute | solution.py:32
  34.9 2.1 %far_gradients.1 = (f32[2,2,128,256]{3,2,1,0:T(8,128)S(1)}, bf16[2,2,128,256]{3,2,1,0:T(8,128)(2,1)S(1)}, bf16[128,640]{1,0:T(8,128)(2,1)S(1)}, bf16[640,128]{1,...) custom-call(s32[2,8,128]{2,1,0:T(8,128)S(1)} %copy-done.2, ...), custom_call_target="tpu_custom_call" | custom-call | flops 1509949440 | bytes 6553600 | tf_op jit(solution)/shard_map/far_gradients/pallas_call | solution.py:270
  37.1 1.5 %near_gradients.1 = (f32[2,2,128,256]{3,2,1,0:T(8,128)S(1)}, bf16[2,2,128,256]{3,2,1,0:T(8,128)(2,1)S(1)}, bf16[128,640]{1,0:T(8,128)(2,1)}) custom-call(s32[2,8,128]{2,1,0:T(8,128)S(1)} %copy-done.2, bf16[8,256,640]{2,1,0:T(8,128)(2,1)S(1)} %get-tuple-element.31.refs_5_.refs_1_, bf16[128,640]{1,0:T(8,128)(2,1)S(1)} %get-tuple-element.36.refs_2_, ...), custom_call_target="tpu_custom_call" | custom-call | flops 671088640 | bytes 1310720 | tf_op jit(solution)/shard_map/near_gradients/pallas_call | solution.py:305
  38.6 0.5 collective-permute-start.15
  39.1 1.0 %collective-permute-done.13 = bf16[2,2,128,256]{3,2,1,0:T(8,128)(2,1)S(1)} collective-permute-done((bf16[2,2,128,256]{3,2,1,0:T(8,128)(2,1)S(1)}, bf16[2,2,128,256]{3,2,1,0:T(8,128)(2,1)S(1)}, u32[]{:S(2)}, u32[]{:S(2)}) %collective-permute-start.13) | collective-permute-done | bytes 262176 | tf_op jit(solution)/shard_map/ppermute | solution.py:27
  40.2 0.7 %collective-permute-start.14 = (bf16[2,128,256]{2,1,0:T(8,128)(2,1)S(1)}, bf16[2,128,256]{2,1,0:T(8,128)(2,1)S(1)}, u32[]{:S(2)}, u32[]{:S(2)}) collective-permute-start(bf16[2,128,256]{2,1,0:T(8,128)(2,1)S(1)} %fusion.3), channel_id=1, source_target_pairs={{0,16},{8,24},{16,0},{24,8},{32,48},{40,56},{48,32},{56,40},{64,80... | collective-permute-start | bytes 393224 | tf_op jit(solution)/shard_map/ppermute | solution.py:27
  41.0 1.5 %collective-permute-start.16 = (bf16[2,128,256]{2,1,0:T(8,128)(2,1)S(1)}, bf16[2,128,256]{2,1,0:T(8,128)(2,1)S(1)}, u32[]{:S(2)}, u32[]{:S(2)}) collective-permute-start(bf16[2,128,256]{2,1,0:T(8,128)(2,1)S(1)} %fusion.4), channel_id=1, source_target_pairs={{0,16},{8,24},{16,0},{24,8},{32,48},{40,56},{48,32},{56,40},{64,80... | collective-permute-start | bytes 393224 | tf_op jit(solution)/shard_map/ppermute | solution.py:27
  42.5 4.1 %collective-permute-done.14 = bf16[2,128,256]{2,1,0:T(8,128)(2,1)S(1)} collective-permute-done((bf16[2,128,256]{2,1,0:T(8,128)(2,1)S(1)}, bf16[2,128,256]{2,1,0:T(8,128)(2,1)S(1)}, u32[]{:S(2)}, u32[]{:S(2)}) %collective-permute-start.14) | collective-permute-done | bytes 131104 | tf_op jit(solution)/shard_map/ppermute | solution.py:27
  46.7 1.7 %collective-permute-start.19 = (bf16[128,256]{1,0:T(8,128)(2,1)S(1)}, bf16[128,256]{1,0:T(8,128)(2,1)S(1)}, u32[]{:S(2)}, u32[]{:S(2)}) collective-permute-start(bf16[128,256]{1,0:T(8,128)(2,1)S(1)} %fusion.9), channel_id=1, source_target_pairs={{0,32},{8,40},{16,48},{24,56},{32,0},{40,8},{48,16},{56,24},{64,96... | collective-permute-start | bytes 196616 | tf_op jit(solution)/shard_map/ppermute | solution.py:27
  48.7 4.0 %collective-permute-start.17 = (bf16[128,256]{1,0:T(8,128)(2,1)S(1)}, bf16[128,256]{1,0:T(8,128)(2,1)S(1)}, u32[]{:S(2)}, u32[]{:S(2)}) collective-permute-start(bf16[128,256]{1,0:T(8,128)(2,1)S(1)} %get-tuple-element.45), channel_id=1, source_target_pairs={{0,64},{8,72},{16,80},{24,88},{32,96},{40,104},{48,112},{56,120},{... | collective-permute-start | bytes 196616 | tf_op jit(solution)/shard_map/ppermute | solution.py:27
  52.7 3.4 %collective-permute-done.17 = bf16[128,256]{1,0:T(8,128)(2,1)S(1)} collective-permute-done((bf16[128,256]{1,0:T(8,128)(2,1)S(1)}, bf16[128,256]{1,0:T(8,128)(2,1)S(1)}, u32[]{:S(2)}, u32[]{:S(2)}) %collective-permute-start.17) | collective-permute-done | bytes 65568 | tf_op jit(solution)/shard_map/ppermute | solution.py:27
  56.2 2.6 %collective-permute-done.18 = bf16[128,256]{1,0:T(8,128)(2,1)S(1)} collective-permute-done((bf16[128,256]{1,0:T(8,128)(2,1)S(1)}, bf16[128,256]{1,0:T(8,128)(2,1)S(1)}, u32[]{:S(2)}, u32[]{:S(2)}) %collective-permute-start.18) | collective-permute-done | bytes 65568 | tf_op jit(solution)/shard_map/ppermute | solution.py:27
  58.8 0.6 %fusion.10 = (bf16[128,128]{1,0:T(8,128)(2,1)}, bf16[128,128]{1,0:T(8,128)(2,1)}) fusion(bf16[128,256]{1,0:T(8,128)(2,1)S(1)} %fusion.8), kind=kLoop, calls=%fused_computation.25 | loop fusion | bytes 131072 | tf_op jit(solution)/shard_map/slice | solution.py:352
  (33 shorter events, 1.3 us)
Async XLA Ops:
  2.4 32.5 %copy-start = (bf16[640,128]{1,0:T(8,128)(2,1)S(1)}, bf16[640,128]{1,0:T(8,128)(2,1)}, u32[]{:S(2)}) copy-start(bf16[640,128]{1,0:T(8,128)(2,1)} %get-tuple-element.33.refs_2_.refs_4_) | copy-start | bytes 491524
  2.4 10.7 %collective-permute-start.3 = (bf16[128,256]{1,0:T(8,128)(2,1)}, bf16[128,256]{1,0:T(8,128)(2,1)S(1)}, u32[]{:S(2)}, u32[]{:S(2)}) collective-permute-start(bf16[128,256]{1,0:T(8,128)(2,1)} %get-tuple-element.26), channel_id=1, source_target_pairs={{0,96},{8,104},{16,112},{24,120},{32,64},{40,72},{48,80},{56,88},{... | collective-permute-start | bytes 196616 | tf_op jit(solution)/shard_map/ppermute | solution.py:27
  7.1 6.1 %collective-permute-start.2 = (bf16[128,256]{1,0:T(8,128)(2,1)}, bf16[128,256]{1,0:T(8,128)(2,1)S(1)}, u32[]{:S(2)}, u32[]{:S(2)}) collective-permute-start(bf16[128,256]{1,0:T(8,128)(2,1)} %get-tuple-element.26), channel_id=1, source_target_pairs={{0,64},{8,72},{16,80},{24,88},{32,96},{40,104},{48,112},{56,120},{... | collective-permute-start | bytes 196616 | tf_op jit(solution)/shard_map/ppermute | solution.py:27
  7.1 5.3 %collective-permute-start = (bf16[128,256]{1,0:T(8,128)(2,1)}, bf16[128,256]{1,0:T(8,128)(2,1)S(1)}, u32[]{:S(2)}, u32[]{:S(2)}) collective-permute-start(bf16[128,256]{1,0:T(8,128)(2,1)} %get-tuple-element.26), channel_id=1, source_target_pairs={{0,16},{8,24},{16,0},{24,8},{32,48},{40,56},{48,32},{56,40},{64,80... | collective-permute-start | bytes 196616 | tf_op jit(solution)/shard_map/ppermute | solution.py:27
  8.6 8.1 %collective-permute-start.9 = (bf16[128,640]{1,0:T(8,128)(2,1)}, bf16[128,640]{1,0:T(8,128)(2,1)S(1)}, u32[]{:S(2)}, u32[]{:S(2)}) collective-permute-start(bf16[128,640]{1,0:T(8,128)(2,1)} %param.10), channel_id=1, source_target_pairs={{0,4},{1,5},{2,6},{3,7},{4,0},{5,1},{6,2},{7,3},{8,12},{9,13},{10,... | collective-permute-start | bytes 491528 | tf_op jit(solution)/shard_map/ppermute | solution.py:32
  12.4 9.5 %collective-permute-start.1 = (bf16[256,256]{1,0:T(8,128)(2,1)S(1)}, bf16[256,256]{1,0:T(8,128)(2,1)S(1)}, u32[]{:S(2)}, u32[]{:S(2)}) collective-permute-start(bf16[256,256]{1,0:T(8,128)(2,1)S(1)} %constant_dynamic-update-slice_fusion.refs_0_.refs_7_), channel_id=1, source_target_pairs={{0,32},{8,40},{16,48},{24,56},{32,0},{40,8},{48,16},{56,24},{64,96... | collective-permute-start | bytes 393224 | tf_op jit(solution)/shard_map/ppermute | solution.py:27
  13.2 8.8 %collective-permute-start.4 = (bf16[256,256]{1,0:T(8,128)(2,1)S(1)}, bf16[256,256]{1,0:T(8,128)(2,1)S(1)}, u32[]{:S(2)}, u32[]{:S(2)}) collective-permute-start(bf16[256,256]{1,0:T(8,128)(2,1)S(1)} %constant_dynamic-update-slice_fusion.2.refs_2_.refs_10_), channel_id=1, source_target_pairs={{0,16},{8,24},{16,0},{24,8},{32,48},{40,56},{48,32},{56,40},{64,80... | collective-permute-start | bytes 393224 | tf_op jit(solution)/shard_map/ppermute | solution.py:27
  17.7 15.4 %collective-permute-start.12 = (bf16[2,128,640]{2,1,0:T(8,128)(2,1)S(1)}, bf16[2,128,640]{2,1,0:T(8,128)(2,1)S(1)}, u32[]{:S(2)}, u32[]{:S(2)}) collective-permute-start(bf16[2,128,640]{2,1,0:T(8,128)(2,1)S(1)} %pad_maximum_fusion.refs_6_), channel_id=1, source_target_pairs={{0,3},{1,2},{2,1},{3,0},{4,7},{5,6},{6,5},{7,4},{8,11},{9,10},{10,... | collective-permute-start | bytes 983048 | tf_op jit(solution)/shard_map/ppermute | solution.py:32
  19.3 13.8 %collective-permute-start.11 = (bf16[2,128,640]{2,1,0:T(8,128)(2,1)S(1)}, bf16[2,128,640]{2,1,0:T(8,128)(2,1)S(1)}, u32[]{:S(2)}, u32[]{:S(2)}) collective-permute-start(bf16[2,128,640]{2,1,0:T(8,128)(2,1)S(1)} %pad_maximum_fusion.refs_6_), channel_id=1, source_target_pairs={{0,2},{1,3},{2,0},{3,1},{4,6},{5,7},{6,4},{7,5},{8,10},{9,11},{10,... | collective-permute-start | bytes 983048 | tf_op jit(solution)/shard_map/ppermute | solution.py:32
  20.4 14.5 %collective-permute-start.10 = (bf16[2,128,640]{2,1,0:T(8,128)(2,1)S(1)}, bf16[2,128,640]{2,1,0:T(8,128)(2,1)S(1)}, u32[]{:S(2)}, u32[]{:S(2)}) collective-permute-start(bf16[2,128,640]{2,1,0:T(8,128)(2,1)S(1)} %pad_maximum_fusion.refs_6_), channel_id=1, source_target_pairs={{0,1},{1,0},{2,3},{3,2},{4,5},{5,4},{6,7},{7,6},{8,9},{9,8},{10,11... | collective-permute-start | bytes 983048 | tf_op jit(solution)/shard_map/ppermute | solution.py:32
  21.9 1.3 %collective-permute-start.5 = (bf16[256,256]{1,0:T(8,128)(2,1)S(1)}, bf16[256,256]{1,0:T(8,128)(2,1)S(1)}, u32[]{:S(2)}, u32[]{:S(2)}) collective-permute-start(bf16[256,256]{1,0:T(8,128)(2,1)S(1)} %constant_dynamic-update-slice_fusion.refs_0_.refs_7_), channel_id=1, source_target_pairs={{0,8},{8,0},{16,24},{24,16},{32,40},{40,32},{48,56},{56,48},{64,72... | collective-permute-start | bytes 393224 | tf_op jit(solution)/shard_map/ppermute | solution.py:27
  21.9 1.5 %collective-permute-start.6 = (bf16[256,256]{1,0:T(8,128)(2,1)S(1)}, bf16[256,256]{1,0:T(8,128)(2,1)S(1)}, u32[]{:S(2)}, u32[]{:S(2)}) collective-permute-start(bf16[256,256]{1,0:T(8,128)(2,1)S(1)} %collective-permute-done.1.refs_1_.refs_8_), channel_id=1, source_target_pairs={{0,8},{8,0},{16,24},{24,16},{32,40},{40,32},{48,56},{56,48},{64,72... | collective-permute-start | bytes 393224 | tf_op jit(solution)/shard_map/ppermute | solution.py:27
  23.3 1.3 %collective-permute-start.7 = (bf16[256,256]{1,0:T(8,128)(2,1)S(1)}, bf16[256,256]{1,0:T(8,128)(2,1)S(1)}, u32[]{:S(2)}, u32[]{:S(2)}) collective-permute-start(bf16[256,256]{1,0:T(8,128)(2,1)S(1)} %constant_dynamic-update-slice_fusion.2.refs_2_.refs_10_), channel_id=1, source_target_pairs={{0,8},{8,0},{16,24},{24,16},{32,40},{40,32},{48,56},{56,48},{64,72... | collective-permute-start | bytes 393224 | tf_op jit(solution)/shard_map/ppermute | solution.py:27
  23.5 1.3 %collective-permute-start.8 = (bf16[256,256]{1,0:T(8,128)(2,1)S(1)}, bf16[256,256]{1,0:T(8,128)(2,1)S(1)}, u32[]{:S(2)}, u32[]{:S(2)}) collective-permute-start(bf16[256,256]{1,0:T(8,128)(2,1)S(1)} %collective-permute-done.4.refs_3_.refs_11_), channel_id=1, source_target_pairs={{0,8},{8,0},{16,24},{24,16},{32,40},{40,32},{48,56},{56,48},{64,72... | collective-permute-start | bytes 393224 | tf_op jit(solution)/shard_map/ppermute | solution.py:27
  24.8 0.9 %copy-start.1 = (bf16[128,640]{1,0:T(8,128)(2,1)S(1)}, bf16[128,640]{1,0:T(8,128)(2,1)}, u32[]{:S(2)}) copy-start(bf16[128,640]{1,0:T(8,128)(2,1)} %get-tuple-element.25.qt_ref) | copy-start | bytes 491524
  25.7 0.7 %copy-start.2 = (s32[2,8,128]{2,1,0:T(8,128)S(1)}, s32[2,8,128]{2,1,0:T(8,128)}, u32[]{:S(2)}) copy-start(s32[2,8,128]{2,1,0:T(8,128)} %get-tuple-element.24.geo_ref.refs_0_) | copy-start | bytes 24580
  38.6 1.5 %collective-permute-start.13 = (bf16[2,2,128,256]{3,2,1,0:T(8,128)(2,1)S(1)}, bf16[2,2,128,256]{3,2,1,0:T(8,128)(2,1)S(1)}, u32[]{:S(2)}, u32[]{:S(2)}) collective-permute-start(bf16[2,2,128,256]{3,2,1,0:T(8,128)(2,1)S(1)} %get-tuple-element.42), channel_id=1, source_target_pairs={{0,8},{8,0},{16,24},{24,16},{32,40},{40,32},{48,56},{56,48},{64,72... | collective-permute-start | bytes 786440 | tf_op jit(solution)/shard_map/ppermute | solution.py:27
  38.6 2.3 %collective-permute-start.15 = (bf16[2,2,128,256]{3,2,1,0:T(8,128)(2,1)S(1)}, bf16[2,2,128,256]{3,2,1,0:T(8,128)(2,1)S(1)}, u32[]{:S(2)}, u32[]{:S(2)}) collective-permute-start(bf16[2,2,128,256]{3,2,1,0:T(8,128)(2,1)S(1)} %get-tuple-element.44), channel_id=1, source_target_pairs={{0,8},{8,0},{16,24},{24,16},{32,40},{40,32},{48,56},{56,48},{64,72... | collective-permute-start | bytes 786440 | tf_op jit(solution)/shard_map/ppermute | solution.py:27
  40.2 6.4 %collective-permute-start.14 = (bf16[2,128,256]{2,1,0:T(8,128)(2,1)S(1)}, bf16[2,128,256]{2,1,0:T(8,128)(2,1)S(1)}, u32[]{:S(2)}, u32[]{:S(2)}) collective-permute-start(bf16[2,128,256]{2,1,0:T(8,128)(2,1)S(1)} %fusion.3), channel_id=1, source_target_pairs={{0,16},{8,24},{16,0},{24,8},{32,48},{40,56},{48,32},{56,40},{64,80... | collective-permute-start | bytes 393224 | tf_op jit(solution)/shard_map/ppermute | solution.py:27
  41.0 7.6 %collective-permute-start.16 = (bf16[2,128,256]{2,1,0:T(8,128)(2,1)S(1)}, bf16[2,128,256]{2,1,0:T(8,128)(2,1)S(1)}, u32[]{:S(2)}, u32[]{:S(2)}) collective-permute-start(bf16[2,128,256]{2,1,0:T(8,128)(2,1)S(1)} %fusion.4), channel_id=1, source_target_pairs={{0,16},{8,24},{16,0},{24,8},{32,48},{40,56},{48,32},{56,40},{64,80... | collective-permute-start | bytes 393224 | tf_op jit(solution)/shard_map/ppermute | solution.py:27
  46.7 6.0 %collective-permute-start.19 = (bf16[128,256]{1,0:T(8,128)(2,1)S(1)}, bf16[128,256]{1,0:T(8,128)(2,1)S(1)}, u32[]{:S(2)}, u32[]{:S(2)}) collective-permute-start(bf16[128,256]{1,0:T(8,128)(2,1)S(1)} %fusion.9), channel_id=1, source_target_pairs={{0,32},{8,40},{16,48},{24,56},{32,0},{40,8},{48,16},{56,24},{64,96... | collective-permute-start | bytes 196616 | tf_op jit(solution)/shard_map/ppermute | solution.py:27
  48.7 7.5 %collective-permute-start.17 = (bf16[128,256]{1,0:T(8,128)(2,1)S(1)}, bf16[128,256]{1,0:T(8,128)(2,1)S(1)}, u32[]{:S(2)}, u32[]{:S(2)}) collective-permute-start(bf16[128,256]{1,0:T(8,128)(2,1)S(1)} %get-tuple-element.45), channel_id=1, source_target_pairs={{0,64},{8,72},{16,80},{24,88},{32,96},{40,104},{48,112},{56,120},{... | collective-permute-start | bytes 196616 | tf_op jit(solution)/shard_map/ppermute | solution.py:27
  52.7 6.1 %collective-permute-start.18 = (bf16[128,256]{1,0:T(8,128)(2,1)S(1)}, bf16[128,256]{1,0:T(8,128)(2,1)S(1)}, u32[]{:S(2)}, u32[]{:S(2)}) collective-permute-start(bf16[128,256]{1,0:T(8,128)(2,1)S(1)} %get-tuple-element.46), channel_id=1, source_target_pairs={{0,96},{8,104},{16,112},{24,120},{32,64},{40,72},{48,80},{56,88},{... | collective-permute-start | bytes 196616 | tf_op jit(solution)/shard_map/ppermute | solution.py:27

commit v2 on v1

--- a/solution.py
+++ b/solution.py
@@ -51,12 +51,13 @@
     return [own ^ (z * 4 + y * 2 + tile // 4) for y, z in TILE_BLOCKS[tile % 4]]
 
 
-def own_geometry(geo_ref, count):
+def own_geometry(qt_ref, count):
+    geo = qt_ref[HEAD_DIM:, :count].astype(F32)
     place = lax.axis_index("ctx")
     own = place % HALF
     base = place - own
-    low_block = jnp.maximum(jnp.min(geo_ref[0]) // count - base, 0)
-    return place, own, base, low_block
+    low_block = jnp.maximum(jnp.min(geo[0:1]).astype(jnp.int32) - base, 0)
+    return geo, place, own, base, low_block
 
 
 def tile_active(own, low_block, tile):
@@ -64,18 +65,22 @@
     return ((first <= own) & (first >= low_block)) | ((second <= own) & (second >= low_block))
 
 
+GEO_ROWS = 16
+HEAD_RUNS = (slice(0, 256), slice(256, 512), slice(512, 640))
+
+
 def fold_rows(values, reduce):
     rows, lanes = values.shape
     return reduce(values.reshape(rows // 8, 8, lanes), axis=0)
 
 
-def prepare_kernel(lens_ref, prompts_ref, k_ref, v_ref, q_ref, kv_ref, qt_ref, qs_ref, geo_ref):
+def prepare_kernel(lens_ref, prompts_ref, k_ref, v_ref, q_ref, kv_ref, qt_ref, qs_ref):
     kv_ref[:, :HEAD_DIM] = k_ref[...]
     kv_ref[:, HEAD_DIM:] = v_ref[...]
     for h in range(GROUP):
-        qt_ref[:, heads(h)] = q_ref[:, heads(h)].T
+        qt_ref[:HEAD_DIM, heads(h)] = q_ref[:, heads(h)].T
         qs_ref[heads(h), :] = q_ref[:, heads(h)]
-    rows, count = geo_ref.shape[1:]
+    rows, count = GEO_ROWS, q_ref.shape[0]
     position = lax.axis_index("ctx") * count + lax.broadcasted_iota(jnp.int32, (rows, count), 1)
     start = jnp.int32(0)
     begin = jnp.zeros((rows, count), jnp.int32)
@@ -85,19 +90,22 @@
         begin = jnp.where(position >= start, start, begin)
         answer_from = jnp.where(position >= start, answer, answer_from)
         start = start + lens_ref[s]
-    geo_ref[0] = begin
-    geo_ref[1] = jnp.where(position >= answer_from, 1, 0)
-
-
-def attend_kernel(geo_ref, w_ref, qt_ref, *refs):
+    kind = lax.broadcasted_iota(jnp.int32, (rows, count), 0)
+    answer = jnp.where(position >= answer_from, 1, 0)
+    small = jnp.where(kind == 0, begin // count, jnp.where(kind == 1, begin % count, answer))
+    qt_ref[HEAD_DIM:, :count] = small.astype(F32).astype(BF16)
+    qt_ref[HEAD_DIM:, count:] = jnp.zeros((rows, qt_ref.shape[1] - count), BF16)
+
+
+def attend_kernel(w_ref, qt_ref, *refs):
     kv_refs = refs[:TILES]
     p_ref, o_ref, inv_ref, w_out, s_ref, m_ref, l_ref, sem = refs[TILES:]
     weights = pltpu.make_async_copy(w_ref, w_out, sem)
     weights.start()
     count = kv_refs[0].shape[0] // 2
-    place, own, base, low_block = own_geometry(geo_ref, count)
+    geo, place, own, base, low_block = own_geometry(qt_ref, count)
     q_pos = place * count + lax.broadcasted_iota(jnp.int32, (count, count), 1)
-    q_start = geo_ref[0, 0:1, :]
+    q_start = (geo[0:1] * count + geo[1:2]).astype(jnp.int32)
     m_ref[...] = jnp.full(m_ref.shape, NEG, F32)
     l_ref[...] = jnp.zeros(l_ref.shape, F32)
     o_ref[...] = jnp.zeros(o_ref.shape, F32)
@@ -106,16 +114,16 @@
 
         @pl.when(tile_active(own, low_block, tile))
         def _(tile=tile):
-            biases = []
-            for block in tile_blocks(own, tile):
+            for n, block in enumerate(tile_blocks(own, tile)):
+                rows = slice(n * count, (n + 1) * count)
                 k_pos = (base + block) * count + lax.broadcasted_iota(jnp.int32, (count, count), 0)
-                biases.append(jnp.where((k_pos <= q_pos) & (k_pos >= q_start), 0.0, NEG).astype(F32))
-            bias = jnp.concatenate(biases, axis=0)
-            keys = kv_refs[tile][:, :HEAD_DIM]
-            for h in range(GROUP):
-                scores = dot_nn(keys, qt_ref[:, heads(h)]) * LOG2_SCALE + bias
-                s_ref[tile, :, heads(h)] = scores
-                m_ref[:, heads(h)] = jnp.maximum(m_ref[:, heads(h)], fold_rows(scores, jnp.max))
+                bias = jnp.where((k_pos <= q_pos) & (k_pos >= q_start), 0.0, NEG).astype(F32)
+                keys = kv_refs[tile][rows, :HEAD_DIM]
+                for run in HEAD_RUNS:
+                    wide = (run.stop - run.start) // HEAD_DIM
+                    scores = dot_nn(keys, qt_ref[:HEAD_DIM, run]) * LOG2_SCALE + jnp.concatenate([bias] * wide, axis=1)
+                    s_ref[tile, rows, run] = scores
+                    m_ref[:, run] = jnp.maximum(m_ref[:, run], fold_rows(scores, jnp.max))
 
     m_ref[...] = jnp.broadcast_to(jnp.max(m_ref[...], axis=0, keepdims=True), m_ref.shape)
 
@@ -124,12 +132,13 @@
         @pl.when(tile_active(own, low_block, tile))
         def _(tile=tile):
             values = kv_refs[tile][:, HEAD_DIM:].T
-            for h in range(GROUP):
-                probs = jnp.exp2(s_ref[tile, :, heads(h)] - m_ref[0:1, heads(h)])
-                l_ref[:, heads(h)] = l_ref[:, heads(h)] + fold_rows(probs, jnp.sum)
-                half = probs.astype(BF16)
-                p_ref[tile, :, heads(h)] = half
-                o_ref[:, heads(h)] += dot_nn(values, half)
+            for run in HEAD_RUNS:
+                for n in range(2):
+                    rows = slice(n * count, (n + 1) * count)
+                    probs = jnp.exp2(s_ref[tile, rows, run] - m_ref[0:1, run])
+                    l_ref[:, run] = l_ref[:, run] + fold_rows(probs, jnp.sum)
+                    p_ref[tile, rows, run] = probs.astype(BF16)
+                o_ref[:, run] += dot_nn(values, p_ref[tile, :, run])
 
     inverse = 1.0 / jnp.sum(l_ref[...], axis=0, keepdims=True)
     inv_ref[...] = jnp.broadcast_to(inverse, inv_ref.shape)
@@ -139,10 +148,12 @@
 def tile_gradients(tile, p_ref, kv_ref, gt_ref, g_ref, qs_ref, delta_ref, ds_ref, dqt_ref, out):
     count = out.shape[2]
     keys, values = kv_ref[:, :HEAD_DIM], kv_ref[:, HEAD_DIM:]
-    for h in range(GROUP):
-        dprobs = dot_nn(values, gt_ref[:, heads(h)])
-        probs = p_ref[tile, :, heads(h)].astype(F32)
-        ds_ref[:, heads(h)] = (probs * (dprobs - delta_ref[0:1, heads(h)])).astype(BF16)
+    for run in HEAD_RUNS:
+        for n in range(2):
+            rows = slice(n * count, (n + 1) * count)
+            dprobs = dot_nn(values[rows], gt_ref[:, run])
+            probs = p_ref[tile, rows, run].astype(F32)
+            ds_ref[rows, run] = (probs * (dprobs - delta_ref[0:1, run])).astype(BF16)
     dvalue = dot_nn(p_ref[tile], g_ref[...])
     dkey = dot_nn(ds_ref[...], qs_ref[...]) * SCALE
     dqt_ref[...] += dot_nn(keys.T, ds_ref[...])
@@ -152,8 +163,8 @@
         out[y, z % 2, :, HEAD_DIM:] = dvalue[rows].astype(out.dtype)
 
 
-def all_tiles(group, geo_ref, count, p_ref, kv_refs, gt_ref, g_ref, qs_ref, delta_ref, ds_ref, dqt_ref, keep_ref, send_ref):
-    _, own, _, low_block = own_geometry(geo_ref, count)
+def all_tiles(group, qt_ref, count, p_ref, kv_refs, gt_ref, g_ref, qs_ref, delta_ref, ds_ref, dqt_ref, keep_ref, send_ref):
+    _, _, own, _, low_block = own_geometry(qt_ref, count)
     for core, out in ((1, send_ref), (0, keep_ref)):
         for n, member in enumerate(group):
             tile = core * 4 + member
@@ -170,20 +181,21 @@
                     out[y, z % 2] = jnp.zeros(out.shape[2:], out.dtype)
 
 
-def far_kernel(group, geo_ref, w_ref, qs_ref, o_ref, inv_ref, p_ref, *refs):
-    og_refs, kv_refs = refs[:4], refs[4 : 4 + 2 * len(group)]
-    keep_ref, send_ref, gt_ref, g_ref, delta_ref, dqt_ref, ds_ref, acc_ref = refs[4 + 2 * len(group) :]
+def far_kernel(group, qt_ref, w_ref, qs_ref, o_ref, inv_ref, p_ref, *refs):
+    og_refs, kv_refs = refs[:5], refs[5 : 5 + 2 * len(group)]
+    keep_ref, send_ref, gt_ref, g_ref, delta_ref, dqt_ref, ds_ref, acc_ref = refs[5 + 2 * len(group) :]
     _, count, width = og_refs[0].shape
     mine = lax.axis_index("head")
-    parts = [(slot ^ (4 * n), slot, n) for slot in range(4) for n in range(2)]
-    for n, (slot, array, half) in enumerate(parts):
+    parts = [(0, og_refs[0][0]), (4, og_refs[0][1]), (2, og_refs[3][...]), (6, og_refs[4][...])]
+    parts += [(1, og_refs[1][0]), (5, og_refs[1][1]), (3, og_refs[2][0]), (7, og_refs[2][1])]
+    for n, (slot, block) in enumerate(parts):
         columns = pl.ds(pl.multiple_of((mine ^ slot) * width, HEAD_DIM), width)
-        part = dot_nt(w_ref[:, columns], og_refs[array][half])
+        part = dot_nt(w_ref[:, columns], block)
         if n == 0:
             acc_ref[...] = part
         else:
             acc_ref[...] += part
-    answer = geo_ref[1, 0:1, :].astype(F32)
+    answer = qt_ref[HEAD_DIM:, :count].astype(F32)[2:3]
     for h in range(GROUP):
         inverse = inv_ref[0:1, heads(h)]
         grads = (acc_ref[heads(h), :] * answer).astype(BF16).astype(F32)
@@ -193,16 +205,16 @@
         delta = jnp.sum(scaled.astype(F32) * (o_ref[:, heads(h)] * inverse), axis=0, keepdims=True)
         delta_ref[:, heads(h)] = jnp.broadcast_to(delta, (8, HEAD_DIM))
     dqt_ref[...] = jnp.zeros(dqt_ref.shape, F32)
-    all_tiles(group, geo_ref, count, p_ref, kv_refs, gt_ref, g_ref, qs_ref, delta_ref, ds_ref, dqt_ref, keep_ref, send_ref)
-
-
-def near_kernel(group, geo_ref, p_ref, gt_ref, g_ref, qs_ref, delta_ref, dqt_in, *refs):
+    all_tiles(group, qt_ref, count, p_ref, kv_refs, gt_ref, g_ref, qs_ref, delta_ref, ds_ref, dqt_ref, keep_ref, send_ref)
+
+
+def near_kernel(group, qt_ref, p_ref, gt_ref, g_ref, qs_ref, delta_ref, dqt_in, *refs):
     n_kv = 2 * len(group)
     kv_refs = refs[:n_kv]
     keep_ref, send_ref, dq_ref, ds_ref, dqt_ref = refs[n_kv:]
     count = dq_ref.shape[0]
     dqt_ref[...] = dqt_in[...]
-    all_tiles(group, geo_ref, count, p_ref, kv_refs, gt_ref, g_ref, qs_ref, delta_ref, ds_ref, dqt_ref, keep_ref, send_ref)
+    all_tiles(group, qt_ref, count, p_ref, kv_refs, gt_ref, g_ref, qs_ref, delta_ref, ds_ref, dqt_ref, keep_ref, send_ref)
     for h in range(GROUP):
         dq_ref[:, heads(h)] = (dqt_ref[:, heads(h)] * SCALE).T.astype(BF16)
 
@@ -219,17 +231,16 @@
         prepare_kernel,
         out_shape=(
             jax.ShapeDtypeStruct((count, 2 * HEAD_DIM), BF16),
-            jax.ShapeDtypeStruct((HEAD_DIM, features), BF16),
+            jax.ShapeDtypeStruct((HEAD_DIM + GEO_ROWS, features), BF16),
             jax.ShapeDtypeStruct((features, HEAD_DIM), BF16),
-            jax.ShapeDtypeStruct((2, 8, count), jnp.int32),
         ),
         in_specs=[SMEM_SPEC] * 2 + [VMEM_SPEC] * 3,
-        out_specs=(VMEM_SPEC,) * 4,
+        out_specs=(VMEM_SPEC,) * 3,
         name="prepare",
     )(seq_lengths, prompt_lengths, keys, values, queries)
 
 
-def attend(geometry, weight, query_t, kv_tiles):
+def attend(weight, query_t, kv_tiles):
     _, features = query_t.shape
     keys = kv_tiles[0].shape[0]
     flops = 2 * TILES * keys * features * HEAD_DIM
@@ -241,7 +252,7 @@
             jax.ShapeDtypeStruct((8, features), F32),
             jax.ShapeDtypeStruct(weight.shape, BF16),
         ),
-        in_specs=[VMEM_SPEC, ANY_SPEC] + [VMEM_SPEC] * (1 + TILES),
+        in_specs=[ANY_SPEC] + [VMEM_SPEC] * (1 + TILES),
         out_specs=(VMEM_SPEC,) * 4,
         scratch_shapes=[
             pltpu.VMEM((TILES, keys, features), F32),
@@ -254,10 +265,10 @@
             flops=2 * flops, bytes_accessed=TILES * keys * features * 2, transcendentals=TILES * keys * features
         ),
         name="attend",
-    )(geometry, weight, query_t, *kv_tiles)
-
-
-def far_gradients(group, geometry, weight, query_s, attended, probs, blocks, kv_tiles):
+    )(weight, query_t, *kv_tiles)
+
+
+def far_gradients(group, query_t, weight, query_s, attended, probs, blocks, kv_tiles):
     _, count, width = blocks[0].shape
     features = query_s.shape[0]
     keys = kv_tiles[0].shape[0]
@@ -288,10 +299,10 @@
             flops=4 * flops + 2 * weight.size * count, bytes_accessed=2 * weight.size, transcendentals=0
         ),
         name="far_gradients",
-    )(geometry, weight, query_s, *attended, probs, *blocks, *kv_tiles)
-
-
-def near_gradients(group, geometry, probs, shared, kv_tiles):
+    )(query_t, weight, query_s, *attended, probs, *blocks, *kv_tiles)
+
+
+def near_gradients(group, query_t, probs, shared, kv_tiles):
     features, _ = shared[1].shape
     keys = kv_tiles[0].shape[0]
     count = keys // 2
@@ -317,7 +328,7 @@
             flops=4 * flops, bytes_accessed=2 * n_kv * keys * features, transcendentals=0
         ),
         name="near_gradients",
-    )(geometry, probs, *shared, *kv_tiles)
+    )(query_t, probs, *shared, *kv_tiles)
 
 
 def over_cores_and_y(keep, send):
@@ -326,30 +337,39 @@
 
 
 def shards(queries, keys, values, out_grad, out_weight, seq_lengths, prompt_lengths):
-    own, query_t, query_s, geometry = prepare(seq_lengths, prompt_lengths, keys, values, queries)
+    own, query_t, query_s = prepare(seq_lengths, prompt_lengths, keys, values, queries)
+    own, out_grad = lax.optimization_barrier((own, out_grad))
     og_pair = jnp.stack([out_grad, head_swap(out_grad, 4)])
     reach = jnp.concatenate([ctx_swap(own, 8), ctx_swap(own, 12)], axis=0)
     pair = jnp.concatenate([own, ctx_swap(own, 2)], axis=0)
-    blocks = [og_pair] + [head_swap(og_pair, x) for x in (1, 2, 3)]
+    across = head_swap(out_grad, 2)
+    both = head_swap(across, 4)
+    blocks = [og_pair, head_swap(og_pair, 1), head_swap(og_pair, 3), across, both]
     tiles = [*lax.optimization_barrier((pair, ctx_swap(pair, 4))), *lax.optimization_barrier((reach, ctx_swap(reach, 2)))]
     tiles += [ctx_swap(tile, 1) for tile in tiles]
     far, near = (2, 3), (0, 1)
-    probs, *attended, weight = attend(geometry, out_weight, query_t, tiles)
+    probs, *attended, weight = attend(out_weight, query_t, tiles)
     far_keep, far_send, grads_t, grads, delta, dquery_t = far_gradients(
-        far, geometry, weight, query_s, attended, probs, blocks, [tiles[4 * core + n] for core in (0, 1) for n in far]
+        far, query_t, weight, query_s, attended, probs, blocks, [tiles[4 * core + n] for core in (0, 1) for n in far]
     )
     shared = (grads_t, grads, query_s, delta, dquery_t)
     near_keep, near_send, query_grad = near_gradients(
-        near, geometry, probs, shared, [tiles[4 * core + n] for core in (0, 1) for n in near]
+        near, query_t, probs, shared, [tiles[4 * core + n] for core in (0, 1) for n in near]
     )
-    far_total = over_cores_and_y(far_keep, far_send)
-    near_total = over_cores_and_y(near_keep, near_send)
-    kv_grad = near_total[0]
-    kv_grad = kv_grad + ctx_swap(far_total[0].astype(BF16), 8).astype(F32)
-    kv_grad = kv_grad + ctx_swap(far_total[1].astype(BF16), 12).astype(F32)
-    kv_grad = kv_grad + ctx_swap(near_total[1].astype(BF16), 4).astype(F32)
-    kv_grad = kv_grad.astype(BF16)
-    return (query_grad, kv_grad[:, :HEAD_DIM], kv_grad[:, HEAD_DIM:])
+    far_received, near_send = lax.optimization_barrier((ctx_swap(far_send, 1), near_send))
+    far_sum = far_keep + far_received.astype(F32)
+    near_sum = near_keep + ctx_swap(near_send, 1).astype(F32)
+    far_across = ctx_swap(far_sum[1].astype(BF16), 2)
+    near_payload = near_sum[1].astype(BF16)
+    far_across, _ = lax.optimization_barrier((far_across, near_payload))
+    far_total = far_sum[0] + far_across.astype(F32)
+    near_total = near_sum[0] + ctx_swap(near_payload, 2).astype(F32)
+    beyond = lax.optimization_barrier((far_total[0].astype(BF16), far_total[1].astype(BF16)))
+    near_total_own, beside = lax.optimization_barrier((near_total[0], near_total[1].astype(BF16)))
+    received = [near_total_own, ctx_swap(beyond[0], 8), ctx_swap(beyond[1], 12), ctx_swap(beside, 4)]
+    parts = [slice(0, HEAD_DIM), slice(HEAD_DIM, 2 * HEAD_DIM)]
+    key_grad, value_grad = [sum(array[:, p].astype(F32) for array in received).astype(BF16) for p in parts]
+    return (query_grad, key_grad, value_grad)
 
 
 def solution(mesh):

time: 59.8 us -> 55.6 us (0.930)
  waiting for transfers between devices: 21.7 us -> 15.6 us
  starting transfers between devices: 24.4 us -> 27.1 us
  local copies, waits for them, and re-layouts: 3.16 us -> 1.85 us
  other arithmetic: 1.17 us -> 1.8 us
    ppermute x4 -> x5, waiting for transfers between devices: 8.26 us -> 4.53 us  [head_swap(): return lax.ppermute(value, 'head', [(i, i ^ bits) for i in range(count)])]
    ppermute x4 -> x5, starting transfers between devices: 7.08 us -> 10.7 us  [head_swap(): return lax.ppermute(value, 'head', [(i, i ^ bits) for i in range(count)])]
    ppermute x16, waiting for transfers between devices: 13.4 us -> 11 us  [ctx_swap(): return lax.ppermute(value, 'ctx', [(i, i ^ bits) for i in range(count)])]
    ppermute x16, starting transfers between devices: 17.3 us -> 16.4 us  [ctx_swap(): return lax.ppermute(value, 'ctx', [(i, i ^ bits) for i in range(count)])]
    unnamed x8 -> x6, local copies, waits for them, and re-layouts: 2.46 us -> 1.77 us
    slice x1 -> x0, local copies, waits for them, and re-layouts: 0.63 us -> none  [shards(): return (query_grad, kv_grad[:, :HEAD_DIM], kv_grad[:, HEAD_DIM:])]
    convert_element_type x1, other arithmetic: 0.03 us -> 0.66 us  [shards(): sum((array[:, p].astype(F32) for array in received)).astype(BF16)]
  transfers between devices with their start and end apart: 20 -> 21, of which waited for: 11 -> 7; matrix products, arithmetic and copies ran while one was open for 3% -> 4% of each run, Pallas kernels for 5% -> 8%
where the time goes in v2:
time: 55.6 us; the launch traced here: 55.4 us
  starting transfers between devices  27.1 us (49%)
  waiting for transfers between devices  15.6 us (28%)
  Pallas kernels  8.3 us (15%)
  local copies, waits for them, and re-layouts  1.85 us (3%)
  other arithmetic  1.8 us (3%)
  between operations  0.77 us (1%)
    ppermute x16, starting transfers between devices, ctx_swap(): return lax.ppermute(value, 'ctx', [(i, i ^ bits) for i in range(count)])  16.4 us
    ppermute x16, waiting for transfers between devices, ctx_swap(): return lax.ppermute(value, 'ctx', [(i, i ^ bits) for i in range(count)])  11 us
    ppermute x5, starting transfers between devices, head_swap(): return lax.ppermute(value, 'head', [(i, i ^ bits) for i in range(count)])  10.7 us
    ppermute x5, waiting for transfers between devices, head_swap(): return lax.ppermute(value, 'head', [(i, i ^ bits) for i in range(count)])  4.53 us
    pallas_call x1, Pallas kernels, attend(): pl.pallas_call(attend_kernel, out_shape=(jax.ShapeDtypeStruct((TILES, key...  2.87 us
    pallas_call x1, Pallas kernels, far_gradients(): pl.pallas_call(kernel, out_shape=(jax.ShapeDtypeStruct(partial, F32), jax...  2.15 us
    pallas_call x1, Pallas kernels, prepare(): pl.pallas_call(prepare_kernel, out_shape=(jax.ShapeDtypeStruct((count, 2...  1.8 us
    unnamed x6, local copies, waits for them, and re-layouts  1.77 us
  transfers between devices with their start and end apart: 21, of which 7 were waited for; matrix products, arithmetic and copies ran while one was open for 4% of the time, Pallas kernels for 8%

profile of v2, /device:TPU:2, one launch (start us, length us, event | category | flops | bytes accessed | tf_op | source)
XLA Modules:
  0.0 55.4 jit_solution(1960681920599406698)
XLA Ops:
  0.6 1.8 %prepare.1 = (bf16[128,256]{1,0:T(8,128)(2,1)}, bf16[144,640]{1,0:T(8,128)(2,1)}, bf16[640,128]{1,0:T(8,128)(2,1)}) custom-call(s32[4]{0:T(128)} %lens_ref.1, s32[4]{0:T(128)} %prompts_ref.1, bf16[128,128]{1,0:T(8,128)(2,1)} %k_ref.1, bf16[128,128]{1,0:T(8,128)(2,1)} %v_ref.1, bf16[128,640]{1,0:T(8,128)(2,1)} %q_ref.1), custom_call_target="tpu_custom_call" | custom-call | tf_op jit(solution)/shard_map/prepare/pallas_call | solution.py:230
  2.4 4.6 %collective-permute-start.3 = (bf16[128,256]{1,0:T(8,128)(2,1)}, bf16[128,256]{1,0:T(8,128)(2,1)S(1)}, u32[]{:S(2)}, u32[]{:S(2)}) collective-permute-start(bf16[128,256]{1,0:T(8,128)(2,1)} %get-tuple-element.34), channel_id=1, source_target_pairs={{0,96},{8,104},{16,112},{24,120},{32,64},{40,72},{48,80},{56,88},{... | collective-permute-start | bytes 196616 | tf_op jit(solution)/shard_map/ppermute | solution.py:27
  7.1 1.6 %collective-permute-start = (bf16[128,256]{1,0:T(8,128)(2,1)}, bf16[128,256]{1,0:T(8,128)(2,1)S(1)}, u32[]{:S(2)}, u32[]{:S(2)}) collective-permute-start(bf16[128,256]{1,0:T(8,128)(2,1)} %get-tuple-element.34), channel_id=1, source_target_pairs={{0,16},{8,24},{16,0},{24,8},{32,48},{40,56},{48,32},{56,40},{64,80... | collective-permute-start | bytes 196616 | tf_op jit(solution)/shard_map/ppermute | solution.py:27
  8.6 2.1 %collective-permute-start.12 = (bf16[128,640]{1,0:T(8,128)(2,1)}, bf16[128,640]{1,0:T(8,128)(2,1)S(1)}, u32[]{:S(2)}, u32[]{:S(2)}) collective-permute-start(bf16[128,640]{1,0:T(8,128)(2,1)} %param.10), channel_id=1, source_target_pairs={{0,2},{1,3},{2,0},{3,1},{4,6},{5,7},{6,4},{7,5},{8,10},{9,11},{10,... | collective-permute-start | bytes 491528 | tf_op jit(solution)/shard_map/ppermute | solution.py:32
  10.8 2.9 %collective-permute-start.9 = (bf16[128,640]{1,0:T(8,128)(2,1)}, bf16[128,640]{1,0:T(8,128)(2,1)S(1)}, u32[]{:S(2)}, u32[]{:S(2)}) collective-permute-start(bf16[128,640]{1,0:T(8,128)(2,1)} %param.10), channel_id=1, source_target_pairs={{0,4},{1,5},{2,6},{3,7},{4,0},{5,1},{6,2},{7,3},{8,12},{9,13},{10,... | collective-permute-start | bytes 491528 | tf_op jit(solution)/shard_map/ppermute | solution.py:32
  13.7 0.8 %constant_dynamic-update-slice_fusion.1 = bf16[256,256]{1,0:T(8,128)(2,1)S(1)} fusion(bf16[128,256]{1,0:T(8,128)(2,1)} %get-tuple-element.34), kind=kLoop, calls=%fused_computation.20 | loop fusion | bytes 131072
  14.5 0.7 %collective-permute-start.1 = (bf16[256,256]{1,0:T(8,128)(2,1)S(1)}, bf16[256,256]{1,0:T(8,128)(2,1)S(1)}, u32[]{:S(2)}, u32[]{:S(2)}) collective-permute-start(bf16[256,256]{1,0:T(8,128)(2,1)S(1)} %constant_dynamic-update-slice_fusion.refs_0_.refs_7_), channel_id=1, source_target_pairs={{0,32},{8,40},{16,48},{24,56},{32,0},{40,8},{48,16},{56,24},{64,96... | collective-permute-start | bytes 393224 | tf_op jit(solution)/shard_map/ppermute | solution.py:27
  15.3 0.2 collective-permute-start.4
  15.5 3.4 %collective-permute-done.9 = bf16[128,640]{1,0:T(8,128)(2,1)S(1)} collective-permute-done((bf16[128,640]{1,0:T(8,128)(2,1)}, bf16[128,640]{1,0:T(8,128)(2,1)S(1)}, u32[]{:S(2)}, u32[]{:S(2)}) %collective-permute-start.9) | collective-permute-done | bytes 163872 | tf_op jit(solution)/shard_map/ppermute | solution.py:32
  18.9 1.0 %pad_maximum_fusion.refs_6_ = bf16[2,128,640]{2,1,0:T(8,128)(2,1)S(1)} fusion(bf16[1,128,640]{2,1,0:T(8,128)(2,1)S(1)} %bitcast.25, bf16[1,128,640]{2,1,0:T(8,128)(2,1)} %bitcast.24), kind=kLoop, calls=%fused_computation.2 | loop fusion | flops 163840 | bytes 655360 | tf_op jit(solution)/shard_map/stack | solution.py:342
  19.8 0.1 collective-permute-start.11
  19.9 2.6 %collective-permute-start.10 = (bf16[2,128,640]{2,1,0:T(8,128)(2,1)S(1)}, bf16[2,128,640]{2,1,0:T(8,128)(2,1)S(1)}, u32[]{:S(2)}, u32[]{:S(2)}) collective-permute-start(bf16[2,128,640]{2,1,0:T(8,128)(2,1)S(1)} %pad_maximum_fusion.refs_6_), channel_id=1, source_target_pairs={{0,1},{1,0},{2,3},{3,2},{4,5},{5,4},{6,7},{7,6},{8,9},{9,8},{10,11... | collective-permute-start | bytes 983048 | tf_op jit(solution)/shard_map/ppermute | solution.py:32
  22.5 0.5 collective-permute-start.6
  23.1 0.7 %collective-permute-done.5.refs_4_.refs_9_ = bf16[256,256]{1,0:T(8,128)(2,1)S(1)} collective-permute-done((bf16[256,256]{1,0:T(8,128)(2,1)S(1)}, bf16[256,256]{1,0:T(8,128)(2,1)S(1)}, u32[]{:S(2)}, u32[]{:S(2)}) %collective-permute-start.5) | collective-permute-done | bytes 131104 | tf_op jit(solution)/shard_map/ppermute | solution.py:27
  23.9 0.1 collective-permute-start.8
  24.1 3.0 %collective-permute-start.13 = (bf16[128,640]{1,0:T(8,128)(2,1)S(1)}, bf16[128,640]{1,0:T(8,128)(2,1)S(1)}, u32[]{:S(2)}, u32[]{:S(2)}) collective-permute-start(bf16[128,640]{1,0:T(8,128)(2,1)S(1)} %collective-permute-done.12.refs_9_), channel_id=1, source_target_pairs={{0,4},{1,5},{2,6},{3,7},{4,0},{5,1},{6,2},{7,3},{8,12},{9,13},{10,... | collective-permute-start | bytes 491528 | tf_op jit(solution)/shard_map/ppermute | solution.py:32
  27.0 0.9 %copy-done = bf16[144,640]{1,0:T(8,128)(2,1)S(1)} copy-done((bf16[144,640]{1,0:T(8,128)(2,1)S(1)}, bf16[144,640]{1,0:T(8,128)(2,1)}, u32[]{:S(2)}) %copy-start) | copy-done | bytes 184344
  28.0 2.9 %attend.1 = (bf16[8,256,640]{2,1,0:T(8,128)(2,1)S(1)}, f32[128,640]{1,0:T(8,128)S(1)}, f32[8,640]{1,0:T(8,128)S(1)}, bf16[640,5120]{1,0:T(8,128)(2,1)S(1)}) custom-call(bf16[640,5120]{1,0:T(8,128)(2,1)} %w_ref.1, bf16[144,640]{1,0:T(8,128)(2,1)S(1)} %copy-done, bf16[256,256]{1,0:T(8,128)(2,1)S(1)} %constant_dynamic-update-slice_fusion.refs_0_.refs_7_, ...), custom_call_target="tpu_custom_call" | custom-call | flops 671088640 | bytes 2621440 | tf_op jit(solution)/shard_map/attend/pallas_call | solution.py:247
  30.8 1.2 %collective-permute-done.13.refs_10_ = bf16[128,640]{1,0:T(8,128)(2,1)S(1)} collective-permute-done((bf16[128,640]{1,0:T(8,128)(2,1)S(1)}, bf16[128,640]{1,0:T(8,128)(2,1)S(1)}, u32[]{:S(2)}, u32[]{:S(2)}) %collective-permute-start.13) | collective-permute-done | bytes 163872 | tf_op jit(solution)/shard_map/ppermute | solution.py:32
  32.0 2.1 %far_gradients.1 = (f32[2,2,128,256]{3,2,1,0:T(8,128)S(1)}, bf16[2,2,128,256]{3,2,1,0:T(8,128)(2,1)S(1)}, bf16[128,640]{1,0:T(8,128)(2,1)S(1)}, bf16[640,128]{1,...) custom-call(bf16[144,640]{1,0:T(8,128)(2,1)S(1)} %copy-done, ...), custom_call_target="tpu_custom_call" | custom-call | flops 1509949440 | bytes 6553600 | tf_op jit(solution)/shard_map/far_gradients/pallas_call | solution.py:281
  34.2 0.1 collective-permute-start.14
  34.3 1.5 %near_gradients.1 = (f32[2,2,128,256]{3,2,1,0:T(8,128)S(1)}, bf16[2,2,128,256]{3,2,1,0:T(8,128)(2,1)S(1)}, bf16[128,640]{1,0:T(8,128)(2,1)}) custom-call(bf16[144,640]{1,0:T(8,128)(2,1)S(1)} %copy-done, bf16[8,256,640]{2,1,0:T(8,128)(2,1)S(1)} %get-tuple-element.39.refs_5_.refs_1_, bf16[128,640]{1,0:T(8,128)(2,1)S(1)} %get-tuple-element.45.refs_2_, ...), custom_call_target="tpu_custom_call" | custom-call | flops 671088640 | bytes 1310720 | tf_op jit(solution)/shard_map/near_gradients/pallas_call | solution.py:316
  35.8 0.9 %collective-permute-start.15 = (bf16[2,2,128,256]{3,2,1,0:T(8,128)(2,1)S(1)}, bf16[2,2,128,256]{3,2,1,0:T(8,128)(2,1)S(1)}, u32[]{:S(2)}, u32[]{:S(2)}) collective-permute-start(bf16[2,2,128,256]{3,2,1,0:T(8,128)(2,1)S(1)} %get-tuple-element.53), channel_id=1, source_target_pairs={{0,8},{8,0},{16,24},{24,16},{32,40},{40,32},{48,56},{56,48},{64,72... | collective-permute-start | bytes 786440 | tf_op jit(solution)/shard_map/ppermute | solution.py:27
  36.8 0.3 collective-permute-start.17
  37.1 0.8 %collective-permute-done.15 = bf16[2,2,128,256]{3,2,1,0:T(8,128)(2,1)S(1)} collective-permute-done((bf16[2,2,128,256]{3,2,1,0:T(8,128)(2,1)S(1)}, bf16[2,2,128,256]{3,2,1,0:T(8,128)(2,1)S(1)}, u32[]{:S(2)}, u32[]{:S(2)}) %collective-permute-start.15) | collective-permute-done | bytes 262176 | tf_op jit(solution)/shard_map/ppermute | solution.py:27
  38.0 1.1 %collective-permute-start.16 = (bf16[2,128,256]{2,1,0:T(8,128)(2,1)S(1)}, bf16[2,128,256]{2,1,0:T(8,128)(2,1)S(1)}, u32[]{:S(2)}, u32[]{:S(2)}) collective-permute-start(bf16[2,128,256]{2,1,0:T(8,128)(2,1)S(1)} %fusion.3), channel_id=1, source_target_pairs={{0,16},{8,24},{16,0},{24,8},{32,48},{40,56},{48,32},{56,40},{64,80... | collective-permute-start | bytes 393224 | tf_op jit(solution)/shard_map/ppermute | solution.py:27
  39.1 4.2 %collective-permute-done.17 = bf16[2,128,256]{2,1,0:T(8,128)(2,1)S(1)} collective-permute-done((bf16[2,128,256]{2,1,0:T(8,128)(2,1)S(1)}, bf16[2,128,256]{2,1,0:T(8,128)(2,1)S(1)}, u32[]{:S(2)}, u32[]{:S(2)}) %collective-permute-start.17) | collective-permute-done | bytes 131104 | tf_op jit(solution)/shard_map/ppermute | solution.py:27
  43.3 5.4 %collective-permute-start.18 = (bf16[128,256]{1,0:T(8,128)(2,1)S(1)}, bf16[128,256]{1,0:T(8,128)(2,1)S(1)}, u32[]{:S(2)}, u32[]{:S(2)}) collective-permute-start(bf16[128,256]{1,0:T(8,128)(2,1)S(1)} %get-tuple-element.58), channel_id=1, source_target_pairs={{0,64},{8,72},{16,80},{24,88},{32,96},{40,104},{48,112},{56,120},{... | collective-permute-start | bytes 196616 | tf_op jit(solution)/shard_map/ppermute | solution.py:27
  48.7 0.7 %collective-permute-start.20 = (bf16[128,256]{1,0:T(8,128)(2,1)S(1)}, bf16[128,256]{1,0:T(8,128)(2,1)S(1)}, u32[]{:S(2)}, u32[]{:S(2)}) collective-permute-start(bf16[128,256]{1,0:T(8,128)(2,1)S(1)} %fusion.5), channel_id=1, source_target_pairs={{0,32},{8,40},{16,48},{24,56},{32,0},{40,8},{48,16},{56,24},{64,96... | collective-permute-start | bytes 196616 | tf_op jit(solution)/shard_map/ppermute | solution.py:27
  49.5 1.4 %collective-permute-done.18 = bf16[128,256]{1,0:T(8,128)(2,1)S(1)} collective-permute-done((bf16[128,256]{1,0:T(8,128)(2,1)S(1)}, bf16[128,256]{1,0:T(8,128)(2,1)S(1)}, u32[]{:S(2)}, u32[]{:S(2)}) %collective-permute-start.18) | collective-permute-done | bytes 65568 | tf_op jit(solution)/shard_map/ppermute | solution.py:27
  50.9 3.8 %collective-permute-done.19 = bf16[128,256]{1,0:T(8,128)(2,1)S(1)} collective-permute-done((bf16[128,256]{1,0:T(8,128)(2,1)S(1)}, bf16[128,256]{1,0:T(8,128)(2,1)S(1)}, u32[]{:S(2)}, u32[]{:S(2)}) %collective-permute-start.19) | collective-permute-done | bytes 65568 | tf_op jit(solution)/shard_map/ppermute | solution.py:27
  54.7 0.7 %add_convert_fusion = (bf16[128,128]{1,0:T(8,128)(2,1)}, bf16[128,128]{1,0:T(8,128)(2,1)}) fusion(f32[128,256]{1,0:T(8,128)S(1)} %slice_bitcast_fusion.2, bf16[128,256]{1,0:T(8,128)(2,1)S(1)} %collective-permute-done.20, bf16[128,256]{1,0:T(8,128)(2,1)S(1)} %collective-permute-done.19, bf16[128,256]{1,0:T(8,128)(2,1)S(1)} %collective-permute-done.18), kind=kLoop, calls=%fused_computation.17 | loop fusion | flops 229376 | bytes 393216 | tf_op jit(solution)/shard_map/convert_element_type | solution.py:371
  (33 shorter events, 0.5 us)
Async XLA Ops:
  2.4 29.6 %copy-start.1 = (bf16[640,128]{1,0:T(8,128)(2,1)S(1)}, bf16[640,128]{1,0:T(8,128)(2,1)}, u32[]{:S(2)}) copy-start(bf16[640,128]{1,0:T(8,128)(2,1)} %get-tuple-element.41.refs_2_.refs_4_) | copy-start | bytes 491524
  2.4 12.8 %collective-permute-start.3 = (bf16[128,256]{1,0:T(8,128)(2,1)}, bf16[128,256]{1,0:T(8,128)(2,1)S(1)}, u32[]{:S(2)}, u32[]{:S(2)}) collective-permute-start(bf16[128,256]{1,0:T(8,128)(2,1)} %get-tuple-element.34), channel_id=1, source_target_pairs={{0,96},{8,104},{16,112},{24,120},{32,64},{40,72},{48,80},{56,88},{... | collective-permute-start | bytes 196616 | tf_op jit(solution)/shard_map/ppermute | solution.py:27
  7.1 8.2 %collective-permute-start.2 = (bf16[128,256]{1,0:T(8,128)(2,1)}, bf16[128,256]{1,0:T(8,128)(2,1)S(1)}, u32[]{:S(2)}, u32[]{:S(2)}) collective-permute-start(bf16[128,256]{1,0:T(8,128)(2,1)} %get-tuple-element.34), channel_id=1, source_target_pairs={{0,64},{8,72},{16,80},{24,88},{32,96},{40,104},{48,112},{56,120},{... | collective-permute-start | bytes 196616 | tf_op jit(solution)/shard_map/ppermute | solution.py:27
  7.1 7.5 %collective-permute-start = (bf16[128,256]{1,0:T(8,128)(2,1)}, bf16[128,256]{1,0:T(8,128)(2,1)S(1)}, u32[]{:S(2)}, u32[]{:S(2)}) collective-permute-start(bf16[128,256]{1,0:T(8,128)(2,1)} %get-tuple-element.34), channel_id=1, source_target_pairs={{0,16},{8,24},{16,0},{24,8},{32,48},{40,56},{48,32},{56,40},{64,80... | collective-permute-start | bytes 196616 | tf_op jit(solution)/shard_map/ppermute | solution.py:27
  8.6 14.4 %collective-permute-start.12 = (bf16[128,640]{1,0:T(8,128)(2,1)}, bf16[128,640]{1,0:T(8,128)(2,1)S(1)}, u32[]{:S(2)}, u32[]{:S(2)}) collective-permute-start(bf16[128,640]{1,0:T(8,128)(2,1)} %param.10), channel_id=1, source_target_pairs={{0,2},{1,3},{2,0},{3,1},{4,6},{5,7},{6,4},{7,5},{8,10},{9,11},{10,... | collective-permute-start | bytes 491528 | tf_op jit(solution)/shard_map/ppermute | solution.py:32
  10.8 8.1 %collective-permute-start.9 = (bf16[128,640]{1,0:T(8,128)(2,1)}, bf16[128,640]{1,0:T(8,128)(2,1)S(1)}, u32[]{:S(2)}, u32[]{:S(2)}) collective-permute-start(bf16[128,640]{1,0:T(8,128)(2,1)} %param.10), channel_id=1, source_target_pairs={{0,4},{1,5},{2,6},{3,7},{4,0},{5,1},{6,2},{7,3},{8,12},{9,13},{10,... | collective-permute-start | bytes 491528 | tf_op jit(solution)/shard_map/ppermute | solution.py:32
  14.5 8.0 %collective-permute-start.1 = (bf16[256,256]{1,0:T(8,128)(2,1)S(1)}, bf16[256,256]{1,0:T(8,128)(2,1)S(1)}, u32[]{:S(2)}, u32[]{:S(2)}) collective-permute-start(bf16[256,256]{1,0:T(8,128)(2,1)S(1)} %constant_dynamic-update-slice_fusion.refs_0_.refs_7_), channel_id=1, source_target_pairs={{0,32},{8,40},{16,48},{24,56},{32,0},{40,8},{48,16},{56,24},{64,96... | collective-permute-start | bytes 393224 | tf_op jit(solution)/shard_map/ppermute | solution.py:27
  15.3 7.2 %collective-permute-start.4 = (bf16[256,256]{1,0:T(8,128)(2,1)S(1)}, bf16[256,256]{1,0:T(8,128)(2,1)S(1)}, u32[]{:S(2)}, u32[]{:S(2)}) collective-permute-start(bf16[256,256]{1,0:T(8,128)(2,1)S(1)} %constant_dynamic-update-slice_fusion.2.refs_2_.refs_11_), channel_id=1, source_target_pairs={{0,16},{8,24},{16,0},{24,8},{32,48},{40,56},{48,32},{56,40},{64,80... | collective-permute-start | bytes 393224 | tf_op jit(solution)/shard_map/ppermute | solution.py:27
  19.8 12.2 %collective-permute-start.11 = (bf16[2,128,640]{2,1,0:T(8,128)(2,1)S(1)}, bf16[2,128,640]{2,1,0:T(8,128)(2,1)S(1)}, u32[]{:S(2)}, u32[]{:S(2)}) collective-permute-start(bf16[2,128,640]{2,1,0:T(8,128)(2,1)S(1)} %pad_maximum_fusion.refs_6_), channel_id=1, source_target_pairs={{0,3},{1,2},{2,1},{3,0},{4,7},{5,6},{6,5},{7,4},{8,11},{9,10},{10,... | collective-permute-start | bytes 983048 | tf_op jit(solution)/shard_map/ppermute | solution.py:32
  19.9 12.1 %collective-permute-start.10 = (bf16[2,128,640]{2,1,0:T(8,128)(2,1)S(1)}, bf16[2,128,640]{2,1,0:T(8,128)(2,1)S(1)}, u32[]{:S(2)}, u32[]{:S(2)}) collective-permute-start(bf16[2,128,640]{2,1,0:T(8,128)(2,1)S(1)} %pad_maximum_fusion.refs_6_), channel_id=1, source_target_pairs={{0,1},{1,0},{2,3},{3,2},{4,5},{5,4},{6,7},{7,6},{8,9},{9,8},{10,11... | collective-permute-start | bytes 983048 | tf_op jit(solution)/shard_map/ppermute | solution.py:32
  22.5 1.3 %collective-permute-start.5 = (bf16[256,256]{1,0:T(8,128)(2,1)S(1)}, bf16[256,256]{1,0:T(8,128)(2,1)S(1)}, u32[]{:S(2)}, u32[]{:S(2)}) collective-permute-start(bf16[256,256]{1,0:T(8,128)(2,1)S(1)} %constant_dynamic-update-slice_fusion.refs_0_.refs_7_), channel_id=1, source_target_pairs={{0,8},{8,0},{16,24},{24,16},{32,40},{40,32},{48,56},{56,48},{64,72... | collective-permute-start | bytes 393224 | tf_op jit(solution)/shard_map/ppermute | solution.py:27
  22.5 1.5 %collective-permute-start.6 = (bf16[256,256]{1,0:T(8,128)(2,1)S(1)}, bf16[256,256]{1,0:T(8,128)(2,1)S(1)}, u32[]{:S(2)}, u32[]{:S(2)}) collective-permute-start(bf16[256,256]{1,0:T(8,128)(2,1)S(1)} %collective-permute-done.1.refs_1_.refs_8_), channel_id=1, source_target_pairs={{0,8},{8,0},{16,24},{24,16},{32,40},{40,32},{48,56},{56,48},{64,72... | collective-permute-start | bytes 393224 | tf_op jit(solution)/shard_map/ppermute | solution.py:27
  23.0 4.0 %collective-permute-start.7 = (bf16[256,256]{1,0:T(8,128)(2,1)S(1)}, bf16[256,256]{1,0:T(8,128)(2,1)S(1)}, u32[]{:S(2)}, u32[]{:S(2)}) collective-permute-start(bf16[256,256]{1,0:T(8,128)(2,1)S(1)} %constant_dynamic-update-slice_fusion.2.refs_2_.refs_11_), channel_id=1, source_target_pairs={{0,8},{8,0},{16,24},{24,16},{32,40},{40,32},{48,56},{56,48},{64,72... | collective-permute-start | bytes 393224 | tf_op jit(solution)/shard_map/ppermute | solution.py:27
  23.9 3.2 %collective-permute-start.8 = (bf16[256,256]{1,0:T(8,128)(2,1)S(1)}, bf16[256,256]{1,0:T(8,128)(2,1)S(1)}, u32[]{:S(2)}, u32[]{:S(2)}) collective-permute-start(bf16[256,256]{1,0:T(8,128)(2,1)S(1)} %collective-permute-done.4.refs_3_.refs_12_), channel_id=1, source_target_pairs={{0,8},{8,0},{16,24},{24,16},{32,40},{40,32},{48,56},{56,48},{64,72... | collective-permute-start | bytes 393224 | tf_op jit(solution)/shard_map/ppermute | solution.py:27
  24.1 7.9 %collective-permute-start.13 = (bf16[128,640]{1,0:T(8,128)(2,1)S(1)}, bf16[128,640]{1,0:T(8,128)(2,1)S(1)}, u32[]{:S(2)}, u32[]{:S(2)}) collective-permute-start(bf16[128,640]{1,0:T(8,128)(2,1)S(1)} %collective-permute-done.12.refs_9_), channel_id=1, source_target_pairs={{0,4},{1,5},{2,6},{3,7},{4,0},{5,1},{6,2},{7,3},{8,12},{9,13},{10,... | collective-permute-start | bytes 491528 | tf_op jit(solution)/shard_map/ppermute | solution.py:32
  27.0 0.9 %copy-start = (bf16[144,640]{1,0:T(8,128)(2,1)S(1)}, bf16[144,640]{1,0:T(8,128)(2,1)}, u32[]{:S(2)}) copy-start(bf16[144,640]{1,0:T(8,128)(2,1)} %get-tuple-element.32.qt_ref.refs_0_) | copy-start | bytes 552964
  34.2 1.6 %collective-permute-start.14 = (bf16[2,2,128,256]{3,2,1,0:T(8,128)(2,1)S(1)}, bf16[2,2,128,256]{3,2,1,0:T(8,128)(2,1)S(1)}, u32[]{:S(2)}, u32[]{:S(2)}) collective-permute-start(bf16[2,2,128,256]{3,2,1,0:T(8,128)(2,1)S(1)} %get-tuple-element.51), channel_id=1, source_target_pairs={{0,8},{8,0},{16,24},{24,16},{32,40},{40,32},{48,56},{56,48},{64,72... | collective-permute-start | bytes 786440 | tf_op jit(solution)/shard_map/ppermute | solution.py:27
  35.8 2.1 %collective-permute-start.15 = (bf16[2,2,128,256]{3,2,1,0:T(8,128)(2,1)S(1)}, bf16[2,2,128,256]{3,2,1,0:T(8,128)(2,1)S(1)}, u32[]{:S(2)}, u32[]{:S(2)}) collective-permute-start(bf16[2,2,128,256]{3,2,1,0:T(8,128)(2,1)S(1)} %get-tuple-element.53), channel_id=1, source_target_pairs={{0,8},{8,0},{16,24},{24,16},{32,40},{40,32},{48,56},{56,48},{64,72... | collective-permute-start | bytes 786440 | tf_op jit(solution)/shard_map/ppermute | solution.py:27
  36.8 6.5 %collective-permute-start.17 = (bf16[2,128,256]{2,1,0:T(8,128)(2,1)S(1)}, bf16[2,128,256]{2,1,0:T(8,128)(2,1)S(1)}, u32[]{:S(2)}, u32[]{:S(2)}) collective-permute-start(bf16[2,128,256]{2,1,0:T(8,128)(2,1)S(1)} %fusion.4), channel_id=1, source_target_pairs={{0,16},{8,24},{16,0},{24,8},{32,48},{40,56},{48,32},{56,40},{64,80... | collective-permute-start | bytes 393224 | tf_op jit(solution)/shard_map/ppermute | solution.py:27
  38.0 10.7 %collective-permute-start.16 = (bf16[2,128,256]{2,1,0:T(8,128)(2,1)S(1)}, bf16[2,128,256]{2,1,0:T(8,128)(2,1)S(1)}, u32[]{:S(2)}, u32[]{:S(2)}) collective-permute-start(bf16[2,128,256]{2,1,0:T(8,128)(2,1)S(1)} %fusion.3), channel_id=1, source_target_pairs={{0,16},{8,24},{16,0},{24,8},{32,48},{40,56},{48,32},{56,40},{64,80... | collective-permute-start | bytes 393224 | tf_op jit(solution)/shard_map/ppermute | solution.py:27
  43.3 7.6 %collective-permute-start.18 = (bf16[128,256]{1,0:T(8,128)(2,1)S(1)}, bf16[128,256]{1,0:T(8,128)(2,1)S(1)}, u32[]{:S(2)}, u32[]{:S(2)}) collective-permute-start(bf16[128,256]{1,0:T(8,128)(2,1)S(1)} %get-tuple-element.58), channel_id=1, source_target_pairs={{0,64},{8,72},{16,80},{24,88},{32,96},{40,104},{48,112},{56,120},{... | collective-permute-start | bytes 196616 | tf_op jit(solution)/shard_map/ppermute | solution.py:27
  48.7 6.1 %collective-permute-start.19 = (bf16[128,256]{1,0:T(8,128)(2,1)S(1)}, bf16[128,256]{1,0:T(8,128)(2,1)S(1)}, u32[]{:S(2)}, u32[]{:S(2)}) collective-permute-start(bf16[128,256]{1,0:T(8,128)(2,1)S(1)} %get-tuple-element.59), channel_id=1, source_target_pairs={{0,96},{8,104},{16,112},{24,120},{32,64},{40,72},{48,80},{56,88},{... | collective-permute-start | bytes 196616 | tf_op jit(solution)/shard_map/ppermute | solution.py:27
  48.7 6.0 %collective-permute-start.20 = (bf16[128,256]{1,0:T(8,128)(2,1)S(1)}, bf16[128,256]{1,0:T(8,128)(2,1)S(1)}, u32[]{:S(2)}, u32[]{:S(2)}) collective-permute-start(bf16[128,256]{1,0:T(8,128)(2,1)S(1)} %fusion.5), channel_id=1, source_target_pairs={{0,32},{8,40},{16,48},{24,56},{32,0},{40,8},{48,16},{56,24},{64,96... | collective-permute-start | bytes 196616 | tf_op jit(solution)/shard_map/ppermute | solution.py:27

commit v3 on v2

--- a/solution.py
+++ b/solution.py
@@ -25,6 +25,11 @@
 def ctx_swap(value, bits):
     count = lax.axis_size("ctx")
     return lax.ppermute(value, "ctx", [(i, i ^ bits) for i in range(count)])
+
+
+def send_back(value, bits):
+    count = lax.axis_size("ctx")
+    return lax.ppermute(value, "ctx", [(i, i ^ bits) for i in range(count) if i ^ bits < i])
 
 
 def head_swap(value, bits):
@@ -163,12 +168,12 @@
         out[y, z % 2, :, HEAD_DIM:] = dvalue[rows].astype(out.dtype)
 
 
-def all_tiles(group, qt_ref, count, p_ref, kv_refs, gt_ref, g_ref, qs_ref, delta_ref, ds_ref, dqt_ref, keep_ref, send_ref):
+def all_tiles(outs, group, qt_ref, count, p_ref, kv_refs, gt_ref, g_ref, qs_ref, delta_ref, ds_ref, dqt_ref):
     _, _, own, _, low_block = own_geometry(qt_ref, count)
-    for core, out in ((1, send_ref), (0, keep_ref)):
+    for n_core, (core, out) in enumerate(outs):
         for n, member in enumerate(group):
             tile = core * 4 + member
-            kv_ref = kv_refs[core * len(group) + n]
+            kv_ref = kv_refs[n_core * len(group) + n]
             active = tile_active(own, low_block, tile)
 
             @pl.when(active)
@@ -205,18 +210,21 @@
         delta = jnp.sum(scaled.astype(F32) * (o_ref[:, heads(h)] * inverse), axis=0, keepdims=True)
         delta_ref[:, heads(h)] = jnp.broadcast_to(delta, (8, HEAD_DIM))
     dqt_ref[...] = jnp.zeros(dqt_ref.shape, F32)
-    all_tiles(group, qt_ref, count, p_ref, kv_refs, gt_ref, g_ref, qs_ref, delta_ref, ds_ref, dqt_ref, keep_ref, send_ref)
-
-
-def near_kernel(group, qt_ref, p_ref, gt_ref, g_ref, qs_ref, delta_ref, dqt_in, *refs):
-    n_kv = 2 * len(group)
-    kv_refs = refs[:n_kv]
-    keep_ref, send_ref, dq_ref, ds_ref, dqt_ref = refs[n_kv:]
-    count = dq_ref.shape[0]
+    outs = ((1, send_ref), (0, keep_ref))
+    all_tiles(outs, group, qt_ref, count, p_ref, kv_refs, gt_ref, g_ref, qs_ref, delta_ref, ds_ref, dqt_ref)
+
+
+def near_kernel(core, group, qt_ref, p_ref, gt_ref, g_ref, qs_ref, delta_ref, dqt_in, *refs):
+    kv_refs = refs[: len(group)]
+    out_ref, result_ref, ds_ref, dqt_ref = refs[len(group) :]
+    count = out_ref.shape[2]
     dqt_ref[...] = dqt_in[...]
-    all_tiles(group, qt_ref, count, p_ref, kv_refs, gt_ref, g_ref, qs_ref, delta_ref, ds_ref, dqt_ref, keep_ref, send_ref)
-    for h in range(GROUP):
-        dq_ref[:, heads(h)] = (dqt_ref[:, heads(h)] * SCALE).T.astype(BF16)
+    all_tiles(((core, out_ref),), group, qt_ref, count, p_ref, kv_refs, gt_ref, g_ref, qs_ref, delta_ref, ds_ref, dqt_ref)
+    if core == 1:
+        result_ref[...] = dqt_ref[...]
+    else:
+        for h in range(GROUP):
+            result_ref[:, heads(h)] = (dqt_ref[:, heads(h)] * SCALE).T.astype(BF16)
 
 
 VMEM_SPEC = pl.BlockSpec(memory_space=pltpu.VMEM)
@@ -302,26 +310,26 @@
     )(query_t, weight, query_s, *attended, probs, *blocks, *kv_tiles)
 
 
-def near_gradients(group, query_t, probs, shared, kv_tiles):
+def near_gradients(core, group, query_t, probs, shared, kv_tiles):
     features, _ = shared[1].shape
     keys = kv_tiles[0].shape[0]
     count = keys // 2
     n_kv = len(kv_tiles)
     flops = 2 * n_kv * keys * features * HEAD_DIM
     partial = (2, len(group), count, 2 * HEAD_DIM)
+    result = ((HEAD_DIM, features), F32) if core == 1 else ((count, features), BF16)
 
     def kernel(*refs):
-        near_kernel(group, *refs)
+        near_kernel(core, group, *refs)
 
     return pl.pallas_call(
         kernel,
         out_shape=(
-            jax.ShapeDtypeStruct(partial, F32),
-            jax.ShapeDtypeStruct(partial, BF16),
-            jax.ShapeDtypeStruct((count, features), BF16),
+            jax.ShapeDtypeStruct(partial, BF16 if core == 1 else F32),
+            jax.ShapeDtypeStruct(*result),
         ),
         in_specs=[VMEM_SPEC] * (7 + n_kv),
-        out_specs=(VMEM_SPEC,) * 3,
+        out_specs=(VMEM_SPEC,) * 2,
         scratch_shapes=[pltpu.VMEM((keys, features), BF16), pltpu.VMEM((HEAD_DIM, features), F32)],
         compiler_params=PARAMS,
         cost_estimate=pl.CostEstimate(
@@ -329,11 +337,6 @@
         ),
         name="near_gradients",
     )(query_t, probs, *shared, *kv_tiles)
-
-
-def over_cores_and_y(keep, send):
-    total = keep + ctx_swap(send, 1).astype(F32)
-    return total[0] + ctx_swap(total[1].astype(BF16), 2).astype(F32)
 
 
 def shards(queries, keys, values, out_grad, out_weight, seq_lengths, prompt_lengths):
@@ -350,23 +353,24 @@
     far, near = (2, 3), (0, 1)
     probs, *attended, weight = attend(out_weight, query_t, tiles)
     far_keep, far_send, grads_t, grads, delta, dquery_t = far_gradients(
-        far, query_t, weight, query_s, attended, probs, blocks, [tiles[4 * core + n] for core in (0, 1) for n in far]
+        far, query_t, weight, query_s, attended, probs, blocks, [tiles[4 * core + n] for core in (1, 0) for n in far]
     )
-    shared = (grads_t, grads, query_s, delta, dquery_t)
-    near_keep, near_send, query_grad = near_gradients(
-        near, query_t, probs, shared, [tiles[4 * core + n] for core in (0, 1) for n in near]
-    )
+    shared = (grads_t, grads, query_s, delta)
+    near_send, dquery_t = near_gradients(1, near, query_t, probs, (*shared, dquery_t), [tiles[4 + n] for n in near])
     far_received, near_send = lax.optimization_barrier((ctx_swap(far_send, 1), near_send))
     far_sum = far_keep + far_received.astype(F32)
+    far_payload = far_sum[1].astype(BF16)
+    dquery_t, _ = lax.optimization_barrier((dquery_t, far_payload))
+    near_keep, query_grad = near_gradients(0, near, query_t, probs, (*shared, dquery_t), [tiles[n] for n in near])
     near_sum = near_keep + ctx_swap(near_send, 1).astype(F32)
-    far_across = ctx_swap(far_sum[1].astype(BF16), 2)
+    far_across = ctx_swap(far_payload, 2)
     near_payload = near_sum[1].astype(BF16)
     far_across, _ = lax.optimization_barrier((far_across, near_payload))
     far_total = far_sum[0] + far_across.astype(F32)
     near_total = near_sum[0] + ctx_swap(near_payload, 2).astype(F32)
     beyond = lax.optimization_barrier((far_total[0].astype(BF16), far_total[1].astype(BF16)))
     near_total_own, beside = lax.optimization_barrier((near_total[0], near_total[1].astype(BF16)))
-    received = [near_total_own, ctx_swap(beyond[0], 8), ctx_swap(beyond[1], 12), ctx_swap(beside, 4)]
+    received = [near_total_own, send_back(beyond[0], 8), send_back(beyond[1], 12), ctx_swap(beside, 4)]
     parts = [slice(0, HEAD_DIM), slice(HEAD_DIM, 2 * HEAD_DIM)]
     key_grad, value_grad = [sum(array[:, p].astype(F32) for array in received).astype(BF16) for p in parts]
     return (query_grad, key_grad, value_grad)

time: 55.6 us -> 53.6 us (0.964)
  starting transfers between devices: 27.1 us -> 24.6 us
    ppermute x0 -> x2, waiting for transfers between devices: none -> 6.49 us  [send_back(): lax.ppermute(value, 'ctx', [(i, i ^ bits) for i in range(count) if i ^ bi...]
    ppermute x16 -> x14, waiting for transfers between devices: 11 us -> 4.78 us  [ctx_swap(): return lax.ppermute(value, 'ctx', [(i, i ^ bits) for i in range(count)])]
    ppermute x16 -> x14, starting transfers between devices: 16.4 us -> 11.4 us  [ctx_swap(): return lax.ppermute(value, 'ctx', [(i, i ^ bits) for i in range(count)])]
    ppermute x0 -> x2, starting transfers between devices: none -> 2.58 us  [send_back(): lax.ppermute(value, 'ctx', [(i, i ^ bits) for i in range(count) if i ^ bi...]
    pallas_call x1 -> x2, Pallas kernels: 1.48 us -> 1.65 us  [near_gradients(): pl.pallas_call(kernel, out_shape=(jax.ShapeDtypeStruct(partial, BF16 if c...]
  transfers between devices with their start and end apart: 21 -> 21, of which waited for: 7 -> 6; matrix products, arithmetic and copies ran while one was open for 4% -> 4% of each run, Pallas kernels for 8% -> 8%
where the time goes in v3:
time: 53.6 us; the launch traced here: 53.3 us
  starting transfers between devices  24.6 us (46%)
  waiting for transfers between devices  15.8 us (29%)
  Pallas kernels  8.46 us (16%)
  local copies, waits for them, and re-layouts  1.85 us (3%)
  other arithmetic  1.79 us (3%)
  between operations  0.81 us (2%)
    ppermute x14, starting transfers between devices, ctx_swap(): return lax.ppermute(value, 'ctx', [(i, i ^ bits) for i in range(count)])  11.4 us
    ppermute x5, starting transfers between devices, head_swap(): return lax.ppermute(value, 'head', [(i, i ^ bits) for i in range(count)])  10.7 us
    ppermute x2, waiting for transfers between devices, send_back(): lax.ppermute(value, 'ctx', [(i, i ^ bits) for i in range(count) if i ^ bi...  6.49 us
    ppermute x14, waiting for transfers between devices, ctx_swap(): return lax.ppermute(value, 'ctx', [(i, i ^ bits) for i in range(count)])  4.78 us
    ppermute x5, waiting for transfers between devices, head_swap(): return lax.ppermute(value, 'head', [(i, i ^ bits) for i in range(count)])  4.53 us
    pallas_call x1, Pallas kernels, attend(): pl.pallas_call(attend_kernel, out_shape=(jax.ShapeDtypeStruct((TILES, key...  2.87 us
    ppermute x2, starting transfers between devices, send_back(): lax.ppermute(value, 'ctx', [(i, i ^ bits) for i in range(count) if i ^ bi...  2.58 us
    pallas_call x1, Pallas kernels, far_gradients(): pl.pallas_call(kernel, out_shape=(jax.ShapeDtypeStruct(partial, F32), jax...  2.14 us
  transfers between devices with their start and end apart: 21, of which 6 were waited for; matrix products, arithmetic and copies ran while one was open for 4% of the time, Pallas kernels for 8%

profile of v3, /device:TPU:2, one launch (start us, length us, event | category | flops | bytes accessed | tf_op | source)
XLA Modules:
  0.0 53.3 jit_solution(7016158178819030770)
XLA Ops:
  0.6 1.8 %prepare.1 = (bf16[128,256]{1,0:T(8,128)(2,1)}, bf16[144,640]{1,0:T(8,128)(2,1)}, bf16[640,128]{1,0:T(8,128)(2,1)}) custom-call(s32[4]{0:T(128)} %lens_ref.1, s32[4]{0:T(128)} %prompts_ref.1, bf16[128,128]{1,0:T(8,128)(2,1)} %k_ref.1, bf16[128,128]{1,0:T(8,128)(2,1)} %v_ref.1, bf16[128,640]{1,0:T(8,128)(2,1)} %q_ref.1), custom_call_target="tpu_custom_call" | custom-call | tf_op jit(solution)/shard_map/prepare/pallas_call | solution.py:238
  2.4 4.6 %collective-permute-start.3 = (bf16[128,256]{1,0:T(8,128)(2,1)}, bf16[128,256]{1,0:T(8,128)(2,1)S(1)}, u32[]{:S(2)}, u32[]{:S(2)}) collective-permute-start(bf16[128,256]{1,0:T(8,128)(2,1)} %get-tuple-element.36), channel_id=1, source_target_pairs={{0,96},{8,104},{16,112},{24,120},{32,64},{40,72},{48,80},{56,88},{... | collective-permute-start | bytes 196616 | tf_op jit(solution)/shard_map/ppermute | solution.py:27
  7.1 1.6 %collective-permute-start = (bf16[128,256]{1,0:T(8,128)(2,1)}, bf16[128,256]{1,0:T(8,128)(2,1)S(1)}, u32[]{:S(2)}, u32[]{:S(2)}) collective-permute-start(bf16[128,256]{1,0:T(8,128)(2,1)} %get-tuple-element.36), channel_id=1, source_target_pairs={{0,16},{8,24},{16,0},{24,8},{32,48},{40,56},{48,32},{56,40},{64,80... | collective-permute-start | bytes 196616 | tf_op jit(solution)/shard_map/ppermute | solution.py:27
  8.6 2.1 %collective-permute-start.12 = (bf16[128,640]{1,0:T(8,128)(2,1)}, bf16[128,640]{1,0:T(8,128)(2,1)S(1)}, u32[]{:S(2)}, u32[]{:S(2)}) collective-permute-start(bf16[128,640]{1,0:T(8,128)(2,1)} %param.10), channel_id=1, source_target_pairs={{0,2},{1,3},{2,0},{3,1},{4,6},{5,7},{6,4},{7,5},{8,10},{9,11},{10,... | collective-permute-start | bytes 491528 | tf_op jit(solution)/shard_map/ppermute | solution.py:37
  10.8 2.9 %collective-permute-start.9 = (bf16[128,640]{1,0:T(8,128)(2,1)}, bf16[128,640]{1,0:T(8,128)(2,1)S(1)}, u32[]{:S(2)}, u32[]{:S(2)}) collective-permute-start(bf16[128,640]{1,0:T(8,128)(2,1)} %param.10), channel_id=1, source_target_pairs={{0,4},{1,5},{2,6},{3,7},{4,0},{5,1},{6,2},{7,3},{8,12},{9,13},{10,... | collective-permute-start | bytes 491528 | tf_op jit(solution)/shard_map/ppermute | solution.py:37
  13.7 0.8 %constant_dynamic-update-slice_fusion.1 = bf16[256,256]{1,0:T(8,128)(2,1)S(1)} fusion(bf16[128,256]{1,0:T(8,128)(2,1)} %get-tuple-element.36), kind=kLoop, calls=%fused_computation.20 | loop fusion | bytes 131072
  14.5 0.7 %collective-permute-start.1 = (bf16[256,256]{1,0:T(8,128)(2,1)S(1)}, bf16[256,256]{1,0:T(8,128)(2,1)S(1)}, u32[]{:S(2)}, u32[]{:S(2)}) collective-permute-start(bf16[256,256]{1,0:T(8,128)(2,1)S(1)} %constant_dynamic-update-slice_fusion.refs_0_.refs_7_), channel_id=1, source_target_pairs={{0,32},{8,40},{16,48},{24,56},{32,0},{40,8},{48,16},{56,24},{64,96... | collective-permute-start | bytes 393224 | tf_op jit(solution)/shard_map/ppermute | solution.py:27
  15.3 0.2 collective-permute-start.4
  15.5 3.4 %collective-permute-done.9 = bf16[128,640]{1,0:T(8,128)(2,1)S(1)} collective-permute-done((bf16[128,640]{1,0:T(8,128)(2,1)}, bf16[128,640]{1,0:T(8,128)(2,1)S(1)}, u32[]{:S(2)}, u32[]{:S(2)}) %collective-permute-start.9) | collective-permute-done | bytes 163872 | tf_op jit(solution)/shard_map/ppermute | solution.py:37
  18.9 1.0 %pad_maximum_fusion.refs_6_ = bf16[2,128,640]{2,1,0:T(8,128)(2,1)S(1)} fusion(bf16[1,128,640]{2,1,0:T(8,128)(2,1)S(1)} %bitcast.25, bf16[1,128,640]{2,1,0:T(8,128)(2,1)} %bitcast.24), kind=kLoop, calls=%fused_computation.2 | loop fusion | flops 163840 | bytes 655360 | tf_op jit(solution)/shard_map/stack | solution.py:345
  19.9 2.6 %collective-permute-start.10 = (bf16[2,128,640]{2,1,0:T(8,128)(2,1)S(1)}, bf16[2,128,640]{2,1,0:T(8,128)(2,1)S(1)}, u32[]{:S(2)}, u32[]{:S(2)}) collective-permute-start(bf16[2,128,640]{2,1,0:T(8,128)(2,1)S(1)} %pad_maximum_fusion.refs_6_), channel_id=1, source_target_pairs={{0,1},{1,0},{2,3},{3,2},{4,5},{5,4},{6,7},{7,6},{8,9},{9,8},{10,11... | collective-permute-start | bytes 983048 | tf_op jit(solution)/shard_map/ppermute | solution.py:37
  22.5 0.5 collective-permute-start.6
  23.1 0.7 %collective-permute-done.5.refs_4_.refs_7_ = bf16[256,256]{1,0:T(8,128)(2,1)S(1)} collective-permute-done((bf16[256,256]{1,0:T(8,128)(2,1)S(1)}, bf16[256,256]{1,0:T(8,128)(2,1)S(1)}, u32[]{:S(2)}, u32[]{:S(2)}) %collective-permute-start.5) | collective-permute-done | bytes 131104 | tf_op jit(solution)/shard_map/ppermute | solution.py:27
  23.9 0.1 collective-permute-start.8
  24.1 3.0 %collective-permute-start.13 = (bf16[128,640]{1,0:T(8,128)(2,1)S(1)}, bf16[128,640]{1,0:T(8,128)(2,1)S(1)}, u32[]{:S(2)}, u32[]{:S(2)}) collective-permute-start(bf16[128,640]{1,0:T(8,128)(2,1)S(1)} %collective-permute-done.12.refs_9_), channel_id=1, source_target_pairs={{0,4},{1,5},{2,6},{3,7},{4,0},{5,1},{6,2},{7,3},{8,12},{9,13},{10,... | collective-permute-start | bytes 491528 | tf_op jit(solution)/shard_map/ppermute | solution.py:37
  27.0 0.9 %copy-done = bf16[144,640]{1,0:T(8,128)(2,1)S(1)} copy-done((bf16[144,640]{1,0:T(8,128)(2,1)S(1)}, bf16[144,640]{1,0:T(8,128)(2,1)}, u32[]{:S(2)}) %copy-start) | copy-done | bytes 184344
  28.0 2.9 %attend.1 = (bf16[8,256,640]{2,1,0:T(8,128)(2,1)S(1)}, f32[128,640]{1,0:T(8,128)S(1)}, f32[8,640]{1,0:T(8,128)S(1)}, bf16[640,5120]{1,0:T(8,128)(2,1)S(1)}) custom-call(bf16[640,5120]{1,0:T(8,128)(2,1)} %w_ref.1, bf16[144,640]{1,0:T(8,128)(2,1)S(1)} %copy-done, bf16[256,256]{1,0:T(8,128)(2,1)S(1)} %constant_dynamic-update-slice_fusion.refs_0_.refs_7_, ...), custom_call_target="tpu_custom_call" | custom-call | flops 671088640 | bytes 2621440 | tf_op jit(solution)/shard_map/attend/pallas_call | solution.py:255
  30.8 1.2 %collective-permute-done.13.refs_10_ = bf16[128,640]{1,0:T(8,128)(2,1)S(1)} collective-permute-done((bf16[128,640]{1,0:T(8,128)(2,1)S(1)}, bf16[128,640]{1,0:T(8,128)(2,1)S(1)}, u32[]{:S(2)}, u32[]{:S(2)}) %collective-permute-start.13) | collective-permute-done | bytes 163872 | tf_op jit(solution)/shard_map/ppermute | solution.py:37
  32.0 2.1 %far_gradients.1 = (f32[2,2,128,256]{3,2,1,0:T(8,128)S(1)}, bf16[2,2,128,256]{3,2,1,0:T(8,128)(2,1)S(1)}, bf16[128,640]{1,0:T(8,128)(2,1)S(1)}, bf16[640,128]{1,...) custom-call(bf16[144,640]{1,0:T(8,128)(2,1)S(1)} %copy-done, ...), custom_call_target="tpu_custom_call" | custom-call | flops 1509949440 | bytes 6553600 | tf_op jit(solution)/shard_map/far_gradients/pallas_call | solution.py:289
  34.2 0.1 collective-permute-start.14
  34.3 0.2 near_gradients.2
  34.5 1.3 %collective-permute-done.14 = bf16[2,2,128,256]{3,2,1,0:T(8,128)(2,1)S(1)} collective-permute-done((bf16[2,2,128,256]{3,2,1,0:T(8,128)(2,1)S(1)}, bf16[2,2,128,256]{3,2,1,0:T(8,128)(2,1)S(1)}, u32[]{:S(2)}, u32[]{:S(2)}) %collective-permute-start.14) | collective-permute-done | bytes 262176 | tf_op jit(solution)/shard_map/ppermute | solution.py:27
  35.8 0.1 collective-permute-start.15
  36.0 0.3 collective-permute-start.17
  36.3 1.5 %near_gradients.3 = (f32[2,2,128,256]{3,2,1,0:T(8,128)S(1)}, bf16[128,640]{1,0:T(8,128)(2,1)}) custom-call(bf16[144,640]{1,0:T(8,128)(2,1)S(1)} %copy-done, bf16[8,256,640]{2,1,0:T(8,128)(2,1)S(1)} %get-tuple-element.41.refs_5_.refs_1_, bf16[128,640]{1,0:T(8,128)(2,1)S(1)} %get-tuple-element.47.refs_2_, bf16[640,128]{1,0:T(8,128)(2,1)S(1)} %get-tuple-element.48.refs_3_, ...), custom_call_target="tpu_custom_call" | custom-call | flops 335544320 | bytes 655360 | tf_op jit(solution)/shard_map/near_gradients/pallas_call | solution.py:325
  37.8 1.9 %collective-permute-start.16 = (bf16[2,128,256]{2,1,0:T(8,128)(2,1)S(1)}, bf16[2,128,256]{2,1,0:T(8,128)(2,1)S(1)}, u32[]{:S(2)}, u32[]{:S(2)}) collective-permute-start(bf16[2,128,256]{2,1,0:T(8,128)(2,1)S(1)} %fusion.4), channel_id=1, source_target_pairs={{0,16},{8,24},{16,0},{24,8},{32,48},{40,56},{48,32},{56,40},{64,80... | collective-permute-start | bytes 393224 | tf_op jit(solution)/shard_map/ppermute | solution.py:27
  39.8 2.7 %collective-permute-done.17 = bf16[2,128,256]{2,1,0:T(8,128)(2,1)S(1)} collective-permute-done((bf16[2,128,256]{2,1,0:T(8,128)(2,1)S(1)}, bf16[2,128,256]{2,1,0:T(8,128)(2,1)S(1)}, u32[]{:S(2)}, u32[]{:S(2)}) %collective-permute-start.17) | collective-permute-done | bytes 131104 | tf_op jit(solution)/shard_map/ppermute | solution.py:27
  42.5 1.3 %collective-permute-start.18 = (bf16[128,256]{1,0:T(8,128)(2,1)S(1)}, bf16[128,256]{1,0:T(8,128)(2,1)S(1)}, u32[]{:S(2)}, u32[]{:S(2)}) collective-permute-start(bf16[128,256]{1,0:T(8,128)(2,1)S(1)} %get-tuple-element.62), channel_id=1, source_target_pairs={{64,0},{72,8},{80,16},{88,24},{96,32},{104,40},{112,48},{120,56},{... | collective-permute-start | bytes 196616 | tf_op jit(solution)/shard_map/ppermute | solution.py:32
  43.8 1.3 %collective-permute-start.19 = (bf16[128,256]{1,0:T(8,128)(2,1)S(1)}, bf16[128,256]{1,0:T(8,128)(2,1)S(1)}, u32[]{:S(2)}, u32[]{:S(2)}) collective-permute-start(bf16[128,256]{1,0:T(8,128)(2,1)S(1)} %get-tuple-element.63), channel_id=1, source_target_pairs={{64,32},{72,40},{80,48},{88,56},{96,0},{104,8},{112,16},{120,24},{... | collective-permute-start | bytes 196616 | tf_op jit(solution)/shard_map/ppermute | solution.py:32
  45.2 1.0 %collective-permute-start.20 = (bf16[128,256]{1,0:T(8,128)(2,1)S(1)}, bf16[128,256]{1,0:T(8,128)(2,1)S(1)}, u32[]{:S(2)}, u32[]{:S(2)}) collective-permute-start(bf16[128,256]{1,0:T(8,128)(2,1)S(1)} %fusion.5), channel_id=1, source_target_pairs={{0,32},{8,40},{16,48},{24,56},{32,0},{40,8},{48,16},{56,24},{64,96... | collective-permute-start | bytes 196616 | tf_op jit(solution)/shard_map/ppermute | solution.py:27
  46.2 6.5 %collective-permute-done.18 = bf16[128,256]{1,0:T(8,128)(2,1)S(1)} collective-permute-done((bf16[128,256]{1,0:T(8,128)(2,1)S(1)}, bf16[128,256]{1,0:T(8,128)(2,1)S(1)}, u32[]{:S(2)}, u32[]{:S(2)}) %collective-permute-start.18) | collective-permute-done | bytes 65568 | tf_op jit(solution)/shard_map/ppermute | solution.py:32
  52.7 0.7 %add_convert_fusion = (bf16[128,128]{1,0:T(8,128)(2,1)}, bf16[128,128]{1,0:T(8,128)(2,1)}) fusion(f32[128,256]{1,0:T(8,128)S(1)} %slice_bitcast_fusion.2, bf16[128,256]{1,0:T(8,128)(2,1)S(1)} %collective-permute-done.20, bf16[128,256]{1,0:T(8,128)(2,1)S(1)} %collective-permute-done.19, bf16[128,256]{1,0:T(8,128)(2,1)S(1)} %collective-permute-done.18), kind=kLoop, calls=%fused_computation.17 | loop fusion | flops 229376 | bytes 393216 | tf_op jit(solution)/shard_map/convert_element_type | solution.py:375
  (34 shorter events, 0.5 us)
Async XLA Ops:
  2.4 29.6 %copy-start.1 = (bf16[640,128]{1,0:T(8,128)(2,1)S(1)}, bf16[640,128]{1,0:T(8,128)(2,1)}, u32[]{:S(2)}) copy-start(bf16[640,128]{1,0:T(8,128)(2,1)} %get-tuple-element.43.refs_2_.refs_4_) | copy-start | bytes 491524
  2.4 12.8 %collective-permute-start.3 = (bf16[128,256]{1,0:T(8,128)(2,1)}, bf16[128,256]{1,0:T(8,128)(2,1)S(1)}, u32[]{:S(2)}, u32[]{:S(2)}) collective-permute-start(bf16[128,256]{1,0:T(8,128)(2,1)} %get-tuple-element.36), channel_id=1, source_target_pairs={{0,96},{8,104},{16,112},{24,120},{32,64},{40,72},{48,80},{56,88},{... | collective-permute-start | bytes 196616 | tf_op jit(solution)/shard_map/ppermute | solution.py:27
  7.1 8.2 %collective-permute-start.2 = (bf16[128,256]{1,0:T(8,128)(2,1)}, bf16[128,256]{1,0:T(8,128)(2,1)S(1)}, u32[]{:S(2)}, u32[]{:S(2)}) collective-permute-start(bf16[128,256]{1,0:T(8,128)(2,1)} %get-tuple-element.36), channel_id=1, source_target_pairs={{0,64},{8,72},{16,80},{24,88},{32,96},{40,104},{48,112},{56,120},{... | collective-permute-start | bytes 196616 | tf_op jit(solution)/shard_map/ppermute | solution.py:27
  7.1 7.5 %collective-permute-start = (bf16[128,256]{1,0:T(8,128)(2,1)}, bf16[128,256]{1,0:T(8,128)(2,1)S(1)}, u32[]{:S(2)}, u32[]{:S(2)}) collective-permute-start(bf16[128,256]{1,0:T(8,128)(2,1)} %get-tuple-element.36), channel_id=1, source_target_pairs={{0,16},{8,24},{16,0},{24,8},{32,48},{40,56},{48,32},{56,40},{64,80... | collective-permute-start | bytes 196616 | tf_op jit(solution)/shard_map/ppermute | solution.py:27
  8.6 14.4 %collective-permute-start.12 = (bf16[128,640]{1,0:T(8,128)(2,1)}, bf16[128,640]{1,0:T(8,128)(2,1)S(1)}, u32[]{:S(2)}, u32[]{:S(2)}) collective-permute-start(bf16[128,640]{1,0:T(8,128)(2,1)} %param.10), channel_id=1, source_target_pairs={{0,2},{1,3},{2,0},{3,1},{4,6},{5,7},{6,4},{7,5},{8,10},{9,11},{10,... | collective-permute-start | bytes 491528 | tf_op jit(solution)/shard_map/ppermute | solution.py:37
  10.8 8.1 %collective-permute-start.9 = (bf16[128,640]{1,0:T(8,128)(2,1)}, bf16[128,640]{1,0:T(8,128)(2,1)S(1)}, u32[]{:S(2)}, u32[]{:S(2)}) collective-permute-start(bf16[128,640]{1,0:T(8,128)(2,1)} %param.10), channel_id=1, source_target_pairs={{0,4},{1,5},{2,6},{3,7},{4,0},{5,1},{6,2},{7,3},{8,12},{9,13},{10,... | collective-permute-start | bytes 491528 | tf_op jit(solution)/shard_map/ppermute | solution.py:37
  14.5 8.0 %collective-permute-start.1 = (bf16[256,256]{1,0:T(8,128)(2,1)S(1)}, bf16[256,256]{1,0:T(8,128)(2,1)S(1)}, u32[]{:S(2)}, u32[]{:S(2)}) collective-permute-start(bf16[256,256]{1,0:T(8,128)(2,1)S(1)} %constant_dynamic-update-slice_fusion.refs_0_.refs_7_), channel_id=1, source_target_pairs={{0,32},{8,40},{16,48},{24,56},{32,0},{40,8},{48,16},{56,24},{64,96... | collective-permute-start | bytes 393224 | tf_op jit(solution)/shard_map/ppermute | solution.py:27
  15.3 7.2 %collective-permute-start.4 = (bf16[256,256]{1,0:T(8,128)(2,1)S(1)}, bf16[256,256]{1,0:T(8,128)(2,1)S(1)}, u32[]{:S(2)}, u32[]{:S(2)}) collective-permute-start(bf16[256,256]{1,0:T(8,128)(2,1)S(1)} %constant_dynamic-update-slice_fusion.2.refs_2_.refs_13_), channel_id=1, source_target_pairs={{0,16},{8,24},{16,0},{24,8},{32,48},{40,56},{48,32},{56,40},{64,80... | collective-permute-start | bytes 393224 | tf_op jit(solution)/shard_map/ppermute | solution.py:27
  19.8 12.2 %collective-permute-start.11 = (bf16[2,128,640]{2,1,0:T(8,128)(2,1)S(1)}, bf16[2,128,640]{2,1,0:T(8,128)(2,1)S(1)}, u32[]{:S(2)}, u32[]{:S(2)}) collective-permute-start(bf16[2,128,640]{2,1,0:T(8,128)(2,1)S(1)} %pad_maximum_fusion.refs_6_), channel_id=1, source_target_pairs={{0,3},{1,2},{2,1},{3,0},{4,7},{5,6},{6,5},{7,4},{8,11},{9,10},{10,... | collective-permute-start | bytes 983048 | tf_op jit(solution)/shard_map/ppermute | solution.py:37
  19.9 12.1 %collective-permute-start.10 = (bf16[2,128,640]{2,1,0:T(8,128)(2,1)S(1)}, bf16[2,128,640]{2,1,0:T(8,128)(2,1)S(1)}, u32[]{:S(2)}, u32[]{:S(2)}) collective-permute-start(bf16[2,128,640]{2,1,0:T(8,128)(2,1)S(1)} %pad_maximum_fusion.refs_6_), channel_id=1, source_target_pairs={{0,1},{1,0},{2,3},{3,2},{4,5},{5,4},{6,7},{7,6},{8,9},{9,8},{10,11... | collective-permute-start | bytes 983048 | tf_op jit(solution)/shard_map/ppermute | solution.py:37
  22.5 1.3 %collective-permute-start.5 = (bf16[256,256]{1,0:T(8,128)(2,1)S(1)}, bf16[256,256]{1,0:T(8,128)(2,1)S(1)}, u32[]{:S(2)}, u32[]{:S(2)}) collective-permute-start(bf16[256,256]{1,0:T(8,128)(2,1)S(1)} %constant_dynamic-update-slice_fusion.refs_0_.refs_7_), channel_id=1, source_target_pairs={{0,8},{8,0},{16,24},{24,16},{32,40},{40,32},{48,56},{56,48},{64,72... | collective-permute-start | bytes 393224 | tf_op jit(solution)/shard_map/ppermute | solution.py:27
  22.5 1.5 %collective-permute-start.6 = (bf16[256,256]{1,0:T(8,128)(2,1)S(1)}, bf16[256,256]{1,0:T(8,128)(2,1)S(1)}, u32[]{:S(2)}, u32[]{:S(2)}) collective-permute-start(bf16[256,256]{1,0:T(8,128)(2,1)S(1)} %collective-permute-done.1.refs_1_.refs_8_), channel_id=1, source_target_pairs={{0,8},{8,0},{16,24},{24,16},{32,40},{40,32},{48,56},{56,48},{64,72... | collective-permute-start | bytes 393224 | tf_op jit(solution)/shard_map/ppermute | solution.py:27
  23.0 4.0 %collective-permute-start.7 = (bf16[256,256]{1,0:T(8,128)(2,1)S(1)}, bf16[256,256]{1,0:T(8,128)(2,1)S(1)}, u32[]{:S(2)}, u32[]{:S(2)}) collective-permute-start(bf16[256,256]{1,0:T(8,128)(2,1)S(1)} %constant_dynamic-update-slice_fusion.2.refs_2_.refs_13_), channel_id=1, source_target_pairs={{0,8},{8,0},{16,24},{24,16},{32,40},{40,32},{48,56},{56,48},{64,72... | collective-permute-start | bytes 393224 | tf_op jit(solution)/shard_map/ppermute | solution.py:27
  23.9 3.2 %collective-permute-start.8 = (bf16[256,256]{1,0:T(8,128)(2,1)S(1)}, bf16[256,256]{1,0:T(8,128)(2,1)S(1)}, u32[]{:S(2)}, u32[]{:S(2)}) collective-permute-start(bf16[256,256]{1,0:T(8,128)(2,1)S(1)} %collective-permute-done.4.refs_3_.refs_14_), channel_id=1, source_target_pairs={{0,8},{8,0},{16,24},{24,16},{32,40},{40,32},{48,56},{56,48},{64,72... | collective-permute-start | bytes 393224 | tf_op jit(solution)/shard_map/ppermute | solution.py:27
  24.1 7.9 %collective-permute-start.13 = (bf16[128,640]{1,0:T(8,128)(2,1)S(1)}, bf16[128,640]{1,0:T(8,128)(2,1)S(1)}, u32[]{:S(2)}, u32[]{:S(2)}) collective-permute-start(bf16[128,640]{1,0:T(8,128)(2,1)S(1)} %collective-permute-done.12.refs_9_), channel_id=1, source_target_pairs={{0,4},{1,5},{2,6},{3,7},{4,0},{5,1},{6,2},{7,3},{8,12},{9,13},{10,... | collective-permute-start | bytes 491528 | tf_op jit(solution)/shard_map/ppermute | solution.py:37
  27.0 0.9 %copy-start = (bf16[144,640]{1,0:T(8,128)(2,1)S(1)}, bf16[144,640]{1,0:T(8,128)(2,1)}, u32[]{:S(2)}) copy-start(bf16[144,640]{1,0:T(8,128)(2,1)} %get-tuple-element.34.qt_ref.refs_0_) | copy-start | bytes 552964
  34.2 1.6 %collective-permute-start.14 = (bf16[2,2,128,256]{3,2,1,0:T(8,128)(2,1)S(1)}, bf16[2,2,128,256]{3,2,1,0:T(8,128)(2,1)S(1)}, u32[]{:S(2)}, u32[]{:S(2)}) collective-permute-start(bf16[2,2,128,256]{3,2,1,0:T(8,128)(2,1)S(1)} %get-tuple-element.53), channel_id=1, source_target_pairs={{0,8},{8,0},{16,24},{24,16},{32,40},{40,32},{48,56},{56,48},{64,72... | collective-permute-start | bytes 786440 | tf_op jit(solution)/shard_map/ppermute | solution.py:27
  35.8 2.0 %collective-permute-start.15 = (bf16[2,2,128,256]{3,2,1,0:T(8,128)(2,1)S(1)}, bf16[2,2,128,256]{3,2,1,0:T(8,128)(2,1)S(1)}, u32[]{:S(2)}, u32[]{:S(2)}) collective-permute-start(bf16[2,2,128,256]{3,2,1,0:T(8,128)(2,1)S(1)} %get-tuple-element.59), channel_id=1, source_target_pairs={{0,8},{8,0},{16,24},{24,16},{32,40},{40,32},{48,56},{56,48},{64,72... | collective-permute-start | bytes 786440 | tf_op jit(solution)/shard_map/ppermute | solution.py:27
  36.0 6.4 %collective-permute-start.17 = (bf16[2,128,256]{2,1,0:T(8,128)(2,1)S(1)}, bf16[2,128,256]{2,1,0:T(8,128)(2,1)S(1)}, u32[]{:S(2)}, u32[]{:S(2)}) collective-permute-start(bf16[2,128,256]{2,1,0:T(8,128)(2,1)S(1)} %fusion.3), channel_id=1, source_target_pairs={{0,16},{8,24},{16,0},{24,8},{32,48},{40,56},{48,32},{56,40},{64,80... | collective-permute-start | bytes 393224 | tf_op jit(solution)/shard_map/ppermute | solution.py:27
  37.8 7.2 %collective-permute-start.16 = (bf16[2,128,256]{2,1,0:T(8,128)(2,1)S(1)}, bf16[2,128,256]{2,1,0:T(8,128)(2,1)S(1)}, u32[]{:S(2)}, u32[]{:S(2)}) collective-permute-start(bf16[2,128,256]{2,1,0:T(8,128)(2,1)S(1)} %fusion.4), channel_id=1, source_target_pairs={{0,16},{8,24},{16,0},{24,8},{32,48},{40,56},{48,32},{56,40},{64,80... | collective-permute-start | bytes 393224 | tf_op jit(solution)/shard_map/ppermute | solution.py:27
  42.5 10.2 %collective-permute-start.18 = (bf16[128,256]{1,0:T(8,128)(2,1)S(1)}, bf16[128,256]{1,0:T(8,128)(2,1)S(1)}, u32[]{:S(2)}, u32[]{:S(2)}) collective-permute-start(bf16[128,256]{1,0:T(8,128)(2,1)S(1)} %get-tuple-element.62), channel_id=1, source_target_pairs={{64,0},{72,8},{80,16},{88,24},{96,32},{104,40},{112,48},{120,56},{... | collective-permute-start | bytes 196616 | tf_op jit(solution)/shard_map/ppermute | solution.py:32
  43.8 8.9 %collective-permute-start.19 = (bf16[128,256]{1,0:T(8,128)(2,1)S(1)}, bf16[128,256]{1,0:T(8,128)(2,1)S(1)}, u32[]{:S(2)}, u32[]{:S(2)}) collective-permute-start(bf16[128,256]{1,0:T(8,128)(2,1)S(1)} %get-tuple-element.63), channel_id=1, source_target_pairs={{64,32},{72,40},{80,48},{88,56},{96,0},{104,8},{112,16},{120,24},{... | collective-permute-start | bytes 196616 | tf_op jit(solution)/shard_map/ppermute | solution.py:32
  45.2 7.5 %collective-permute-start.20 = (bf16[128,256]{1,0:T(8,128)(2,1)S(1)}, bf16[128,256]{1,0:T(8,128)(2,1)S(1)}, u32[]{:S(2)}, u32[]{:S(2)}) collective-permute-start(bf16[128,256]{1,0:T(8,128)(2,1)S(1)} %fusion.5), channel_id=1, source_target_pairs={{0,32},{8,40},{16,48},{24,56},{32,0},{40,8},{48,16},{56,24},{64,96... | collective-permute-start | bytes 196616 | tf_op jit(solution)/shard_map/ppermute | solution.py:27

commit v4 on v3

--- a/solution.py
+++ b/solution.py
@@ -186,20 +186,27 @@
                     out[y, z % 2] = jnp.zeros(out.shape[2:], out.dtype)
 
 
-def far_kernel(group, qt_ref, w_ref, qs_ref, o_ref, inv_ref, p_ref, *refs):
-    og_refs, kv_refs = refs[:5], refs[5 : 5 + 2 * len(group)]
-    keep_ref, send_ref, gt_ref, g_ref, delta_ref, dqt_ref, ds_ref, acc_ref = refs[5 + 2 * len(group) :]
-    _, count, width = og_refs[0].shape
+def add_parts(acc_ref, total, w_ref, parts):
     mine = lax.axis_index("head")
-    parts = [(0, og_refs[0][0]), (4, og_refs[0][1]), (2, og_refs[3][...]), (6, og_refs[4][...])]
-    parts += [(1, og_refs[1][0]), (5, og_refs[1][1]), (3, og_refs[2][0]), (7, og_refs[2][1])]
-    for n, (slot, block) in enumerate(parts):
+    for slot, block in parts:
+        width = block.shape[1]
         columns = pl.ds(pl.multiple_of((mine ^ slot) * width, HEAD_DIM), width)
         part = dot_nt(w_ref[:, columns], block)
-        if n == 0:
-            acc_ref[...] = part
-        else:
-            acc_ref[...] += part
+        acc_ref[...] = part if total is None else total + part
+        total = acc_ref[...]
+
+
+def project_kernel(w_ref, pair_ref, one_ref, three_ref, across_ref, acc_ref):
+    parts = [(0, pair_ref[0]), (4, pair_ref[1]), (2, across_ref[...]), (1, one_ref[0])]
+    parts += [(5, one_ref[1]), (3, three_ref[0]), (7, three_ref[1])]
+    add_parts(acc_ref, None, w_ref, parts)
+
+
+def far_kernel(group, qt_ref, w_ref, acc_in, og_ref, qs_ref, o_ref, inv_ref, p_ref, *refs):
+    kv_refs = refs[: 2 * len(group)]
+    keep_ref, send_ref, gt_ref, g_ref, delta_ref, dqt_ref, ds_ref, acc_ref = refs[2 * len(group) :]
+    count = og_ref.shape[0]
+    add_parts(acc_ref, acc_in[...], w_ref, [(6, og_ref[...])])
     answer = qt_ref[HEAD_DIM:, :count].astype(F32)[2:3]
     for h in range(GROUP):
         inverse = inv_ref[0:1, heads(h)]
@@ -276,8 +283,22 @@
     )(weight, query_t, *kv_tiles)
 
 
-def far_gradients(group, query_t, weight, query_s, attended, probs, blocks, kv_tiles):
-    _, count, width = blocks[0].shape
+def project(weight, pair, one, three, across):
+    count, _ = across.shape
+    features = weight.shape[0]
+    return pl.pallas_call(
+        project_kernel,
+        out_shape=jax.ShapeDtypeStruct((features, count), F32),
+        in_specs=[VMEM_SPEC] * 5,
+        out_specs=VMEM_SPEC,
+        compiler_params=PARAMS,
+        cost_estimate=pl.CostEstimate(flops=2 * weight.size * count, bytes_accessed=2 * weight.size, transcendentals=0),
+        name="project",
+    )(weight, pair, one, three, across)
+
+
+def far_gradients(group, query_t, weight, acc, last, query_s, attended, probs, kv_tiles):
+    count, _ = last.shape
     features = query_s.shape[0]
     keys = kv_tiles[0].shape[0]
     flops = 2 * len(kv_tiles) * keys * features * HEAD_DIM
@@ -296,7 +317,7 @@
             jax.ShapeDtypeStruct((8, features), F32),
             jax.ShapeDtypeStruct((HEAD_DIM, features), F32),
         ),
-        in_specs=[VMEM_SPEC] * (6 + len(blocks) + len(kv_tiles)),
+        in_specs=[VMEM_SPEC] * (8 + len(kv_tiles)),
         out_specs=(VMEM_SPEC,) * 6,
         scratch_shapes=[
             pltpu.VMEM((keys, features), BF16),
@@ -307,7 +328,7 @@
             flops=4 * flops + 2 * weight.size * count, bytes_accessed=2 * weight.size, transcendentals=0
         ),
         name="far_gradients",
-    )(query_t, weight, query_s, *attended, probs, *blocks, *kv_tiles)
+    )(query_t, weight, acc, last, query_s, *attended, probs, *kv_tiles)
 
 
 def near_gradients(core, group, query_t, probs, shared, kv_tiles):
@@ -347,13 +368,14 @@
     pair = jnp.concatenate([own, ctx_swap(own, 2)], axis=0)
     across = head_swap(out_grad, 2)
     both = head_swap(across, 4)
-    blocks = [og_pair, head_swap(og_pair, 1), head_swap(og_pair, 3), across, both]
+    one, three = head_swap(og_pair, 1), head_swap(og_pair, 3)
     tiles = [*lax.optimization_barrier((pair, ctx_swap(pair, 4))), *lax.optimization_barrier((reach, ctx_swap(reach, 2)))]
     tiles += [ctx_swap(tile, 1) for tile in tiles]
     far, near = (2, 3), (0, 1)
     probs, *attended, weight = attend(out_weight, query_t, tiles)
+    acc = project(weight, og_pair, one, three, across)
     far_keep, far_send, grads_t, grads, delta, dquery_t = far_gradients(
-        far, query_t, weight, query_s, attended, probs, blocks, [tiles[4 * core + n] for core in (1, 0) for n in far]
+        far, query_t, weight, acc, both, query_s, attended, probs, [tiles[4 * core + n] for core in (1, 0) for n in far]
     )
     shared = (grads_t, grads, query_s, delta)
     near_send, dquery_t = near_gradients(1, near, query_t, probs, (*shared, dquery_t), [tiles[4 + n] for n in near])

time: 53.6 us -> 52.5 us (0.979)
  waiting for transfers between devices: 15.8 us -> 14.7 us
    pallas_call x0 -> x1, Pallas kernels: none -> 1.71 us  [project(): pl.pallas_call(project_kernel, out_shape=jax.ShapeDtypeStruct((features,...]
    pallas_call x1, Pallas kernels: 2.14 us -> 0.57 us  [far_gradients(): pl.pallas_call(kernel, out_shape=(jax.ShapeDtypeStruct(partial, F32), jax...]
    ppermute x5, waiting for transfers between devices: 4.53 us -> 3.46 us  [head_swap(): return lax.ppermute(value, 'head', [(i, i ^ bits) for i in range(count)])]
  transfers between devices with their start and end apart: 21 -> 21, of which waited for: 6 -> 5; matrix products, arithmetic and copies ran while one was open for 4% -> 4% of each run, Pallas kernels for 8% -> 12%
where the time goes in v4:
time: 52.5 us; the launch traced here: 52.3 us
  starting transfers between devices  24.5 us (47%)
  waiting for transfers between devices  14.7 us (28%)
  Pallas kernels  8.65 us (16%)
  local copies, waits for them, and re-layouts  1.85 us (4%)
  other arithmetic  1.79 us (3%)
  between operations  0.84 us (2%)
    ppermute x14, starting transfers between devices, ctx_swap(): return lax.ppermute(value, 'ctx', [(i, i ^ bits) for i in range(count)])  11.2 us
    ppermute x5, starting transfers between devices, head_swap(): return lax.ppermute(value, 'head', [(i, i ^ bits) for i in range(count)])  10.7 us
    ppermute x2, waiting for transfers between devices, send_back(): lax.ppermute(value, 'ctx', [(i, i ^ bits) for i in range(count) if i ^ bi...  6.49 us
    ppermute x14, waiting for transfers between devices, ctx_swap(): return lax.ppermute(value, 'ctx', [(i, i ^ bits) for i in range(count)])  4.74 us
    ppermute x5, waiting for transfers between devices, head_swap(): return lax.ppermute(value, 'head', [(i, i ^ bits) for i in range(count)])  3.46 us
    pallas_call x1, Pallas kernels, attend(): pl.pallas_call(attend_kernel, out_shape=(jax.ShapeDtypeStruct((TILES, key...  2.91 us
    ppermute x2, starting transfers between devices, send_back(): lax.ppermute(value, 'ctx', [(i, i ^ bits) for i in range(count) if i ^ bi...  2.58 us
    pallas_call x1, Pallas kernels, prepare(): pl.pallas_call(prepare_kernel, out_shape=(jax.ShapeDtypeStruct((count, 2...  1.8 us
  transfers between devices with their start and end apart: 21, of which 5 were waited for; matrix products, arithmetic and copies ran while one was open for 4% of the time, Pallas kernels for 12%

profile of v4, /device:TPU:2, one launch (start us, length us, event | category | flops | bytes accessed | tf_op | source)
XLA Modules:
  0.0 52.3 jit_solution(2758746230433015265)
XLA Ops:
  0.6 1.8 %prepare.1 = (bf16[128,256]{1,0:T(8,128)(2,1)}, bf16[144,640]{1,0:T(8,128)(2,1)}, bf16[640,128]{1,0:T(8,128)(2,1)}) custom-call(s32[4]{0:T(128)} %lens_ref.1, s32[4]{0:T(128)} %prompts_ref.1, bf16[128,128]{1,0:T(8,128)(2,1)} %k_ref.1, bf16[128,128]{1,0:T(8,128)(2,1)} %v_ref.1, bf16[128,640]{1,0:T(8,128)(2,1)} %q_ref.1), custom_call_target="tpu_custom_call" | custom-call | tf_op jit(solution)/shard_map/prepare/pallas_call | solution.py:245
  2.4 4.6 %collective-permute-start.3 = (bf16[128,256]{1,0:T(8,128)(2,1)}, bf16[128,256]{1,0:T(8,128)(2,1)S(1)}, u32[]{:S(2)}, u32[]{:S(2)}) collective-permute-start(bf16[128,256]{1,0:T(8,128)(2,1)} %get-tuple-element.36), channel_id=1, source_target_pairs={{0,96},{8,104},{16,112},{24,120},{32,64},{40,72},{48,80},{56,88},{... | collective-permute-start | bytes 196616 | tf_op jit(solution)/shard_map/ppermute | solution.py:27
  7.1 1.6 %collective-permute-start = (bf16[128,256]{1,0:T(8,128)(2,1)}, bf16[128,256]{1,0:T(8,128)(2,1)S(1)}, u32[]{:S(2)}, u32[]{:S(2)}) collective-permute-start(bf16[128,256]{1,0:T(8,128)(2,1)} %get-tuple-element.36), channel_id=1, source_target_pairs={{0,16},{8,24},{16,0},{24,8},{32,48},{40,56},{48,32},{56,40},{64,80... | collective-permute-start | bytes 196616 | tf_op jit(solution)/shard_map/ppermute | solution.py:27
  8.6 2.1 %collective-permute-start.12 = (bf16[128,640]{1,0:T(8,128)(2,1)}, bf16[128,640]{1,0:T(8,128)(2,1)S(1)}, u32[]{:S(2)}, u32[]{:S(2)}) collective-permute-start(bf16[128,640]{1,0:T(8,128)(2,1)} %param.10), channel_id=1, source_target_pairs={{0,2},{1,3},{2,0},{3,1},{4,6},{5,7},{6,4},{7,5},{8,10},{9,11},{10,... | collective-permute-start | bytes 491528 | tf_op jit(solution)/shard_map/ppermute | solution.py:37
  10.8 2.9 %collective-permute-start.9 = (bf16[128,640]{1,0:T(8,128)(2,1)}, bf16[128,640]{1,0:T(8,128)(2,1)S(1)}, u32[]{:S(2)}, u32[]{:S(2)}) collective-permute-start(bf16[128,640]{1,0:T(8,128)(2,1)} %param.10), channel_id=1, source_target_pairs={{0,4},{1,5},{2,6},{3,7},{4,0},{5,1},{6,2},{7,3},{8,12},{9,13},{10,... | collective-permute-start | bytes 491528 | tf_op jit(solution)/shard_map/ppermute | solution.py:37
  13.7 0.8 %constant_dynamic-update-slice_fusion.1 = bf16[256,256]{1,0:T(8,128)(2,1)S(1)} fusion(bf16[128,256]{1,0:T(8,128)(2,1)} %get-tuple-element.36), kind=kLoop, calls=%fused_computation.20 | loop fusion | bytes 131072
  14.5 0.7 %collective-permute-start.1 = (bf16[256,256]{1,0:T(8,128)(2,1)S(1)}, bf16[256,256]{1,0:T(8,128)(2,1)S(1)}, u32[]{:S(2)}, u32[]{:S(2)}) collective-permute-start(bf16[256,256]{1,0:T(8,128)(2,1)S(1)} %constant_dynamic-update-slice_fusion.refs_0_.refs_7_), channel_id=1, source_target_pairs={{0,32},{8,40},{16,48},{24,56},{32,0},{40,8},{48,16},{56,24},{64,96... | collective-permute-start | bytes 393224 | tf_op jit(solution)/shard_map/ppermute | solution.py:27
  15.2 0.2 collective-permute-start.4
  15.4 3.5 %collective-permute-done.9 = bf16[128,640]{1,0:T(8,128)(2,1)S(1)} collective-permute-done((bf16[128,640]{1,0:T(8,128)(2,1)}, bf16[128,640]{1,0:T(8,128)(2,1)S(1)}, u32[]{:S(2)}, u32[]{:S(2)}) %collective-permute-start.9) | collective-permute-done | bytes 163872 | tf_op jit(solution)/shard_map/ppermute | solution.py:37
  18.9 1.0 %pad_maximum_fusion.pair_ref = bf16[2,128,640]{2,1,0:T(8,128)(2,1)S(1)} fusion(bf16[1,128,640]{2,1,0:T(8,128)(2,1)S(1)} %bitcast.25, bf16[1,128,640]{2,1,0:T(8,128)(2,1)} %bitcast.24), kind=kLoop, calls=%fused_computation.2 | loop fusion | flops 163840 | bytes 655360 | tf_op jit(solution)/shard_map/stack | solution.py:366
  19.8 0.1 collective-permute-start.11
  19.9 2.6 %collective-permute-start.10 = (bf16[2,128,640]{2,1,0:T(8,128)(2,1)S(1)}, bf16[2,128,640]{2,1,0:T(8,128)(2,1)S(1)}, u32[]{:S(2)}, u32[]{:S(2)}) collective-permute-start(bf16[2,128,640]{2,1,0:T(8,128)(2,1)S(1)} %pad_maximum_fusion.pair_ref), channel_id=1, source_target_pairs={{0,1},{1,0},{2,3},{3,2},{4,5},{5,4},{6,7},{7,6},{8,9},{9,8},{10,11... | collective-permute-start | bytes 983048 | tf_op jit(solution)/shard_map/ppermute | solution.py:37
  22.5 0.5 collective-permute-start.6
  23.1 0.7 %collective-permute-done.5.refs_4_.refs_7_ = bf16[256,256]{1,0:T(8,128)(2,1)S(1)} collective-permute-done((bf16[256,256]{1,0:T(8,128)(2,1)S(1)}, bf16[256,256]{1,0:T(8,128)(2,1)S(1)}, u32[]{:S(2)}, u32[]{:S(2)}) %collective-permute-start.5) | collective-permute-done | bytes 131104 | tf_op jit(solution)/shard_map/ppermute | solution.py:27
  23.9 0.1 collective-permute-start.8
  24.1 3.0 %collective-permute-start.13 = (bf16[128,640]{1,0:T(8,128)(2,1)S(1)}, bf16[128,640]{1,0:T(8,128)(2,1)S(1)}, u32[]{:S(2)}, u32[]{:S(2)}) collective-permute-start(bf16[128,640]{1,0:T(8,128)(2,1)S(1)} %collective-permute-done.12.across_ref), channel_id=1, source_target_pairs={{0,4},{1,5},{2,6},{3,7},{4,0},{5,1},{6,2},{7,3},{8,12},{9,13},{10,... | collective-permute-start | bytes 491528 | tf_op jit(solution)/shard_map/ppermute | solution.py:37
  27.0 0.9 %copy-done = bf16[144,640]{1,0:T(8,128)(2,1)S(1)} copy-done((bf16[144,640]{1,0:T(8,128)(2,1)S(1)}, bf16[144,640]{1,0:T(8,128)(2,1)}, u32[]{:S(2)}) %copy-start) | copy-done | bytes 184344
  28.0 2.9 %attend.1 = (bf16[8,256,640]{2,1,0:T(8,128)(2,1)S(1)}, f32[128,640]{1,0:T(8,128)S(1)}, f32[8,640]{1,0:T(8,128)S(1)}, bf16[640,5120]{1,0:T(8,128)(2,1)S(1)}) custom-call(bf16[640,5120]{1,0:T(8,128)(2,1)} %w_ref.1, bf16[144,640]{1,0:T(8,128)(2,1)S(1)} %copy-done, bf16[256,256]{1,0:T(8,128)(2,1)S(1)} %constant_dynamic-update-slice_fusion.refs_0_.refs_7_, ...), custom_call_target="tpu_custom_call" | custom-call | flops 671088640 | bytes 2621440 | tf_op jit(solution)/shard_map/attend/pallas_call | solution.py:262
  30.9 1.7 %project.1.refs_2_ = f32[640,128]{1,0:T(8,128)S(1)} custom-call(bf16[640,5120]{1,0:T(8,128)(2,1)S(1)} %get-tuple-element.42.w_ref.refs_1_, bf16[2,128,640]{2,1,0:T(8,128)(2,1)S(1)} %pad_maximum_fusion.pair_ref, bf16[2,128,640]{2,1,0:T(8,128)(2,1)S(1)} %collective-permute-done.10.one_ref, bf16[2,128,640]{2,1,0:T(8,128)(2,1)S(1)} %collective-permute-done.11.three_ref, ...), custom_call_target="tpu_custom_call" | custom-call | flops 838860800 | bytes 6553600 | tf_op jit(solution)/shard_map/project/pallas_call | solution.py:289
  32.6 0.6 %far_gradients.1 = (f32[2,2,128,256]{3,2,1,0:T(8,128)S(1)}, bf16[2,2,128,256]{3,2,1,0:T(8,128)(2,1)S(1)}, bf16[128,640]{1,0:T(8,128)(2,1)S(1)}, bf16[640,128]{1,...) custom-call(bf16[144,640]{1,0:T(8,128)(2,1)S(1)} %copy-done, ...), custom_call_target="tpu_custom_call" | custom-call | flops 1509949440 | bytes 6553600 | tf_op jit(solution)/shard_map/far_gradients/pallas_call | solution.py:310
  33.2 0.1 collective-permute-start.14
  33.4 0.2 near_gradients.2
  33.6 1.3 %collective-permute-done.14 = bf16[2,2,128,256]{3,2,1,0:T(8,128)(2,1)S(1)} collective-permute-done((bf16[2,2,128,256]{3,2,1,0:T(8,128)(2,1)S(1)}, bf16[2,2,128,256]{3,2,1,0:T(8,128)(2,1)S(1)}, u32[]{:S(2)}, u32[]{:S(2)}) %collective-permute-start.14) | collective-permute-done | bytes 262176 | tf_op jit(solution)/shard_map/ppermute | solution.py:27
  34.9 0.1 collective-permute-start.15
  35.2 1.5 %near_gradients.3 = (f32[2,2,128,256]{3,2,1,0:T(8,128)S(1)}, bf16[128,640]{1,0:T(8,128)(2,1)}) custom-call(bf16[144,640]{1,0:T(8,128)(2,1)S(1)} %copy-done, bf16[8,256,640]{2,1,0:T(8,128)(2,1)S(1)} %get-tuple-element.41.refs_7_.refs_1_, bf16[128,640]{1,0:T(8,128)(2,1)S(1)} %get-tuple-element.47.refs_2_, bf16[640,128]{1,0:T(8,128)(2,1)S(1)} %get-tuple-element.48.refs_3_, ...), custom_call_target="tpu_custom_call" | custom-call | flops 335544320 | bytes 655360 | tf_op jit(solution)/shard_map/near_gradients/pallas_call | solution.py:346
  36.7 2.1 %collective-permute-start.16 = (bf16[2,128,256]{2,1,0:T(8,128)(2,1)S(1)}, bf16[2,128,256]{2,1,0:T(8,128)(2,1)S(1)}, u32[]{:S(2)}, u32[]{:S(2)}) collective-permute-start(bf16[2,128,256]{2,1,0:T(8,128)(2,1)S(1)} %fusion.4), channel_id=1, source_target_pairs={{0,16},{8,24},{16,0},{24,8},{32,48},{40,56},{48,32},{56,40},{64,80... | collective-permute-start | bytes 393224 | tf_op jit(solution)/shard_map/ppermute | solution.py:27
  38.8 2.7 %collective-permute-done.17 = bf16[2,128,256]{2,1,0:T(8,128)(2,1)S(1)} collective-permute-done((bf16[2,128,256]{2,1,0:T(8,128)(2,1)S(1)}, bf16[2,128,256]{2,1,0:T(8,128)(2,1)S(1)}, u32[]{:S(2)}, u32[]{:S(2)}) %collective-permute-start.17) | collective-permute-done | bytes 131104 | tf_op jit(solution)/shard_map/ppermute | solution.py:27
  41.5 1.3 %collective-permute-start.18 = (bf16[128,256]{1,0:T(8,128)(2,1)S(1)}, bf16[128,256]{1,0:T(8,128)(2,1)S(1)}, u32[]{:S(2)}, u32[]{:S(2)}) collective-permute-start(bf16[128,256]{1,0:T(8,128)(2,1)S(1)} %get-tuple-element.62), channel_id=1, source_target_pairs={{64,0},{72,8},{80,16},{88,24},{96,32},{104,40},{112,48},{120,56},{... | collective-permute-start | bytes 196616 | tf_op jit(solution)/shard_map/ppermute | solution.py:32
  42.8 1.3 %collective-permute-start.19 = (bf16[128,256]{1,0:T(8,128)(2,1)S(1)}, bf16[128,256]{1,0:T(8,128)(2,1)S(1)}, u32[]{:S(2)}, u32[]{:S(2)}) collective-permute-start(bf16[128,256]{1,0:T(8,128)(2,1)S(1)} %get-tuple-element.63), channel_id=1, source_target_pairs={{64,32},{72,40},{80,48},{88,56},{96,0},{104,8},{112,16},{120,24},{... | collective-permute-start | bytes 196616 | tf_op jit(solution)/shard_map/ppermute | solution.py:32
  44.2 0.9 %collective-permute-start.20 = (bf16[128,256]{1,0:T(8,128)(2,1)S(1)}, bf16[128,256]{1,0:T(8,128)(2,1)S(1)}, u32[]{:S(2)}, u32[]{:S(2)}) collective-permute-start(bf16[128,256]{1,0:T(8,128)(2,1)S(1)} %fusion.5), channel_id=1, source_target_pairs={{0,32},{8,40},{16,48},{24,56},{32,0},{40,8},{48,16},{56,24},{64,96... | collective-permute-start | bytes 196616 | tf_op jit(solution)/shard_map/ppermute | solution.py:27
  45.2 6.5 %collective-permute-done.18 = bf16[128,256]{1,0:T(8,128)(2,1)S(1)} collective-permute-done((bf16[128,256]{1,0:T(8,128)(2,1)S(1)}, bf16[128,256]{1,0:T(8,128)(2,1)S(1)}, u32[]{:S(2)}, u32[]{:S(2)}) %collective-permute-start.18) | collective-permute-done | bytes 65568 | tf_op jit(solution)/shard_map/ppermute | solution.py:32
  51.6 0.7 %add_convert_fusion = (bf16[128,128]{1,0:T(8,128)(2,1)}, bf16[128,128]{1,0:T(8,128)(2,1)}) fusion(f32[128,256]{1,0:T(8,128)S(1)} %slice_bitcast_fusion.2, bf16[128,256]{1,0:T(8,128)(2,1)S(1)} %collective-permute-done.20, bf16[128,256]{1,0:T(8,128)(2,1)S(1)} %collective-permute-done.19, bf16[128,256]{1,0:T(8,128)(2,1)S(1)} %collective-permute-done.18), kind=kLoop, calls=%fused_computation.17 | loop fusion | flops 229376 | bytes 393216 | tf_op jit(solution)/shard_map/convert_element_type | solution.py:397
  (35 shorter events, 0.5 us)
Async XLA Ops:
  2.4 12.8 %collective-permute-start.3 = (bf16[128,256]{1,0:T(8,128)(2,1)}, bf16[128,256]{1,0:T(8,128)(2,1)S(1)}, u32[]{:S(2)}, u32[]{:S(2)}) collective-permute-start(bf16[128,256]{1,0:T(8,128)(2,1)} %get-tuple-element.36), channel_id=1, source_target_pairs={{0,96},{8,104},{16,112},{24,120},{32,64},{40,72},{48,80},{56,88},{... | collective-permute-start | bytes 196616 | tf_op jit(solution)/shard_map/ppermute | solution.py:27
  7.1 8.1 %collective-permute-start.2 = (bf16[128,256]{1,0:T(8,128)(2,1)}, bf16[128,256]{1,0:T(8,128)(2,1)S(1)}, u32[]{:S(2)}, u32[]{:S(2)}) collective-permute-start(bf16[128,256]{1,0:T(8,128)(2,1)} %get-tuple-element.36), channel_id=1, source_target_pairs={{0,64},{8,72},{16,80},{24,88},{32,96},{40,104},{48,112},{56,120},{... | collective-permute-start | bytes 196616 | tf_op jit(solution)/shard_map/ppermute | solution.py:27
  7.1 7.5 %collective-permute-start = (bf16[128,256]{1,0:T(8,128)(2,1)}, bf16[128,256]{1,0:T(8,128)(2,1)S(1)}, u32[]{:S(2)}, u32[]{:S(2)}) collective-permute-start(bf16[128,256]{1,0:T(8,128)(2,1)} %get-tuple-element.36), channel_id=1, source_target_pairs={{0,16},{8,24},{16,0},{24,8},{32,48},{40,56},{48,32},{56,40},{64,80... | collective-permute-start | bytes 196616 | tf_op jit(solution)/shard_map/ppermute | solution.py:27
  8.6 14.4 %collective-permute-start.12 = (bf16[128,640]{1,0:T(8,128)(2,1)}, bf16[128,640]{1,0:T(8,128)(2,1)S(1)}, u32[]{:S(2)}, u32[]{:S(2)}) collective-permute-start(bf16[128,640]{1,0:T(8,128)(2,1)} %param.10), channel_id=1, source_target_pairs={{0,2},{1,3},{2,0},{3,1},{4,6},{5,7},{6,4},{7,5},{8,10},{9,11},{10,... | collective-permute-start | bytes 491528 | tf_op jit(solution)/shard_map/ppermute | solution.py:37
  10.8 8.1 %collective-permute-start.9 = (bf16[128,640]{1,0:T(8,128)(2,1)}, bf16[128,640]{1,0:T(8,128)(2,1)S(1)}, u32[]{:S(2)}, u32[]{:S(2)}) collective-permute-start(bf16[128,640]{1,0:T(8,128)(2,1)} %param.10), channel_id=1, source_target_pairs={{0,4},{1,5},{2,6},{3,7},{4,0},{5,1},{6,2},{7,3},{8,12},{9,13},{10,... | collective-permute-start | bytes 491528 | tf_op jit(solution)/shard_map/ppermute | solution.py:37
  14.5 8.0 %collective-permute-start.1 = (bf16[256,256]{1,0:T(8,128)(2,1)S(1)}, bf16[256,256]{1,0:T(8,128)(2,1)S(1)}, u32[]{:S(2)}, u32[]{:S(2)}) collective-permute-start(bf16[256,256]{1,0:T(8,128)(2,1)S(1)} %constant_dynamic-update-slice_fusion.refs_0_.refs_7_), channel_id=1, source_target_pairs={{0,32},{8,40},{16,48},{24,56},{32,0},{40,8},{48,16},{56,24},{64,96... | collective-permute-start | bytes 393224 | tf_op jit(solution)/shard_map/ppermute | solution.py:27
  15.2 7.3 %collective-permute-start.4 = (bf16[256,256]{1,0:T(8,128)(2,1)S(1)}, bf16[256,256]{1,0:T(8,128)(2,1)S(1)}, u32[]{:S(2)}, u32[]{:S(2)}) collective-permute-start(bf16[256,256]{1,0:T(8,128)(2,1)S(1)} %constant_dynamic-update-slice_fusion.2.refs_2_.refs_10_), channel_id=1, source_target_pairs={{0,16},{8,24},{16,0},{24,8},{32,48},{40,56},{48,32},{56,40},{64,80... | collective-permute-start | bytes 393224 | tf_op jit(solution)/shard_map/ppermute | solution.py:27
  19.8 11.1 %collective-permute-start.11 = (bf16[2,128,640]{2,1,0:T(8,128)(2,1)S(1)}, bf16[2,128,640]{2,1,0:T(8,128)(2,1)S(1)}, u32[]{:S(2)}, u32[]{:S(2)}) collective-permute-start(bf16[2,128,640]{2,1,0:T(8,128)(2,1)S(1)} %pad_maximum_fusion.pair_ref), channel_id=1, source_target_pairs={{0,3},{1,2},{2,1},{3,0},{4,7},{5,6},{6,5},{7,4},{8,11},{9,10},{10,... | collective-permute-start | bytes 983048 | tf_op jit(solution)/shard_map/ppermute | solution.py:37
  19.9 11.0 %collective-permute-start.10 = (bf16[2,128,640]{2,1,0:T(8,128)(2,1)S(1)}, bf16[2,128,640]{2,1,0:T(8,128)(2,1)S(1)}, u32[]{:S(2)}, u32[]{:S(2)}) collective-permute-start(bf16[2,128,640]{2,1,0:T(8,128)(2,1)S(1)} %pad_maximum_fusion.pair_ref), channel_id=1, source_target_pairs={{0,1},{1,0},{2,3},{3,2},{4,5},{5,4},{6,7},{7,6},{8,9},{9,8},{10,11... | collective-permute-start | bytes 983048 | tf_op jit(solution)/shard_map/ppermute | solution.py:37
  22.5 1.3 %collective-permute-start.5 = (bf16[256,256]{1,0:T(8,128)(2,1)S(1)}, bf16[256,256]{1,0:T(8,128)(2,1)S(1)}, u32[]{:S(2)}, u32[]{:S(2)}) collective-permute-start(bf16[256,256]{1,0:T(8,128)(2,1)S(1)} %constant_dynamic-update-slice_fusion.refs_0_.refs_7_), channel_id=1, source_target_pairs={{0,8},{8,0},{16,24},{24,16},{32,40},{40,32},{48,56},{56,48},{64,72... | collective-permute-start | bytes 393224 | tf_op jit(solution)/shard_map/ppermute | solution.py:27
  22.5 1.5 %collective-permute-start.6 = (bf16[256,256]{1,0:T(8,128)(2,1)S(1)}, bf16[256,256]{1,0:T(8,128)(2,1)S(1)}, u32[]{:S(2)}, u32[]{:S(2)}) collective-permute-start(bf16[256,256]{1,0:T(8,128)(2,1)S(1)} %collective-permute-done.1.refs_1_.refs_8_), channel_id=1, source_target_pairs={{0,8},{8,0},{16,24},{24,16},{32,40},{40,32},{48,56},{56,48},{64,72... | collective-permute-start | bytes 393224 | tf_op jit(solution)/shard_map/ppermute | solution.py:27
  23.0 4.0 %collective-permute-start.7 = (bf16[256,256]{1,0:T(8,128)(2,1)S(1)}, bf16[256,256]{1,0:T(8,128)(2,1)S(1)}, u32[]{:S(2)}, u32[]{:S(2)}) collective-permute-start(bf16[256,256]{1,0:T(8,128)(2,1)S(1)} %constant_dynamic-update-slice_fusion.2.refs_2_.refs_10_), channel_id=1, source_target_pairs={{0,8},{8,0},{16,24},{24,16},{32,40},{40,32},{48,56},{56,48},{64,72... | collective-permute-start | bytes 393224 | tf_op jit(solution)/shard_map/ppermute | solution.py:27
  23.9 3.2 %collective-permute-start.8 = (bf16[256,256]{1,0:T(8,128)(2,1)S(1)}, bf16[256,256]{1,0:T(8,128)(2,1)S(1)}, u32[]{:S(2)}, u32[]{:S(2)}) collective-permute-start(bf16[256,256]{1,0:T(8,128)(2,1)S(1)} %collective-permute-done.4.refs_3_.refs_11_), channel_id=1, source_target_pairs={{0,8},{8,0},{16,24},{24,16},{32,40},{40,32},{48,56},{56,48},{64,72... | collective-permute-start | bytes 393224 | tf_op jit(solution)/shard_map/ppermute | solution.py:27
  24.1 8.6 %collective-permute-start.13 = (bf16[128,640]{1,0:T(8,128)(2,1)S(1)}, bf16[128,640]{1,0:T(8,128)(2,1)S(1)}, u32[]{:S(2)}, u32[]{:S(2)}) collective-permute-start(bf16[128,640]{1,0:T(8,128)(2,1)S(1)} %collective-permute-done.12.across_ref), channel_id=1, source_target_pairs={{0,4},{1,5},{2,6},{3,7},{4,0},{5,1},{6,2},{7,3},{8,12},{9,13},{10,... | collective-permute-start | bytes 491528 | tf_op jit(solution)/shard_map/ppermute | solution.py:37
  27.0 0.9 %copy-start = (bf16[144,640]{1,0:T(8,128)(2,1)S(1)}, bf16[144,640]{1,0:T(8,128)(2,1)}, u32[]{:S(2)}) copy-start(bf16[144,640]{1,0:T(8,128)(2,1)} %get-tuple-element.34.qt_ref.refs_0_) | copy-start | bytes 552964
  28.0 4.7 %copy-start.1 = (bf16[640,128]{1,0:T(8,128)(2,1)S(1)}, bf16[640,128]{1,0:T(8,128)(2,1)}, u32[]{:S(2)}) copy-start(bf16[640,128]{1,0:T(8,128)(2,1)} %get-tuple-element.44.refs_4_) | copy-start | bytes 491524
  33.2 1.6 %collective-permute-start.14 = (bf16[2,2,128,256]{3,2,1,0:T(8,128)(2,1)S(1)}, bf16[2,2,128,256]{3,2,1,0:T(8,128)(2,1)S(1)}, u32[]{:S(2)}, u32[]{:S(2)}) collective-permute-start(bf16[2,2,128,256]{3,2,1,0:T(8,128)(2,1)S(1)} %get-tuple-element.53), channel_id=1, source_target_pairs={{0,8},{8,0},{16,24},{24,16},{32,40},{40,32},{48,56},{56,48},{64,72... | collective-permute-start | bytes 786440 | tf_op jit(solution)/shard_map/ppermute | solution.py:27
  34.9 1.8 %collective-permute-start.15 = (bf16[2,2,128,256]{3,2,1,0:T(8,128)(2,1)S(1)}, bf16[2,2,128,256]{3,2,1,0:T(8,128)(2,1)S(1)}, u32[]{:S(2)}, u32[]{:S(2)}) collective-permute-start(bf16[2,2,128,256]{3,2,1,0:T(8,128)(2,1)S(1)} %get-tuple-element.59), channel_id=1, source_target_pairs={{0,8},{8,0},{16,24},{24,16},{32,40},{40,32},{48,56},{56,48},{64,72... | collective-permute-start | bytes 786440 | tf_op jit(solution)/shard_map/ppermute | solution.py:27
  35.1 6.4 %collective-permute-start.17 = (bf16[2,128,256]{2,1,0:T(8,128)(2,1)S(1)}, bf16[2,128,256]{2,1,0:T(8,128)(2,1)S(1)}, u32[]{:S(2)}, u32[]{:S(2)}) collective-permute-start(bf16[2,128,256]{2,1,0:T(8,128)(2,1)S(1)} %fusion.3), channel_id=1, source_target_pairs={{0,16},{8,24},{16,0},{24,8},{32,48},{40,56},{48,32},{56,40},{64,80... | collective-permute-start | bytes 393224 | tf_op jit(solution)/shard_map/ppermute | solution.py:27
  36.7 7.4 %collective-permute-start.16 = (bf16[2,128,256]{2,1,0:T(8,128)(2,1)S(1)}, bf16[2,128,256]{2,1,0:T(8,128)(2,1)S(1)}, u32[]{:S(2)}, u32[]{:S(2)}) collective-permute-start(bf16[2,128,256]{2,1,0:T(8,128)(2,1)S(1)} %fusion.4), channel_id=1, source_target_pairs={{0,16},{8,24},{16,0},{24,8},{32,48},{40,56},{48,32},{56,40},{64,80... | collective-permute-start | bytes 393224 | tf_op jit(solution)/shard_map/ppermute | solution.py:27
  41.5 10.1 %collective-permute-start.18 = (bf16[128,256]{1,0:T(8,128)(2,1)S(1)}, bf16[128,256]{1,0:T(8,128)(2,1)S(1)}, u32[]{:S(2)}, u32[]{:S(2)}) collective-permute-start(bf16[128,256]{1,0:T(8,128)(2,1)S(1)} %get-tuple-element.62), channel_id=1, source_target_pairs={{64,0},{72,8},{80,16},{88,24},{96,32},{104,40},{112,48},{120,56},{... | collective-permute-start | bytes 196616 | tf_op jit(solution)/shard_map/ppermute | solution.py:32
  42.8 8.8 %collective-permute-start.19 = (bf16[128,256]{1,0:T(8,128)(2,1)S(1)}, bf16[128,256]{1,0:T(8,128)(2,1)S(1)}, u32[]{:S(2)}, u32[]{:S(2)}) collective-permute-start(bf16[128,256]{1,0:T(8,128)(2,1)S(1)} %get-tuple-element.63), channel_id=1, source_target_pairs={{64,32},{72,40},{80,48},{88,56},{96,0},{104,8},{112,16},{120,24},{... | collective-permute-start | bytes 196616 | tf_op jit(solution)/shard_map/ppermute | solution.py:32
  44.2 7.4 %collective-permute-start.20 = (bf16[128,256]{1,0:T(8,128)(2,1)S(1)}, bf16[128,256]{1,0:T(8,128)(2,1)S(1)}, u32[]{:S(2)}, u32[]{:S(2)}) collective-permute-start(bf16[128,256]{1,0:T(8,128)(2,1)S(1)} %fusion.5), channel_id=1, source_target_pairs={{0,32},{8,40},{16,48},{24,56},{32,0},{40,8},{48,16},{56,24},{64,96... | collective-permute-start | bytes 196616 | tf_op jit(solution)/shard_map/ppermute | solution.py:27

commit v5 on v4

--- a/solution.py
+++ b/solution.py
@@ -365,8 +365,10 @@
     own, out_grad = lax.optimization_barrier((own, out_grad))
     og_pair = jnp.stack([out_grad, head_swap(out_grad, 4)])
     reach = jnp.concatenate([ctx_swap(own, 8), ctx_swap(own, 12)], axis=0)
-    pair = jnp.concatenate([own, ctx_swap(own, 2)], axis=0)
-    across = head_swap(out_grad, 2)
+    mate = ctx_swap(own, 2)
+    pair = jnp.concatenate([own, mate], axis=0)
+    later, _ = lax.optimization_barrier((out_grad, mate))
+    across = head_swap(later, 2)
     both = head_swap(across, 4)
     one, three = head_swap(og_pair, 1), head_swap(og_pair, 3)
     tiles = [*lax.optimization_barrier((pair, ctx_swap(pair, 4))), *lax.optimization_barrier((reach, ctx_swap(reach, 2)))]

time: 52.5 us -> 54 us (1.029)
  starting transfers between devices: 24.5 us -> 27.8 us
  waiting for transfers between devices: 14.7 us -> 12.8 us
    ppermute x5, waiting for transfers between devices: 3.46 us -> 1.04 us  [head_swap(): return lax.ppermute(value, 'head', [(i, i ^ bits) for i in range(count)])]
    ppermute x5, starting transfers between devices: 10.7 us -> 12.3 us  [head_swap(): return lax.ppermute(value, 'head', [(i, i ^ bits) for i in range(count)])]
    ppermute x14, starting transfers between devices: 11.2 us -> 12.9 us  [ctx_swap(): return lax.ppermute(value, 'ctx', [(i, i ^ bits) for i in range(count)])]
    ppermute x2, waiting for transfers between devices: 6.49 us -> 7.45 us  [send_back(): lax.ppermute(value, 'ctx', [(i, i ^ bits) for i in range(count) if i ^ bi...]
  transfers between devices with their start and end apart: 21 -> 21, of which waited for: 5 -> 7; matrix products, arithmetic and copies ran while one was open for 4% -> 4% of each run, Pallas kernels for 12% -> 12%
where the time goes in v5:
time: 54 us; the launch traced here: 53.7 us
  starting transfers between devices  27.8 us (51%)
  waiting for transfers between devices  12.8 us (24%)
  Pallas kernels  8.65 us (16%)
  local copies, waits for them, and re-layouts  1.85 us (3%)
  other arithmetic  1.79 us (3%)
  between operations  0.84 us (2%)
    ppermute x14, starting transfers between devices, ctx_swap(): return lax.ppermute(value, 'ctx', [(i, i ^ bits) for i in range(count)])  12.9 us
    ppermute x5, starting transfers between devices, head_swap(): return lax.ppermute(value, 'head', [(i, i ^ bits) for i in range(count)])  12.3 us
    ppermute x2, waiting for transfers between devices, send_back(): lax.ppermute(value, 'ctx', [(i, i ^ bits) for i in range(count) if i ^ bi...  7.45 us
    ppermute x14, waiting for transfers between devices, ctx_swap(): return lax.ppermute(value, 'ctx', [(i, i ^ bits) for i in range(count)])  4.29 us
    pallas_call x1, Pallas kernels, attend(): pl.pallas_call(attend_kernel, out_shape=(jax.ShapeDtypeStruct((TILES, key...  2.91 us
    ppermute x2, starting transfers between devices, send_back(): lax.ppermute(value, 'ctx', [(i, i ^ bits) for i in range(count) if i ^ bi...  2.58 us
    pallas_call x1, Pallas kernels, prepare(): pl.pallas_call(prepare_kernel, out_shape=(jax.ShapeDtypeStruct((count, 2...  1.8 us
    unnamed x6, local copies, waits for them, and re-layouts  1.77 us
  transfers between devices with their start and end apart: 21, of which 7 were waited for; matrix products, arithmetic and copies ran while one was open for 4% of the time, Pallas kernels for 12%

profile of v5, /device:TPU:2, one launch (start us, length us, event | category | flops | bytes accessed | tf_op | source)
XLA Modules:
  0.0 53.7 jit_solution(14014708373981924634)
XLA Ops:
  0.6 1.8 %prepare.1 = (bf16[128,256]{1,0:T(8,128)(2,1)}, bf16[144,640]{1,0:T(8,128)(2,1)}, bf16[640,128]{1,0:T(8,128)(2,1)}) custom-call(s32[4]{0:T(128)} %lens_ref.1, s32[4]{0:T(128)} %prompts_ref.1, bf16[128,128]{1,0:T(8,128)(2,1)} %k_ref.1, bf16[128,128]{1,0:T(8,128)(2,1)} %v_ref.1, bf16[128,640]{1,0:T(8,128)(2,1)} %q_ref.1), custom_call_target="tpu_custom_call" | custom-call | tf_op jit(solution)/shard_map/prepare/pallas_call | solution.py:245
  2.4 4.6 %collective-permute-start.3 = (bf16[128,256]{1,0:T(8,128)(2,1)}, bf16[128,256]{1,0:T(8,128)(2,1)S(1)}, u32[]{:S(2)}, u32[]{:S(2)}) collective-permute-start(bf16[128,256]{1,0:T(8,128)(2,1)} %get-tuple-element.37), channel_id=1, source_target_pairs={{0,96},{8,104},{16,112},{24,120},{32,64},{40,72},{48,80},{56,88},{... | collective-permute-start | bytes 196616 | tf_op jit(solution)/shard_map/ppermute | solution.py:27
  7.1 1.6 %collective-permute-start = (bf16[128,256]{1,0:T(8,128)(2,1)}, bf16[128,256]{1,0:T(8,128)(2,1)S(1)}, u32[]{:S(2)}, u32[]{:S(2)}) collective-permute-start(bf16[128,256]{1,0:T(8,128)(2,1)} %get-tuple-element.37), channel_id=1, source_target_pairs={{0,16},{8,24},{16,0},{24,8},{32,48},{40,56},{48,32},{56,40},{64,80... | collective-permute-start | bytes 196616 | tf_op jit(solution)/shard_map/ppermute | solution.py:27
  8.6 2.9 %collective-permute-start.9 = (bf16[128,640]{1,0:T(8,128)(2,1)}, bf16[128,640]{1,0:T(8,128)(2,1)S(1)}, u32[]{:S(2)}, u32[]{:S(2)}) collective-permute-start(bf16[128,640]{1,0:T(8,128)(2,1)} %param.10), channel_id=1, source_target_pairs={{0,4},{1,5},{2,6},{3,7},{4,0},{5,1},{6,2},{7,3},{8,12},{9,13},{10,... | collective-permute-start | bytes 491528 | tf_op jit(solution)/shard_map/ppermute | solution.py:37
  11.5 0.8 %constant_dynamic-update-slice_fusion.1 = bf16[256,256]{1,0:T(8,128)(2,1)S(1)} fusion(bf16[128,256]{1,0:T(8,128)(2,1)} %get-tuple-element.37), kind=kLoop, calls=%fused_computation.20 | loop fusion | bytes 131072
  12.4 0.7 %collective-permute-start.1 = (bf16[256,256]{1,0:T(8,128)(2,1)S(1)}, bf16[256,256]{1,0:T(8,128)(2,1)S(1)}, u32[]{:S(2)}, u32[]{:S(2)}) collective-permute-start(bf16[256,256]{1,0:T(8,128)(2,1)S(1)} %constant_dynamic-update-slice_fusion.refs_0_.refs_7_), channel_id=1, source_target_pairs={{0,32},{8,40},{16,48},{24,56},{32,0},{40,8},{48,16},{56,24},{64,96... | collective-permute-start | bytes 393224 | tf_op jit(solution)/shard_map/ppermute | solution.py:27
  13.1 1.1 %collective-permute-start.4 = (bf16[256,256]{1,0:T(8,128)(2,1)S(1)}, bf16[256,256]{1,0:T(8,128)(2,1)S(1)}, u32[]{:S(2)}, u32[]{:S(2)}) collective-permute-start(bf16[256,256]{1,0:T(8,128)(2,1)S(1)} %constant_dynamic-update-slice_fusion.2.refs_2_.refs_10_), channel_id=1, source_target_pairs={{0,16},{8,24},{16,0},{24,8},{32,48},{40,56},{48,32},{56,40},{64,80... | collective-permute-start | bytes 393224 | tf_op jit(solution)/shard_map/ppermute | solution.py:27
  14.2 2.1 %collective-permute-start.12 = (bf16[128,640]{1,0:T(8,128)(2,1)}, bf16[128,640]{1,0:T(8,128)(2,1)S(1)}, u32[]{:S(2)}, u32[]{:S(2)}) collective-permute-start(bf16[128,640]{1,0:T(8,128)(2,1)} %param.10), channel_id=1, source_target_pairs={{0,2},{1,3},{2,0},{3,1},{4,6},{5,7},{6,4},{7,5},{8,10},{9,11},{10,... | collective-permute-start | bytes 491528 | tf_op jit(solution)/shard_map/ppermute | solution.py:37
  16.3 0.5 collective-permute-done.9
  16.8 1.0 %pad_maximum_fusion.pair_ref = bf16[2,128,640]{2,1,0:T(8,128)(2,1)S(1)} fusion(bf16[1,128,640]{2,1,0:T(8,128)(2,1)S(1)} %bitcast.25, bf16[1,128,640]{2,1,0:T(8,128)(2,1)} %bitcast.24), kind=kLoop, calls=%fused_computation.2 | loop fusion | flops 163840 | bytes 655360 | tf_op jit(solution)/shard_map/stack | solution.py:366
  17.7 1.6 %collective-permute-start.11 = (bf16[2,128,640]{2,1,0:T(8,128)(2,1)S(1)}, bf16[2,128,640]{2,1,0:T(8,128)(2,1)S(1)}, u32[]{:S(2)}, u32[]{:S(2)}) collective-permute-start(bf16[2,128,640]{2,1,0:T(8,128)(2,1)S(1)} %pad_maximum_fusion.pair_ref), channel_id=1, source_target_pairs={{0,3},{1,2},{2,1},{3,0},{4,7},{5,6},{6,5},{7,4},{8,11},{9,10},{10,... | collective-permute-start | bytes 983048 | tf_op jit(solution)/shard_map/ppermute | solution.py:37
  19.3 1.8 %collective-permute-start.10 = (bf16[2,128,640]{2,1,0:T(8,128)(2,1)S(1)}, bf16[2,128,640]{2,1,0:T(8,128)(2,1)S(1)}, u32[]{:S(2)}, u32[]{:S(2)}) collective-permute-start(bf16[2,128,640]{2,1,0:T(8,128)(2,1)S(1)} %pad_maximum_fusion.pair_ref), channel_id=1, source_target_pairs={{0,1},{1,0},{2,3},{3,2},{4,5},{5,4},{6,7},{7,6},{8,9},{9,8},{10,11... | collective-permute-start | bytes 983048 | tf_op jit(solution)/shard_map/ppermute | solution.py:37
  21.1 0.5 collective-permute-start.6
  21.6 0.5 %collective-permute-done.12.across_ref = bf16[128,640]{1,0:T(8,128)(2,1)S(1)} collective-permute-done((bf16[128,640]{1,0:T(8,128)(2,1)}, bf16[128,640]{1,0:T(8,128)(2,1)S(1)}, u32[]{:S(2)}, u32[]{:S(2)}) %collective-permute-start.12) | collective-permute-done | bytes 163872 | tf_op jit(solution)/shard_map/ppermute | solution.py:37
  22.2 0.3 collective-permute-done.5.refs_4_.refs_7_
  22.5 0.2 collective-permute-start.8
  22.7 3.9 %collective-permute-start.13 = (bf16[128,640]{1,0:T(8,128)(2,1)S(1)}, bf16[128,640]{1,0:T(8,128)(2,1)S(1)}, u32[]{:S(2)}, u32[]{:S(2)}) collective-permute-start(bf16[128,640]{1,0:T(8,128)(2,1)S(1)} %collective-permute-done.12.across_ref), channel_id=1, source_target_pairs={{0,4},{1,5},{2,6},{3,7},{4,0},{5,1},{6,2},{7,3},{8,12},{9,13},{10,... | collective-permute-start | bytes 491528 | tf_op jit(solution)/shard_map/ppermute | solution.py:37
  26.6 0.9 %copy-done = bf16[144,640]{1,0:T(8,128)(2,1)S(1)} copy-done((bf16[144,640]{1,0:T(8,128)(2,1)S(1)}, bf16[144,640]{1,0:T(8,128)(2,1)}, u32[]{:S(2)}) %copy-start) | copy-done | bytes 184344
  27.5 2.9 %attend.1 = (bf16[8,256,640]{2,1,0:T(8,128)(2,1)S(1)}, f32[128,640]{1,0:T(8,128)S(1)}, f32[8,640]{1,0:T(8,128)S(1)}, bf16[640,5120]{1,0:T(8,128)(2,1)S(1)}) custom-call(bf16[640,5120]{1,0:T(8,128)(2,1)} %w_ref.1, bf16[144,640]{1,0:T(8,128)(2,1)S(1)} %copy-done, bf16[256,256]{1,0:T(8,128)(2,1)S(1)} %constant_dynamic-update-slice_fusion.refs_0_.refs_7_, ...), custom_call_target="tpu_custom_call" | custom-call | flops 671088640 | bytes 2621440 | tf_op jit(solution)/shard_map/attend/pallas_call | solution.py:262
  30.5 1.7 %project.1.refs_2_ = f32[640,128]{1,0:T(8,128)S(1)} custom-call(bf16[640,5120]{1,0:T(8,128)(2,1)S(1)} %get-tuple-element.43.w_ref.refs_1_, bf16[2,128,640]{2,1,0:T(8,128)(2,1)S(1)} %pad_maximum_fusion.pair_ref, bf16[2,128,640]{2,1,0:T(8,128)(2,1)S(1)} %collective-permute-done.10.one_ref, bf16[2,128,640]{2,1,0:T(8,128)(2,1)S(1)} %collective-permute-done.11.three_ref, ...), custom_call_target="tpu_custom_call" | custom-call | flops 838860800 | bytes 6553600 | tf_op jit(solution)/shard_map/project/pallas_call | solution.py:289
  32.2 0.6 %far_gradients.1 = (f32[2,2,128,256]{3,2,1,0:T(8,128)S(1)}, bf16[2,2,128,256]{3,2,1,0:T(8,128)(2,1)S(1)}, bf16[128,640]{1,0:T(8,128)(2,1)S(1)}, bf16[640,128]{1,...) custom-call(bf16[144,640]{1,0:T(8,128)(2,1)S(1)} %copy-done, ...), custom_call_target="tpu_custom_call" | custom-call | flops 1509949440 | bytes 6553600 | tf_op jit(solution)/shard_map/far_gradients/pallas_call | solution.py:310
  33.1 1.3 %collective-permute-done.14 = bf16[2,2,128,256]{3,2,1,0:T(8,128)(2,1)S(1)} collective-permute-done((bf16[2,2,128,256]{3,2,1,0:T(8,128)(2,1)S(1)}, bf16[2,2,128,256]{3,2,1,0:T(8,128)(2,1)S(1)}, u32[]{:S(2)}, u32[]{:S(2)}) %collective-permute-start.14) | collective-permute-done | bytes 262176 | tf_op jit(solution)/shard_map/ppermute | solution.py:27
  34.6 0.2 collective-permute-start.17
  34.9 1.5 %near_gradients.3 = (f32[2,2,128,256]{3,2,1,0:T(8,128)S(1)}, bf16[128,640]{1,0:T(8,128)(2,1)}) custom-call(bf16[144,640]{1,0:T(8,128)(2,1)S(1)} %copy-done, bf16[8,256,640]{2,1,0:T(8,128)(2,1)S(1)} %get-tuple-element.42.refs_7_.refs_1_, bf16[128,640]{1,0:T(8,128)(2,1)S(1)} %get-tuple-element.49.refs_2_, bf16[640,128]{1,0:T(8,128)(2,1)S(1)} %get-tuple-element.50.refs_3_, ...), custom_call_target="tpu_custom_call" | custom-call | flops 335544320 | bytes 655360 | tf_op jit(solution)/shard_map/near_gradients/pallas_call | solution.py:346
  36.4 2.0 %collective-permute-start.16 = (bf16[2,128,256]{2,1,0:T(8,128)(2,1)S(1)}, bf16[2,128,256]{2,1,0:T(8,128)(2,1)S(1)}, u32[]{:S(2)}, u32[]{:S(2)}) collective-permute-start(bf16[2,128,256]{2,1,0:T(8,128)(2,1)S(1)} %fusion.4), channel_id=1, source_target_pairs={{0,16},{8,24},{16,0},{24,8},{32,48},{40,56},{48,32},{56,40},{64,80... | collective-permute-start | bytes 393224 | tf_op jit(solution)/shard_map/ppermute | solution.py:27
  38.4 2.7 %collective-permute-done.17 = bf16[2,128,256]{2,1,0:T(8,128)(2,1)S(1)} collective-permute-done((bf16[2,128,256]{2,1,0:T(8,128)(2,1)S(1)}, bf16[2,128,256]{2,1,0:T(8,128)(2,1)S(1)}, u32[]{:S(2)}, u32[]{:S(2)}) %collective-permute-start.17) | collective-permute-done | bytes 131104 | tf_op jit(solution)/shard_map/ppermute | solution.py:27
  41.1 1.3 %collective-permute-start.18 = (bf16[128,256]{1,0:T(8,128)(2,1)S(1)}, bf16[128,256]{1,0:T(8,128)(2,1)S(1)}, u32[]{:S(2)}, u32[]{:S(2)}) collective-permute-start(bf16[128,256]{1,0:T(8,128)(2,1)S(1)} %get-tuple-element.64), channel_id=1, source_target_pairs={{64,0},{72,8},{80,16},{88,24},{96,32},{104,40},{112,48},{120,56},{... | collective-permute-start | bytes 196616 | tf_op jit(solution)/shard_map/ppermute | solution.py:32
  42.4 1.3 %collective-permute-start.19 = (bf16[128,256]{1,0:T(8,128)(2,1)S(1)}, bf16[128,256]{1,0:T(8,128)(2,1)S(1)}, u32[]{:S(2)}, u32[]{:S(2)}) collective-permute-start(bf16[128,256]{1,0:T(8,128)(2,1)S(1)} %get-tuple-element.65), channel_id=1, source_target_pairs={{64,32},{72,40},{80,48},{88,56},{96,0},{104,8},{112,16},{120,24},{... | collective-permute-start | bytes 196616 | tf_op jit(solution)/shard_map/ppermute | solution.py:32
  43.8 1.7 %collective-permute-start.20 = (bf16[128,256]{1,0:T(8,128)(2,1)S(1)}, bf16[128,256]{1,0:T(8,128)(2,1)S(1)}, u32[]{:S(2)}, u32[]{:S(2)}) collective-permute-start(bf16[128,256]{1,0:T(8,128)(2,1)S(1)} %fusion.5), channel_id=1, source_target_pairs={{0,32},{8,40},{16,48},{24,56},{32,0},{40,8},{48,16},{56,24},{64,96... | collective-permute-start | bytes 196616 | tf_op jit(solution)/shard_map/ppermute | solution.py:27
  45.5 4.4 %collective-permute-done.18 = bf16[128,256]{1,0:T(8,128)(2,1)S(1)} collective-permute-done((bf16[128,256]{1,0:T(8,128)(2,1)S(1)}, bf16[128,256]{1,0:T(8,128)(2,1)S(1)}, u32[]{:S(2)}, u32[]{:S(2)}) %collective-permute-start.18) | collective-permute-done | bytes 65568 | tf_op jit(solution)/shard_map/ppermute | solution.py:32
  49.9 3.1 %collective-permute-done.19 = bf16[128,256]{1,0:T(8,128)(2,1)S(1)} collective-permute-done((bf16[128,256]{1,0:T(8,128)(2,1)S(1)}, bf16[128,256]{1,0:T(8,128)(2,1)S(1)}, u32[]{:S(2)}, u32[]{:S(2)}) %collective-permute-start.19) | collective-permute-done | bytes 65568 | tf_op jit(solution)/shard_map/ppermute | solution.py:32
  53.0 0.7 %add_convert_fusion = (bf16[128,128]{1,0:T(8,128)(2,1)}, bf16[128,128]{1,0:T(8,128)(2,1)}) fusion(f32[128,256]{1,0:T(8,128)S(1)} %slice_bitcast_fusion.2, bf16[128,256]{1,0:T(8,128)(2,1)S(1)} %collective-permute-done.20, bf16[128,256]{1,0:T(8,128)(2,1)S(1)} %collective-permute-done.19, bf16[128,256]{1,0:T(8,128)(2,1)S(1)} %collective-permute-done.18), kind=kLoop, calls=%fused_computation.17 | loop fusion | flops 229376 | bytes 393216 | tf_op jit(solution)/shard_map/convert_element_type | solution.py:399
  (35 shorter events, 0.7 us)
Async XLA Ops:
  2.4 10.6 %collective-permute-start.3 = (bf16[128,256]{1,0:T(8,128)(2,1)}, bf16[128,256]{1,0:T(8,128)(2,1)S(1)}, u32[]{:S(2)}, u32[]{:S(2)}) collective-permute-start(bf16[128,256]{1,0:T(8,128)(2,1)} %get-tuple-element.37), channel_id=1, source_target_pairs={{0,96},{8,104},{16,112},{24,120},{32,64},{40,72},{48,80},{56,88},{... | collective-permute-start | bytes 196616 | tf_op jit(solution)/shard_map/ppermute | solution.py:27
  7.1 6.0 %collective-permute-start.2 = (bf16[128,256]{1,0:T(8,128)(2,1)}, bf16[128,256]{1,0:T(8,128)(2,1)S(1)}, u32[]{:S(2)}, u32[]{:S(2)}) collective-permute-start(bf16[128,256]{1,0:T(8,128)(2,1)} %get-tuple-element.37), channel_id=1, source_target_pairs={{0,64},{8,72},{16,80},{24,88},{32,96},{40,104},{48,112},{56,120},{... | collective-permute-start | bytes 196616 | tf_op jit(solution)/shard_map/ppermute | solution.py:27
  7.1 5.3 %collective-permute-start = (bf16[128,256]{1,0:T(8,128)(2,1)}, bf16[128,256]{1,0:T(8,128)(2,1)S(1)}, u32[]{:S(2)}, u32[]{:S(2)}) collective-permute-start(bf16[128,256]{1,0:T(8,128)(2,1)} %get-tuple-element.37), channel_id=1, source_target_pairs={{0,16},{8,24},{16,0},{24,8},{32,48},{40,56},{48,32},{56,40},{64,80... | collective-permute-start | bytes 196616 | tf_op jit(solution)/shard_map/ppermute | solution.py:27
  8.6 8.1 %collective-permute-start.9 = (bf16[128,640]{1,0:T(8,128)(2,1)}, bf16[128,640]{1,0:T(8,128)(2,1)S(1)}, u32[]{:S(2)}, u32[]{:S(2)}) collective-permute-start(bf16[128,640]{1,0:T(8,128)(2,1)} %param.10), channel_id=1, source_target_pairs={{0,4},{1,5},{2,6},{3,7},{4,0},{5,1},{6,2},{7,3},{8,12},{9,13},{10,... | collective-permute-start | bytes 491528 | tf_op jit(solution)/shard_map/ppermute | solution.py:37
  12.4 8.7 %collective-permute-start.1 = (bf16[256,256]{1,0:T(8,128)(2,1)S(1)}, bf16[256,256]{1,0:T(8,128)(2,1)S(1)}, u32[]{:S(2)}, u32[]{:S(2)}) collective-permute-start(bf16[256,256]{1,0:T(8,128)(2,1)S(1)} %constant_dynamic-update-slice_fusion.refs_0_.refs_7_), channel_id=1, source_target_pairs={{0,32},{8,40},{16,48},{24,56},{32,0},{40,8},{48,16},{56,24},{64,96... | collective-permute-start | bytes 393224 | tf_op jit(solution)/shard_map/ppermute | solution.py:27
  13.1 8.0 %collective-permute-start.4 = (bf16[256,256]{1,0:T(8,128)(2,1)S(1)}, bf16[256,256]{1,0:T(8,128)(2,1)S(1)}, u32[]{:S(2)}, u32[]{:S(2)}) collective-permute-start(bf16[256,256]{1,0:T(8,128)(2,1)S(1)} %constant_dynamic-update-slice_fusion.2.refs_2_.refs_10_), channel_id=1, source_target_pairs={{0,16},{8,24},{16,0},{24,8},{32,48},{40,56},{48,32},{56,40},{64,80... | collective-permute-start | bytes 393224 | tf_op jit(solution)/shard_map/ppermute | solution.py:27
  14.2 8.0 %collective-permute-start.12 = (bf16[128,640]{1,0:T(8,128)(2,1)}, bf16[128,640]{1,0:T(8,128)(2,1)S(1)}, u32[]{:S(2)}, u32[]{:S(2)}) collective-permute-start(bf16[128,640]{1,0:T(8,128)(2,1)} %param.10), channel_id=1, source_target_pairs={{0,2},{1,3},{2,0},{3,1},{4,6},{5,7},{6,4},{7,5},{8,10},{9,11},{10,... | collective-permute-start | bytes 491528 | tf_op jit(solution)/shard_map/ppermute | solution.py:37
  17.7 12.7 %collective-permute-start.11 = (bf16[2,128,640]{2,1,0:T(8,128)(2,1)S(1)}, bf16[2,128,640]{2,1,0:T(8,128)(2,1)S(1)}, u32[]{:S(2)}, u32[]{:S(2)}) collective-permute-start(bf16[2,128,640]{2,1,0:T(8,128)(2,1)S(1)} %pad_maximum_fusion.pair_ref), channel_id=1, source_target_pairs={{0,3},{1,2},{2,1},{3,0},{4,7},{5,6},{6,5},{7,4},{8,11},{9,10},{10,... | collective-permute-start | bytes 983048 | tf_op jit(solution)/shard_map/ppermute | solution.py:37
  19.3 11.1 %collective-permute-start.10 = (bf16[2,128,640]{2,1,0:T(8,128)(2,1)S(1)}, bf16[2,128,640]{2,1,0:T(8,128)(2,1)S(1)}, u32[]{:S(2)}, u32[]{:S(2)}) collective-permute-start(bf16[2,128,640]{2,1,0:T(8,128)(2,1)S(1)} %pad_maximum_fusion.pair_ref), channel_id=1, source_target_pairs={{0,1},{1,0},{2,3},{3,2},{4,5},{5,4},{6,7},{7,6},{8,9},{9,8},{10,11... | collective-permute-start | bytes 983048 | tf_op jit(solution)/shard_map/ppermute | solution.py:37
  21.1 1.3 %collective-permute-start.5 = (bf16[256,256]{1,0:T(8,128)(2,1)S(1)}, bf16[256,256]{1,0:T(8,128)(2,1)S(1)}, u32[]{:S(2)}, u32[]{:S(2)}) collective-permute-start(bf16[256,256]{1,0:T(8,128)(2,1)S(1)} %constant_dynamic-update-slice_fusion.refs_0_.refs_7_), channel_id=1, source_target_pairs={{0,8},{8,0},{16,24},{24,16},{32,40},{40,32},{48,56},{56,48},{64,72... | collective-permute-start | bytes 393224 | tf_op jit(solution)/shard_map/ppermute | solution.py:27
  21.1 1.6 %collective-permute-start.6 = (bf16[256,256]{1,0:T(8,128)(2,1)S(1)}, bf16[256,256]{1,0:T(8,128)(2,1)S(1)}, u32[]{:S(2)}, u32[]{:S(2)}) collective-permute-start(bf16[256,256]{1,0:T(8,128)(2,1)S(1)} %collective-permute-done.1.refs_1_.refs_8_), channel_id=1, source_target_pairs={{0,8},{8,0},{16,24},{24,16},{32,40},{40,32},{48,56},{56,48},{64,72... | collective-permute-start | bytes 393224 | tf_op jit(solution)/shard_map/ppermute | solution.py:27
  22.2 4.4 %collective-permute-start.7 = (bf16[256,256]{1,0:T(8,128)(2,1)S(1)}, bf16[256,256]{1,0:T(8,128)(2,1)S(1)}, u32[]{:S(2)}, u32[]{:S(2)}) collective-permute-start(bf16[256,256]{1,0:T(8,128)(2,1)S(1)} %constant_dynamic-update-slice_fusion.2.refs_2_.refs_10_), channel_id=1, source_target_pairs={{0,8},{8,0},{16,24},{24,16},{32,40},{40,32},{48,56},{56,48},{64,72... | collective-permute-start | bytes 393224 | tf_op jit(solution)/shard_map/ppermute | solution.py:27
  22.5 4.1 %collective-permute-start.8 = (bf16[256,256]{1,0:T(8,128)(2,1)S(1)}, bf16[256,256]{1,0:T(8,128)(2,1)S(1)}, u32[]{:S(2)}, u32[]{:S(2)}) collective-permute-start(bf16[256,256]{1,0:T(8,128)(2,1)S(1)} %collective-permute-done.4.refs_3_.refs_11_), channel_id=1, source_target_pairs={{0,8},{8,0},{16,24},{24,16},{32,40},{40,32},{48,56},{56,48},{64,72... | collective-permute-start | bytes 393224 | tf_op jit(solution)/shard_map/ppermute | solution.py:27
  22.7 9.5 %collective-permute-start.13 = (bf16[128,640]{1,0:T(8,128)(2,1)S(1)}, bf16[128,640]{1,0:T(8,128)(2,1)S(1)}, u32[]{:S(2)}, u32[]{:S(2)}) collective-permute-start(bf16[128,640]{1,0:T(8,128)(2,1)S(1)} %collective-permute-done.12.across_ref), channel_id=1, source_target_pairs={{0,4},{1,5},{2,6},{3,7},{4,0},{5,1},{6,2},{7,3},{8,12},{9,13},{10,... | collective-permute-start | bytes 491528 | tf_op jit(solution)/shard_map/ppermute | solution.py:37
  26.6 0.9 %copy-start = (bf16[144,640]{1,0:T(8,128)(2,1)S(1)}, bf16[144,640]{1,0:T(8,128)(2,1)}, u32[]{:S(2)}) copy-start(bf16[144,640]{1,0:T(8,128)(2,1)} %get-tuple-element.35.qt_ref.refs_0_) | copy-start | bytes 552964
  27.5 4.7 %copy-start.1 = (bf16[640,128]{1,0:T(8,128)(2,1)S(1)}, bf16[640,128]{1,0:T(8,128)(2,1)}, u32[]{:S(2)}) copy-start(bf16[640,128]{1,0:T(8,128)(2,1)} %get-tuple-element.46.refs_4_) | copy-start | bytes 491524
  32.8 1.6 %collective-permute-start.14 = (bf16[2,2,128,256]{3,2,1,0:T(8,128)(2,1)S(1)}, bf16[2,2,128,256]{3,2,1,0:T(8,128)(2,1)S(1)}, u32[]{:S(2)}, u32[]{:S(2)}) collective-permute-start(bf16[2,2,128,256]{3,2,1,0:T(8,128)(2,1)S(1)} %get-tuple-element.55), channel_id=1, source_target_pairs={{0,8},{8,0},{16,24},{24,16},{32,40},{40,32},{48,56},{56,48},{64,72... | collective-permute-start | bytes 786440 | tf_op jit(solution)/shard_map/ppermute | solution.py:27
  34.4 1.9 %collective-permute-start.15 = (bf16[2,2,128,256]{3,2,1,0:T(8,128)(2,1)S(1)}, bf16[2,2,128,256]{3,2,1,0:T(8,128)(2,1)S(1)}, u32[]{:S(2)}, u32[]{:S(2)}) collective-permute-start(bf16[2,2,128,256]{3,2,1,0:T(8,128)(2,1)S(1)} %get-tuple-element.61), channel_id=1, source_target_pairs={{0,8},{8,0},{16,24},{24,16},{32,40},{40,32},{48,56},{56,48},{64,72... | collective-permute-start | bytes 786440 | tf_op jit(solution)/shard_map/ppermute | solution.py:27
  34.6 6.4 %collective-permute-start.17 = (bf16[2,128,256]{2,1,0:T(8,128)(2,1)S(1)}, bf16[2,128,256]{2,1,0:T(8,128)(2,1)S(1)}, u32[]{:S(2)}, u32[]{:S(2)}) collective-permute-start(bf16[2,128,256]{2,1,0:T(8,128)(2,1)S(1)} %fusion.3), channel_id=1, source_target_pairs={{0,16},{8,24},{16,0},{24,8},{32,48},{40,56},{48,32},{56,40},{64,80... | collective-permute-start | bytes 393224 | tf_op jit(solution)/shard_map/ppermute | solution.py:27
  36.4 7.3 %collective-permute-start.16 = (bf16[2,128,256]{2,1,0:T(8,128)(2,1)S(1)}, bf16[2,128,256]{2,1,0:T(8,128)(2,1)S(1)}, u32[]{:S(2)}, u32[]{:S(2)}) collective-permute-start(bf16[2,128,256]{2,1,0:T(8,128)(2,1)S(1)} %fusion.4), channel_id=1, source_target_pairs={{0,16},{8,24},{16,0},{24,8},{32,48},{40,56},{48,32},{56,40},{64,80... | collective-permute-start | bytes 393224 | tf_op jit(solution)/shard_map/ppermute | solution.py:27
  41.1 8.8 %collective-permute-start.18 = (bf16[128,256]{1,0:T(8,128)(2,1)S(1)}, bf16[128,256]{1,0:T(8,128)(2,1)S(1)}, u32[]{:S(2)}, u32[]{:S(2)}) collective-permute-start(bf16[128,256]{1,0:T(8,128)(2,1)S(1)} %get-tuple-element.64), channel_id=1, source_target_pairs={{64,0},{72,8},{80,16},{88,24},{96,32},{104,40},{112,48},{120,56},{... | collective-permute-start | bytes 196616 | tf_op jit(solution)/shard_map/ppermute | solution.py:32
  42.4 10.6 %collective-permute-start.19 = (bf16[128,256]{1,0:T(8,128)(2,1)S(1)}, bf16[128,256]{1,0:T(8,128)(2,1)S(1)}, u32[]{:S(2)}, u32[]{:S(2)}) collective-permute-start(bf16[128,256]{1,0:T(8,128)(2,1)S(1)} %get-tuple-element.65), channel_id=1, source_target_pairs={{64,32},{72,40},{80,48},{88,56},{96,0},{104,8},{112,16},{120,24},{... | collective-permute-start | bytes 196616 | tf_op jit(solution)/shard_map/ppermute | solution.py:32
  43.8 9.2 %collective-permute-start.20 = (bf16[128,256]{1,0:T(8,128)(2,1)S(1)}, bf16[128,256]{1,0:T(8,128)(2,1)S(1)}, u32[]{:S(2)}, u32[]{:S(2)}) collective-permute-start(bf16[128,256]{1,0:T(8,128)(2,1)S(1)} %fusion.5), channel_id=1, source_target_pairs={{0,32},{8,40},{16,48},{24,56},{32,0},{40,8},{48,16},{56,24},{64,96... | collective-permute-start | bytes 196616 | tf_op jit(solution)/shard_map/ppermute | solution.py:27
